TPU v7x, 32 devices: a whole 2x2x4 slice. The times are simulated.
32 devices in a mesh: dp: 8 (over z, x), mp: 4 (over y, core).
Axes of the slice: x: 2, y: 2, z: 4, core: 2. Of those that a mesh axis runs over, the one named last changes fastest.
Arguments:
- frames: bfloat16 [16384, 1024], P(('dp', 'mp')), may hold values from -12 to 12
- out_cotangent: bfloat16 [16384, 1024], P(('dp', 'mp')), may hold values from -6 to 6
- lengths: int32 [16], P('dp'), may hold values from 512 to 1024, as said below
- masked_rows: int32 [8192], P(('dp', 'mp')), may hold values from 0 to 511, as said below
- targets: int32 [8192], P(('dp', 'mp')), may hold values from 0 to 8191
- head_device: int32 [8192, 1], P(('dp', 'mp')), may hold values from 0 to 7; in each aligned block of 256 rows (0 to 255, 256 to 511, ...) at most 64 rows name the same one
- first_gain: float32 [1024], replicated, may hold values from 0.1 to 1.9
- first_in: bfloat16 [1024, 4096], P(None, 'mp'), may hold values from -0.1875 to 0.1875
- first_out: bfloat16 [4096, 1024], P('mp'), may hold values from -0.1875 to 0.1875
- attend_gain: float32 [1024], replicated, may hold values from 0.1 to 1.9
- query_weight: bfloat16 [1024, 1024], P(None, 'mp'), may hold values from -0.375 to 0.375
- key_weight: bfloat16 [1024, 1024], P(None, 'mp'), may hold values from -0.1875 to 0.1875
- value_weight: bfloat16 [1024, 1024], P(None, 'mp'), may hold values from -0.1875 to 0.1875
- attend_out: bfloat16 [1024, 1024], P('mp'), may hold values from -0.75 to 0.75
- mixer_gain: float32 [1024], replicated, may hold values from 0.1 to 1.9
- mixer_value: bfloat16 [1024, 1024], P(None, 'mp'), may hold values from -0.1875 to 0.1875
- mixer_gate: bfloat16 [1024, 1024], P(None, 'mp'), may hold values from -0.1875 to 0.1875
- mixer_depth: float32 [5, 1024], P(None, 'mp'), may hold values from -2.5 to 2.5
- batch_scale: float32 [1024], P('mp'), may hold values from 0.1 to 1.9
- batch_shift: float32 [1024], P('mp'), may hold values from -3 to 3
- mixer_out: bfloat16 [1024, 1024], P('mp'), may hold values from -0.1875 to 0.1875
- second_gain: float32 [1024], replicated, may hold values from 0.1 to 1.9
- second_in: bfloat16 [1024, 4096], P(None, 'mp'), may hold values from -0.1875 to 0.1875
- second_out: bfloat16 [4096, 1024], P('mp'), may hold values from -0.1875 to 0.1875
- final_gain: float32 [1024], replicated, may hold values from 0.1 to 1.9
- head_weight: bfloat16 [1024, 8192], P(None, 'mp'), may hold values from -2 to 2
Outputs:
- output: float32 [16384, 1024], P(('dp', 'mp'))
- loss: float32 [], replicated
- input_grad: float32 [16384, 1024], P(('dp', 'mp'))
- first_gain_grad: float32 [1024], replicated
- first_in_grad: float32 [1024, 4096], P('dp', 'mp')
- first_out_grad: float32 [4096, 1024], P('mp', 'dp')
- attend_gain_grad: float32 [1024], replicated
- query_weight_grad: float32 [1024, 1024], P('dp', 'mp')
- key_weight_grad: float32 [1024, 1024], P('dp', 'mp')
- value_weight_grad: float32 [1024, 1024], P('dp', 'mp')
- attend_out_grad: float32 [1024, 1024], P('mp', 'dp')
- mixer_gain_grad: float32 [1024], replicated
- mixer_value_grad: float32 [1024, 1024], P('dp', 'mp')
- mixer_gate_grad: float32 [1024, 1024], P('dp', 'mp')
- mixer_depth_grad: float32 [5, 1024], P(None, 'mp')
- batch_scale_grad: float32 [1024], P('mp')
- batch_shift_grad: float32 [1024], P('mp')
- mixer_out_grad: float32 [1024, 1024], P('mp', 'dp')
- second_gain_grad: float32 [1024], replicated
- second_in_grad: float32 [1024, 4096], P('dp', 'mp')
- second_out_grad: float32 [4096, 1024], P('mp', 'dp')
- final_gain_grad: float32 [1024], replicated
- head_weight_grad: float32 [1024, 8192], P('dp', 'mp')
Inputs may be any that keep to these rules, and one draw needn't show every extreme that they name: `lengths`: one utterance of every draw has exactly 1024 live frames. `masked_rows`: A row among the device's own 512 frames; where the device holds live frames, the row is one of them. `head_device`: among the 256 slots of one device, at most 64 name the same data index.
All inputs are finite; a program needn't handle non-finite values.
Results may differ from a plain program's by a relative error of at most 0.025.
Values may be sent and summed in bfloat16 or wider, within the bound.
No kernel may reach another device: no remote copies, remote signals or barrier semaphores. Data moves between devices by JAX's collectives and lax.ppermute only.
A program may use at most 256 MiB of HBM per device.

v0:
```python
import jax
import jax.numpy as jnp
from jax import lax
from jax.sharding import PartitionSpec as P

D = 1024
HEAD_DIM = 128
KERNEL = 5
LEN = 1024
SEQ_DEV = 2
TOK_DEV = 2048


NORM_EPSILON = 1e-05
MASKED_SCORE = -1000000000.0


def joined(shard, axis, combine):
    everything = jax.tree.map(lambda part: lax.all_gather(part, axis), shard)
    leading = jax.tree.map(lambda part: part[0], everything)

    def hop(k, so_far):
        return combine(so_far, jax.tree.map(lambda part: part[k], everything))

    return lax.fori_loop(1, lax.axis_size(axis), hop, leading)


def layer_norm(values, gain):
    center = values - jnp.mean(values, axis=-1, keepdims=True)
    spread = jnp.mean(center * center, axis=-1, keepdims=True)
    return center * lax.rsqrt(spread + NORM_EPSILON) * gain


def swish(values):
    return values * jax.nn.sigmoid(values)


def swish_slope(values):
    sigma = jax.nn.sigmoid(values)
    return sigma * (1.0 + values * (1.0 - sigma))


def depth_conv(glu, depth):
    length = glu.shape[1]
    half = KERNEL // 2
    padded = jnp.pad(glu, ((0, 0), (half, half), (0, 0)))
    total = padded[:, 0:length] * depth[0]
    for offset in range(1, KERNEL):
        total = total + padded[:, offset : offset + length] * depth[offset]
    return total


def matmul(left, right):
    return jnp.dot(left, right, preferred_element_type=jnp.float32)


def matmul_t(left, right):
    return lax.dot_general(
        left, right, (((1,), (1,)), ((), ())), preferred_element_type=jnp.float32
    )


def weight_term(left, right):
    return lax.dot_general(
        left, right, (((0,), (0,)), ((), ())), preferred_element_type=jnp.float32
    )


def spread_rows(values):
    return lax.all_gather(values, "mp", axis=0, tiled=True)


def collect_rows(values):
    return lax.psum_scatter(values, "mp", scatter_dimension=0, tiled=True)


def spread_grads(values):
    return lax.all_gather(values, "mp", axis=0, tiled=True)


def collect_grads(values):
    return lax.psum_scatter(values, "mp", scatter_dimension=0, tiled=True)


def weight_grad(left, right):
    return weight_term(left, right)


def combine_parts(first, second):
    top = jnp.maximum(first[0], second[0])
    total = first[1] * jnp.exp(first[0] - top) + second[1] * jnp.exp(second[0] - top)
    return (top, total)


def feed_forward(resid, gain, expand, project):
    normed, norm_pullback = jax.vjp(layer_norm, resid, gain)
    gathered = spread_rows(normed.astype(jnp.bfloat16))
    inner = matmul(gathered, expand)
    active = swish(inner).astype(jnp.bfloat16)
    return (collect_rows(matmul(active, project)), (norm_pullback, gathered, inner, active))


def feed_backward(expand, project, kept, grad_branch):
    norm_pullback, gathered, inner, active = kept
    grad_full = spread_grads(grad_branch.astype(jnp.bfloat16))
    grad_inner = (matmul_t(grad_full, project) * swish_slope(inner)).astype(jnp.bfloat16)
    grad_project = weight_grad(grad_full, active)
    grad_expand = weight_grad(gathered, grad_inner)
    grad_resid, grad_gain = norm_pullback(collect_grads(matmul_t(grad_inner, expand)))
    return (grad_resid, grad_gain, grad_expand, grad_project)


def attend_forward(resid, gain, query_weight, key_weight, value_weight, attend_out, live):
    normed, norm_pullback = jax.vjp(layer_norm, resid, gain)
    gathered = spread_rows(normed.astype(jnp.bfloat16))
    width = query_weight.shape[1]
    shape = (SEQ_DEV, LEN, width // HEAD_DIM, HEAD_DIM)
    query = matmul(gathered, query_weight).astype(jnp.bfloat16).reshape(shape)
    keys = matmul(gathered, key_weight).astype(jnp.bfloat16).reshape(shape)
    values = matmul(gathered, value_weight).astype(jnp.bfloat16).reshape(shape)
    scale = HEAD_DIM ** (-0.5)

    def one_utterance(pack):
        query_part, keys_part, values_part, alive = pack
        scores = (
            jnp.einsum("qhe,khe->hqk", query_part, keys_part, preferred_element_type=jnp.float32)
            * scale
        )
        scores = jnp.where(alive[None, None, :] > 0, scores, MASKED_SCORE)
        top = jnp.max(scores, axis=-1, keepdims=True)
        lifted = jnp.exp(scores - top)
        total = jnp.sum(lifted, axis=-1, keepdims=True)
        shares = (lifted / total).astype(jnp.bfloat16)
        mixed_part = jnp.einsum(
            "hqk,khe->qhe", shares, values_part, preferred_element_type=jnp.float32
        )
        return (mixed_part.astype(jnp.bfloat16), (top + jnp.log(total))[:, :, 0])

    mixed, log_total = lax.map(one_utterance, (query, keys, values, live))
    mixed = mixed.reshape(TOK_DEV, width)
    branch = collect_rows(matmul(mixed, attend_out))
    return (branch, (norm_pullback, gathered, query, keys, values, mixed, log_total))


def attend_backward(query_weight, key_weight, value_weight, attend_out, live, kept, grad_branch):
    norm_pullback, gathered, query, keys, values, mixed, log_total = kept
    width = query_weight.shape[1]
    grad_full = spread_grads(grad_branch.astype(jnp.bfloat16))
    grad_mixed = matmul_t(grad_full, attend_out).astype(jnp.bfloat16).reshape(query.shape)
    grad_attend_out = weight_grad(grad_full, mixed)
    scale = HEAD_DIM ** (-0.5)

    def one_utterance(pack):
        query_part, keys_part, values_part, alive, log_part, grad_part = pack
        scores = (
            jnp.einsum("qhe,khe->hqk", query_part, keys_part, preferred_element_type=jnp.float32)
            * scale
        )
        scores = jnp.where(alive[None, None, :] > 0, scores, MASKED_SCORE)
        shares = jnp.exp(scores - log_part[:, :, None])
        grad_values = jnp.einsum(
            "hqk,qhe->khe",
            shares.astype(jnp.bfloat16),
            grad_part,
            preferred_element_type=jnp.float32,
        )
        grad_shares = jnp.einsum(
            "qhe,khe->hqk", grad_part, values_part, preferred_element_type=jnp.float32
        )
        inner = jnp.sum(shares * grad_shares, axis=-1, keepdims=True)
        grad_scores = (shares * (grad_shares - inner)).astype(jnp.bfloat16)
        grad_query = (
            jnp.einsum("hqk,khe->qhe", grad_scores, keys_part, preferred_element_type=jnp.float32)
            * scale
        )
        grad_keys = (
            jnp.einsum("hqk,qhe->khe", grad_scores, query_part, preferred_element_type=jnp.float32)
            * scale
        )
        return (
            grad_query.astype(jnp.bfloat16),
            grad_keys.astype(jnp.bfloat16),
            grad_values.astype(jnp.bfloat16),
        )

    grad_query, grad_keys, grad_values = lax.map(
        one_utterance, (query, keys, values, live, log_total, grad_mixed)
    )
    grad_query = grad_query.reshape(TOK_DEV, width)
    grad_keys = grad_keys.reshape(TOK_DEV, width)
    grad_values = grad_values.reshape(TOK_DEV, width)
    grad_query_weight = weight_grad(gathered, grad_query)
    grad_key_weight = weight_grad(gathered, grad_keys)
    grad_value_weight = weight_grad(gathered, grad_values)
    summed = (
        matmul_t(grad_query, query_weight)
        + matmul_t(grad_keys, key_weight)
        + matmul_t(grad_values, value_weight)
    )
    grad_resid, grad_gain = norm_pullback(collect_grads(summed))
    return (
        grad_resid,
        grad_gain,
        grad_query_weight,
        grad_key_weight,
        grad_value_weight,
        grad_attend_out,
    )


def mixer_forward(
    resid,
    gain,
    mixer_value,
    mixer_gate,
    mixer_depth,
    batch_scale,
    batch_shift,
    mixer_out,
    live_flat,
):
    normed, norm_pullback = jax.vjp(layer_norm, resid, gain)
    gathered = spread_rows(normed.astype(jnp.bfloat16))
    value_in = matmul(gathered, mixer_value)
    gate_in = matmul(gathered, mixer_gate)
    channels = value_in.shape[1]

    def front(value_part, gate_part, depth):
        glu = value_part * jax.nn.sigmoid(gate_part) * live_flat[:, None]
        return depth_conv(glu.reshape(SEQ_DEV, LEN, channels), depth).reshape(TOK_DEV, channels)

    convolved, front_pullback = jax.vjp(front, value_in, gate_in, mixer_depth)
    weighted = convolved * live_flat[:, None]
    count, first_sum, second_sum = lax.psum(
        (jnp.sum(live_flat), jnp.sum(weighted, axis=0), jnp.sum(weighted * convolved, axis=0)), "dp"
    )
    bn_mean = first_sum / count
    inverse = lax.rsqrt(second_sum / count - bn_mean * bn_mean + NORM_EPSILON)
    normal = (convolved - bn_mean) * inverse
    shaped = normal * batch_scale + batch_shift
    active = swish(shaped).astype(jnp.bfloat16)
    branch = collect_rows(matmul(active, mixer_out))
    return (
        branch,
        (norm_pullback, gathered, front_pullback, normal, inverse, count, shaped, active),
    )


def mixer_backward(mixer_value, mixer_gate, batch_scale, mixer_out, live_flat, kept, grad_branch):
    norm_pullback, gathered, front_pullback, normal, inverse, count, shaped, active = kept
    grad_full = spread_grads(grad_branch.astype(jnp.bfloat16))
    grad_mixer_out = weight_grad(grad_full, active)
    grad_shaped = matmul_t(grad_full, mixer_out) * swish_slope(shaped)
    shift_grad, scale_grad = lax.psum(
        (jnp.sum(grad_shaped, axis=0), jnp.sum(grad_shaped * normal, axis=0)), "dp"
    )
    grad_conv = (
        batch_scale
        * inverse
        * (grad_shaped - live_flat[:, None] / count * (shift_grad + normal * scale_grad))
    )
    grad_value, grad_gate, depth_grad = front_pullback(grad_conv)
    grad_value = grad_value.astype(jnp.bfloat16)
    grad_gate = grad_gate.astype(jnp.bfloat16)
    grad_mixer_value = weight_grad(gathered, grad_value)
    grad_mixer_gate = weight_grad(gathered, grad_gate)
    summed = matmul_t(grad_value, mixer_value) + matmul_t(grad_gate, mixer_gate)
    grad_resid, grad_gain = norm_pullback(collect_grads(summed))
    return (
        grad_resid,
        grad_gain,
        grad_mixer_value,
        grad_mixer_gate,
        depth_grad,
        scale_grad,
        shift_grad,
        grad_mixer_out,
    )


def masked_head(output, own_live, masked_rows, targets, head_device, head_weight):
    rows = output.shape[0]
    sources = lax.axis_size("dp")
    capacity = rows // sources
    keep = own_live[masked_rows]
    chosen = output[masked_rows].astype(jnp.bfloat16)
    destination = head_device[:, 0]
    marks = (destination[:, None] == jnp.arange(sources)[None, :]).astype(jnp.int32)
    order = jnp.sum((jnp.cumsum(marks, axis=0) - marks) * marks, axis=1)
    placer = (destination * capacity + order)[:, None] == jnp.arange(rows)[None, :]
    packed = weight_term(placer.astype(jnp.bfloat16), chosen).astype(jnp.bfloat16)
    labels = (targets + 1) * (keep > 0).astype(jnp.int32)
    codes = jnp.sum(jnp.where(placer, labels[:, None], 0), axis=0)
    arrived, arrived_codes = (
        lax.all_to_all(packed, "dp", split_axis=0, concat_axis=0, tiled=True),
        lax.all_to_all(codes, "dp", split_axis=0, concat_axis=0, tiled=True),
    )
    shared, shared_codes = (
        lax.all_gather(arrived, "mp", axis=0, tiled=True),
        lax.all_gather(arrived_codes, "mp", axis=0, tiled=True),
    )
    logits = matmul(shared, head_weight)
    vocab = head_weight.shape[1]
    hits = (shared_codes - 1 - lax.axis_index("mp") * vocab)[:, None] == jnp.arange(vocab)[None, :]
    top = jnp.max(logits, axis=1)
    total = jnp.sum(jnp.exp(logits - top[:, None]), axis=1)
    picked = jnp.sum(jnp.where(hits, logits, 0.0), axis=1)
    top_all, total_all = joined((top, total), "mp", combine_parts)
    log_total = top_all + jnp.log(total_all)
    counted = (shared_codes > 0).astype(jnp.float32)
    own_total = jnp.sum(
        lax.dynamic_slice_in_dim(counted * log_total, lax.axis_index("mp") * rows, rows)
    )
    own_loss = own_total - jnp.sum(counted * picked)
    grad_logits = (
        counted[:, None] * (jnp.exp(logits - log_total[:, None]) - hits.astype(jnp.float32))
    ).astype(jnp.bfloat16)
    grad_head = weight_grad(shared, grad_logits)
    grad_shared = lax.psum_scatter(
        matmul_t(grad_logits, head_weight), "mp", scatter_dimension=0, tiled=True
    )
    returned = lax.all_to_all(
        grad_shared.astype(jnp.bfloat16), "dp", split_axis=0, concat_axis=0, tiled=True
    )
    grad_chosen = matmul(placer.astype(jnp.bfloat16), returned).astype(jnp.bfloat16)
    picker = (masked_rows[:, None] == jnp.arange(rows)[None, :]).astype(jnp.bfloat16)
    grad_rows = weight_term(picker, grad_chosen)
    return (grad_rows, grad_head, own_loss, jnp.sum(keep))


def on_device(
    frames,
    out_cotangent,
    lengths,
    masked_rows,
    targets,
    head_device,
    first_gain,
    first_in,
    first_out,
    attend_gain,
    query_weight,
    key_weight,
    value_weight,
    attend_out,
    mixer_gain,
    mixer_value,
    mixer_gate,
    mixer_depth,
    batch_scale,
    batch_shift,
    mixer_out,
    second_gain,
    second_in,
    second_out,
    final_gain,
    head_weight,
):
    rows = frames.shape[0]
    live = (jnp.arange(LEN)[None, :] < lengths[:, None]).astype(jnp.float32)
    live_flat = live.reshape(TOK_DEV)
    own_live = lax.dynamic_slice_in_dim(live_flat, lax.axis_index("mp") * rows, rows)
    start = frames.astype(jnp.float32)
    branch, first_kept = feed_forward(start, first_gain, first_in, first_out)
    after_first = start + 0.5 * branch
    branch, attend_kept = attend_forward(
        after_first, attend_gain, query_weight, key_weight, value_weight, attend_out, live
    )
    after_attend = after_first + branch
    branch, mixer_kept = mixer_forward(
        after_attend,
        mixer_gain,
        mixer_value,
        mixer_gate,
        mixer_depth,
        batch_scale,
        batch_shift,
        mixer_out,
        live_flat,
    )
    after_mixer = after_attend + branch
    branch, second_kept = feed_forward(after_mixer, second_gain, second_in, second_out)
    after_second = after_mixer + 0.5 * branch
    output, final_pullback = jax.vjp(layer_norm, after_second, final_gain)
    grad_rows, grad_head, own_loss, own_count = masked_head(
        output, own_live, masked_rows, targets, head_device, head_weight
    )
    grad_second, final_gain_grad = final_pullback(out_cotangent.astype(jnp.float32) + grad_rows)
    back_resid, second_gain_grad, grad_second_in, grad_second_out = feed_backward(
        second_in, second_out, second_kept, 0.5 * grad_second
    )
    grad_mixer = grad_second + back_resid
    (
        back_resid,
        mixer_gain_grad,
        grad_mixer_value,
        grad_mixer_gate,
        depth_grad,
        batch_scale_grad,
        batch_shift_grad,
        grad_mixer_out,
    ) = mixer_backward(
        mixer_value, mixer_gate, batch_scale, mixer_out, live_flat, mixer_kept, grad_mixer
    )
    grad_attend = grad_mixer + back_resid
    back_resid, attend_gain_grad, grad_query, grad_key, grad_value, grad_attend_out = (
        attend_backward(
            query_weight, key_weight, value_weight, attend_out, live, attend_kept, grad_attend
        )
    )
    grad_first = grad_attend + back_resid
    back_resid, first_gain_grad, grad_first_in, grad_first_out = feed_backward(
        first_in, first_out, first_kept, 0.5 * grad_first
    )
    input_grad = grad_first + back_resid
    channels = mixer_value.shape[1]
    offset = lax.axis_index("mp") * channels
    depth_full = lax.dynamic_update_slice_in_dim(
        jnp.zeros((KERNEL, D), jnp.float32), depth_grad, offset, 1
    )
    (
        first_gain_grad,
        attend_gain_grad,
        mixer_gain_grad,
        second_gain_grad,
        final_gain_grad,
        depth_full,
        loss_sum,
        loss_count,
    ) = lax.psum(
        (
            first_gain_grad,
            attend_gain_grad,
            mixer_gain_grad,
            second_gain_grad,
            final_gain_grad,
            depth_full,
            own_loss,
            own_count,
        ),
        ("dp", "mp"),
    )
    mixer_depth_grad = lax.dynamic_slice_in_dim(depth_full, offset, channels, 1)
    loss = loss_sum / loss_count
    (
        grad_first_in,
        grad_first_out,
        grad_query,
        grad_key,
        grad_value,
        grad_attend_out,
        grad_mixer_value,
        grad_mixer_gate,
        grad_mixer_out,
        grad_second_in,
        grad_second_out,
        grad_head,
    ) = (
        lax.psum_scatter(grad_first_in, "dp", scatter_dimension=0, tiled=True),
        lax.psum_scatter(grad_first_out, "dp", scatter_dimension=0, tiled=True),
        lax.psum_scatter(grad_query, "dp", scatter_dimension=0, tiled=True),
        lax.psum_scatter(grad_key, "dp", scatter_dimension=0, tiled=True),
        lax.psum_scatter(grad_value, "dp", scatter_dimension=0, tiled=True),
        lax.psum_scatter(grad_attend_out, "dp", scatter_dimension=0, tiled=True),
        lax.psum_scatter(grad_mixer_value, "dp", scatter_dimension=0, tiled=True),
        lax.psum_scatter(grad_mixer_gate, "dp", scatter_dimension=0, tiled=True),
        lax.psum_scatter(grad_mixer_out, "dp", scatter_dimension=0, tiled=True),
        lax.psum_scatter(grad_second_in, "dp", scatter_dimension=0, tiled=True),
        lax.psum_scatter(grad_second_out, "dp", scatter_dimension=0, tiled=True),
        lax.psum_scatter(grad_head, "dp", scatter_dimension=0, tiled=True),
    )
    return (
        output,
        loss,
        input_grad,
        first_gain_grad,
        grad_first_in,
        grad_first_out.T,
        attend_gain_grad,
        grad_query,
        grad_key,
        grad_value,
        grad_attend_out.T,
        mixer_gain_grad,
        grad_mixer_value,
        grad_mixer_gate,
        mixer_depth_grad,
        batch_scale_grad,
        batch_shift_grad,
        grad_mixer_out.T,
        second_gain_grad,
        grad_second_in,
        grad_second_out.T,
        final_gain_grad,
        grad_head,
    )


def solution(mesh):
    in_specs = (
        P(("dp", "mp"), None),
        P(("dp", "mp"), None),
        P("dp"),
        P(("dp", "mp")),
        P(("dp", "mp")),
        P(("dp", "mp"), None),
        P(),
        P(None, "mp"),
        P("mp", None),
        P(),
        P(None, "mp"),
        P(None, "mp"),
        P(None, "mp"),
        P("mp", None),
        P(),
        P(None, "mp"),
        P(None, "mp"),
        P(None, "mp"),
        P("mp"),
        P("mp"),
        P("mp", None),
        P(),
        P(None, "mp"),
        P("mp", None),
        P(),
        P(None, "mp"),
    )
    out_specs = (
        P(("dp", "mp"), None),
        P(),
        P(("dp", "mp"), None),
        P(),
        P("dp", "mp"),
        P("mp", "dp"),
        P(),
        P("dp", "mp"),
        P("dp", "mp"),
        P("dp", "mp"),
        P("mp", "dp"),
        P(),
        P("dp", "mp"),
        P("dp", "mp"),
        P(None, "mp"),
        P("mp"),
        P("mp"),
        P("mp", "dp"),
        P(),
        P("dp", "mp"),
        P("mp", "dp"),
        P(),
        P("dp", "mp"),
    )
    return jax.shard_map(
        on_device, mesh=mesh, in_specs=in_specs, out_specs=out_specs, check_vma=False
    )
```

profile of v0, /device:TPU:0, one launch (start us, length us, event | category | flops | bytes accessed | tf_op | source)
XLA Modules:
  0.0 2409.3 jit_solution(16573446019505147662)
XLA Ops:
  13.1 37.3 %all-gather.13.cloned.1.call-done = bf16[2048,1024]{1,0:T(8,128)(2,1)} async-done(((bf16[512,1024]{1,0:T(8,128)(2,1)}), bf16[2048,1024]{1,0:T(8,128)(2,1)}) %all-gather.13.cloned.1.call-update) | async-done | bytes 4194320 | tf_op jit(solution)/shard_map/all_gather | solution.py:70
  70.9 71.8 %reduce-scatter.22.cloned.1.call-done = f32[512,1024]{1,0:T(8,128)} async-done(((f32[2048,1024]{1,0:T(8,128)}), f32[512,1024]{1,0:T(8,128)}) %reduce-scatter.22.cloned.1.call-update) | async-done | bytes 2097168 | tf_op jit(solution)/shard_map/reduce_scatter | solution.py:74
  205.7 40.0 %while.43 = (s32[]{:T(128)}, bf16[2,1024,2,128]{3,2,1,0:T(2,128)(2,1)}, f32[2,2,1024]{2,1,0:T(2,128)S(1)}, bf16[2,1024,2,128]{3,2,1,0:T(2,128)(2,1)}, f32[2,1024...) while((s32[]{:T(128)}, ...), condition=%wide.region_8.9_spmd, body=%wide.region_5.8_spmd.sunk | while | flops 1099168768 | bytes 69281432 | solution.py:139
  252.3 71.6 %reduce-scatter.24.cloned.1.call-done = f32[512,1024]{1,0:T(8,128)} async-done(((f32[2048,1024]{1,0:T(8,128)}), f32[512,1024]{1,0:T(8,128)}) %reduce-scatter.24.cloned.1.call-update) | async-done | bytes 2097168 | tf_op jit(solution)/shard_map/reduce_scatter | solution.py:74
  404.4 68.2 %reduce-scatter.26.cloned.1.call-done = f32[512,1024]{1,0:T(8,128)} async-done(((f32[2048,1024]{1,0:T(8,128)}), f32[512,1024]{1,0:T(8,128)}) %reduce-scatter.26.cloned.1.call-update) | async-done | bytes 2097168 | tf_op jit(solution)/shard_map/reduce_scatter | solution.py:74
  532.8 70.3 %reduce-scatter.28.cloned.1.call-done = f32[512,1024]{1,0:T(8,128)} async-done(((f32[2048,1024]{1,0:T(8,128)}), f32[512,1024]{1,0:T(8,128)}) %reduce-scatter.28.cloned.1.call-update) | async-done | bytes 2097168 | tf_op jit(solution)/shard_map/reduce_scatter | solution.py:74
  722.2 71.8 %reduce-scatter.30.cloned.1.call-done = f32[512,1024]{1,0:T(8,128)} async-done(((f32[2048,1024]{1,0:T(8,128)}), f32[512,1024]{1,0:T(8,128)}) %reduce-scatter.30.cloned.1.call-update) | async-done | bytes 2097168 | tf_op jit(solution)/shard_map/reduce_scatter | solution.py:319
  891.0 71.8 %reduce-scatter.32.cloned.1.call-done = f32[512,1024]{1,0:T(8,128)} async-done(((f32[2048,1024]{1,0:T(8,128)}), f32[512,1024]{1,0:T(8,128)}) %reduce-scatter.32.cloned.1.call-update) | async-done | bytes 2097168 | tf_op jit(solution)/shard_map/reduce_scatter | solution.py:82
  1045.8 68.1 %reduce-scatter.34.cloned.1.call-done = f32[512,1024]{1,0:T(8,128)} async-done(((f32[2048,1024]{1,0:T(8,128)}), f32[512,1024]{1,0:T(8,128)}) %reduce-scatter.34.cloned.1.call-update) | async-done | bytes 2097168 | tf_op jit(solution)/shard_map/reduce_scatter | solution.py:82
  1164.2 55.1 %while.45 = (s32[]{:T(128)}, bf16[2,1024,2,128]{3,2,1,0:T(2,128)(2,1)}, bf16[2,1024,2,128]{3,2,1,0:T(2,128)(2,1)}, bf16[2,1024,2,128]{3,2,1,0:T(2,128)(2,1)}, bf...) while((s32[]{:T(128)}, ...), condition=%wide.region_53.54_spmd, body=%wide.region_51.53_spmd.sunk | while | flops 2717121536 | bytes 135334128 | solution.py:186
  1228.1 71.8 %reduce-scatter.36.cloned.1.call-done = f32[512,1024]{1,0:T(8,128)} async-done(((f32[2048,1024]{1,0:T(8,128)}), f32[512,1024]{1,0:T(8,128)}) %reduce-scatter.36.cloned.1.call-update) | async-done | bytes 2097168 | tf_op jit(solution)/shard_map/reduce_scatter | solution.py:82
  1442.6 57.4 %reduce-scatter.56.cloned.1.call-done = f32[128,256]{1,0:T(8,128)} async-done(((f32[1024,256]{1,0:T(8,128)}), f32[128,256]{1,0:T(8,128)}) %reduce-scatter.56.cloned.1.call-update) | async-done | bytes 131088 | tf_op jit(solution)/shard_map/reduce_scatter | solution.py:467
  1501.7 64.0 %reduce-scatter.50.cloned.1.call-done = f32[128,256]{1,0:T(8,128)} async-done(((f32[1024,256]{1,0:T(8,128)}), f32[128,256]{1,0:T(8,128)}) %reduce-scatter.50.cloned.1.call-update) | async-done | bytes 131088 | tf_op jit(solution)/shard_map/reduce_scatter | solution.py:464
  1567.4 89.3 %reduce-scatter.42.cloned.1.call-done = f32[128,1024]{1,0:T(8,128)} async-done(((f32[1024,1024]{1,0:T(8,128)}), f32[128,1024]{1,0:T(8,128)}) %reduce-scatter.42.cloned.1.call-update) | async-done | bytes 524304 | tf_op jit(solution)/shard_map/reduce_scatter | solution.py:460
  1658.8 72.0 %reduce-scatter.38.cloned.1.call-done = f32[512,1024]{1,0:T(8,128)} async-done(((f32[2048,1024]{1,0:T(8,128)}), f32[512,1024]{1,0:T(8,128)}) %reduce-scatter.38.cloned.1.call-update) | async-done | bytes 2097168 | tf_op jit(solution)/shard_map/reduce_scatter | solution.py:82
  1734.1 44.3 %all-reduce.11 = (f32[]{:T(128)}, f32[]{:T(128)}, f32[1024]{0:T(1024)}, f32[1024]{0:T(1024)}, f32[1024]{0:T(1024)}, /*index=5*/f32[5,1024]{1,0:T(8,128)S(1)}, f32[1024]{0:T(1024)}, f32[1024]{0:T(1024)}) all-reduce(f32[]{:T(128)S(6)} %sub.166, f32[]{:T(128)} %reduce_sum.424, ...), channel_id=1, replica_groups=mesh['dp'=8,'mp'=4] {'dp','mp'}, use_global_device_ids=true, to_apply=%region_35.36 | all-reduce | flops 10242 | bytes 81936 | tf_op jit(solution)/shard_map/psum | solution.py:430
  1784.8 100.6 %reduce-scatter.62.cloned.1.call-done = f32[128,2048]{1,0:T(8,128)} async-done(((f32[1024,2048]{1,0:T(8,128)}), f32[128,2048]{1,0:T(8,128)}) %reduce-scatter.62.cloned.1.call-update) | async-done | bytes 1048592 | tf_op jit(solution)/shard_map/reduce_scatter | solution.py:470
  1885.4 91.0 %reduce-scatter.58.cloned.1.call-done = f32[128,1024]{1,0:T(8,128)} async-done(((f32[1024,1024]{1,0:T(8,128)}), f32[128,1024]{1,0:T(8,128)}) %reduce-scatter.58.cloned.1.call-update) | async-done | bytes 524304 | tf_op jit(solution)/shard_map/reduce_scatter | solution.py:468
  1976.4 67.5 %reduce-scatter.52.cloned.1.call-done = f32[128,256]{1,0:T(8,128)} async-done(((f32[1024,256]{1,0:T(8,128)}), f32[128,256]{1,0:T(8,128)}) %reduce-scatter.52.cloned.1.call-update) | async-done | bytes 131088 | tf_op jit(solution)/shard_map/reduce_scatter | solution.py:465
  2043.9 66.3 %reduce-scatter.54.cloned.1.call-done = f32[128,256]{1,0:T(8,128)} async-done(((f32[1024,256]{1,0:T(8,128)}), f32[128,256]{1,0:T(8,128)}) %reduce-scatter.54.cloned.1.call-update) | async-done | bytes 131088 | tf_op jit(solution)/shard_map/reduce_scatter | solution.py:466
  2110.2 66.7 %reduce-scatter.44.cloned.1.call-done = f32[128,256]{1,0:T(8,128)} async-done(((f32[1024,256]{1,0:T(8,128)}), f32[128,256]{1,0:T(8,128)}) %reduce-scatter.44.cloned.1.call-update) | async-done | bytes 131088 | tf_op jit(solution)/shard_map/reduce_scatter | solution.py:461
  2176.9 66.5 %reduce-scatter.46.cloned.1.call-done = f32[128,256]{1,0:T(8,128)} async-done(((f32[1024,256]{1,0:T(8,128)}), f32[128,256]{1,0:T(8,128)}) %reduce-scatter.46.cloned.1.call-update) | async-done | bytes 131088 | tf_op jit(solution)/shard_map/reduce_scatter | solution.py:462
  2243.4 66.7 %reduce-scatter.48.cloned.1.call-done = f32[128,256]{1,0:T(8,128)} async-done(((f32[1024,256]{1,0:T(8,128)}), f32[128,256]{1,0:T(8,128)}) %reduce-scatter.48.cloned.1.call-update) | async-done | bytes 131088 | tf_op jit(solution)/shard_map/reduce_scatter | solution.py:463
  2310.2 91.0 %reduce-scatter.40.cloned.1.call-done = f32[128,1024]{1,0:T(8,128)} async-done(((f32[1024,1024]{1,0:T(8,128)}), f32[128,1024]{1,0:T(8,128)}) %reduce-scatter.40.cloned.1.call-update) | async-done | bytes 524304 | tf_op jit(solution)/shard_map/reduce_scatter | solution.py:459
  (576 shorter events, 841.9 us)
Async XLA Ops:
  13.0 129.7 %reduce-scatter.22.cloned.1.call-start = ((), (), s32[]{:S(2)}) async-start(), calls=%async_computation.25 | async-start | bytes 10485760 | tf_op jit(solution)/shard_map/reduce_scatter | solution.py:74
  147.9 176.0 %reduce-scatter.24.cloned.1.call-start = ((), (), s32[]{:S(2)}) async-start(), calls=%async_computation.27 | async-start | bytes 10485760 | tf_op jit(solution)/shard_map/reduce_scatter | solution.py:74
  329.1 143.4 %reduce-scatter.26.cloned.1.call-start = ((), (), s32[]{:S(2)}) async-start(), calls=%async_computation.29 | async-start | bytes 10485760 | tf_op jit(solution)/shard_map/reduce_scatter | solution.py:74
  477.7 125.4 %reduce-scatter.28.cloned.1.call-start = ((), (), s32[]{:S(2)}) async-start(), calls=%async_computation.31 | async-start | bytes 10485760 | tf_op jit(solution)/shard_map/reduce_scatter | solution.py:74
  531.2 145.1 %all-gather.21.cloned.1.call-start = ((), (), s32[]{:S(2)}) async-start(), calls=%async_computation.32 | async-start | bytes 5242880 | tf_op jit(solution)/shard_map/all_gather | solution.py:299
  650.0 144.0 %reduce-scatter.30.cloned.1.call-start = ((), (), s32[]{:S(2)}) async-start(), calls=%async_computation.33 | async-start | bytes 10485760 | tf_op jit(solution)/shard_map/reduce_scatter | solution.py:319
  722.1 147.8 %all-gather.23.cloned.1.call-start = ((), (), s32[]{:S(2)}) async-start(), calls=%async_computation.34 | async-start | bytes 5242880 | tf_op jit(solution)/shard_map/all_gather | solution.py:78
  837.2 125.5 %reduce-scatter.32.cloned.1.call-start = ((), (), s32[]{:S(2)}) async-start(), calls=%async_computation.35 | async-start | bytes 10485760 | tf_op jit(solution)/shard_map/reduce_scatter | solution.py:82
  969.5 144.5 %reduce-scatter.34.cloned.1.call-start = ((), (), s32[]{:S(2)}) async-start(), calls=%async_computation.37 | async-start | bytes 10485760 | tf_op jit(solution)/shard_map/reduce_scatter | solution.py:82
  1120.3 179.6 %reduce-scatter.36.cloned.1.call-start = ((), (), s32[]{:S(2)}) async-start(), calls=%async_computation.39 | async-start | bytes 10485760 | tf_op jit(solution)/shard_map/reduce_scatter | solution.py:82
  1228.0 113.3 %all-gather.29.cloned.1.call-start = ((), (), s32[]{:S(2)}) async-start(), calls=%async_computation.40 | async-start | bytes 5242880 | tf_op jit(solution)/shard_map/all_gather | solution.py:78
  1306.7 131.0 %reduce-scatter.60.cloned.1.call-start = ((), (), s32[]{:S(2)}) async-start(), calls=%async_computation.52 | async-start | bytes 4718592 | tf_op jit(solution)/shard_map/reduce_scatter | solution.py:469
  1316.9 183.2 %reduce-scatter.56.cloned.1.call-start = ((), (), s32[]{:S(2)}) async-start(), calls=%async_computation.50 | async-start | bytes 1179648 | tf_op jit(solution)/shard_map/reduce_scatter | solution.py:467
  1322.8 242.9 %reduce-scatter.50.cloned.1.call-start = ((), (), s32[]{:S(2)}) async-start(), calls=%async_computation.47 | async-start | bytes 1179648 | tf_op jit(solution)/shard_map/reduce_scatter | solution.py:464
  1327.6 329.1 %reduce-scatter.42.cloned.1.call-start = ((), (), s32[]{:S(2)}) async-start(), calls=%async_computation.43 | async-start | bytes 4718592 | tf_op jit(solution)/shard_map/reduce_scatter | solution.py:460
  1351.4 379.3 %reduce-scatter.38.cloned.1.call-start = ((), (), s32[]{:S(2)}) async-start(), calls=%async_computation.41 | async-start | bytes 10485760 | tf_op jit(solution)/shard_map/reduce_scatter | solution.py:82
  1372.7 512.7 %reduce-scatter.62.cloned.1.call-start = ((), (), s32[]{:S(2)}) async-start(), calls=%async_computation.53 | async-start | bytes 9437184 | tf_op jit(solution)/shard_map/reduce_scatter | solution.py:470
  1389.3 587.1 %reduce-scatter.58.cloned.1.call-start = ((), (), s32[]{:S(2)}) async-start(), calls=%async_computation.51 | async-start | bytes 4718592 | tf_op jit(solution)/shard_map/reduce_scatter | solution.py:468
  1399.5 644.4 %reduce-scatter.52.cloned.1.call-start = ((), (), s32[]{:S(2)}) async-start(), calls=%async_computation.48 | async-start | bytes 1179648 | tf_op jit(solution)/shard_map/reduce_scatter | solution.py:465
  1405.2 705.0 %reduce-scatter.54.cloned.1.call-start = ((), (), s32[]{:S(2)}) async-start(), calls=%async_computation.49 | async-start | bytes 1179648 | tf_op jit(solution)/shard_map/reduce_scatter | solution.py:466
  1409.7 767.2 %reduce-scatter.44.cloned.1.call-start = ((), (), s32[]{:S(2)}) async-start(), calls=%async_computation.44 | async-start | bytes 1179648 | tf_op jit(solution)/shard_map/reduce_scatter | solution.py:461
  1414.5 828.9 %reduce-scatter.46.cloned.1.call-start = ((), (), s32[]{:S(2)}) async-start(), calls=%async_computation.45 | async-start | bytes 1179648 | tf_op jit(solution)/shard_map/reduce_scatter | solution.py:462
  1419.1 891.0 %reduce-scatter.48.cloned.1.call-start = ((), (), s32[]{:S(2)}) async-start(), calls=%async_computation.46 | async-start | bytes 1179648 | tf_op jit(solution)/shard_map/reduce_scatter | solution.py:463
  1423.7 977.5 %reduce-scatter.40.cloned.1.call-start = ((), (), s32[]{:S(2)}) async-start(), calls=%async_computation.42 | async-start | bytes 4718592 | tf_op jit(solution)/shard_map/reduce_scatter | solution.py:459
  (153 other events, 4707.7 us)
Sparse Core Ops, SparseCore 0:
  13.2 37.1 all-gather.12
  71.0 71.7 reduce-scatter.21
  148.0 34.4 all-gather.14
  252.2 71.6 reduce-scatter.23
  404.4 68.0 reduce-scatter.25
  531.4 71.6 reduce-scatter.27
  722.2 71.7 reduce-scatter.29
  891.0 71.6 reduce-scatter.31
  969.6 34.4 all-gather.24
  1045.9 68.0 reduce-scatter.33
  1228.1 71.6 reduce-scatter.35
  1344.8 88.0 reduce-scatter.59
  1436.7 63.2 reduce-scatter.55
  1503.3 62.3 reduce-scatter.49
  1569.8 86.8 reduce-scatter.41
  1659.3 71.4 reduce-scatter.37
  1735.4 149.9 reduce-scatter.61
  1889.4 86.9 reduce-scatter.57
  1980.8 63.1 reduce-scatter.51
  2047.7 62.3 reduce-scatter.53
  2114.4 62.4 reduce-scatter.43
  2180.9 62.5 reduce-scatter.45
  2247.8 62.3 reduce-scatter.47
  2314.2 86.8 reduce-scatter.39
  (6 shorter events, 202.7 us)
where the time goes:
time: 2420 us; the launch traced here: 2410 us
  waiting for transfers between devices  1740 us (72%)
  matrix products  297 us (12%)
  blocking collectives  166 us (7%)
  local copies, waits for them, and re-layouts  93.3 us (4%)
  other arithmetic  86.6 us (4%)
    reduce_scatter x4, waiting for transfers between devices, collect_grads(): return lax.psum_scatter(values, 'mp', scatter_dimension=0, tiled=True)  284 us
    reduce_scatter x4, waiting for transfers between devices, collect_rows(): return lax.psum_scatter(values, 'mp', scatter_dimension=0, tiled=True)  282 us
    all_gather x4, waiting for transfers between devices, spread_rows(): return lax.all_gather(values, 'mp', axis=0, tiled=True)  140 us
    all_gather x4, waiting for transfers between devices, spread_grads(): return lax.all_gather(values, 'mp', axis=0, tiled=True)  114 us
    reduce_scatter x1, waiting for transfers between devices, on_device(): lax.psum_scatter(grad_head, 'dp', scatter_dimension=0, tiled=True)  101 us
    dot_general x14, matrix products, weight_term(): lax.dot_general(left, right, (((0,), (0,)), ((), ())), preferred_element_...  93.9 us
    reduce_scatter x1, waiting for transfers between devices, on_device(): lax.psum_scatter(grad_second_in, 'dp', scatter_dimension=0, tiled=True)  91 us
    reduce_scatter x1, waiting for transfers between devices, on_device(): lax.psum_scatter(grad_first_in, 'dp', scatter_dimension=0, tiled=True)  91 us
  transfers between devices with their start and end apart: 31, of which 30 were waited for; matrix products, arithmetic and copies ran while one was open for 5% of the time, Pallas kernels for 0%

commit v1 on v0

--- a/solution.py
+++ b/solution.py
@@ -1,6 +1,8 @@
 import jax
 import jax.numpy as jnp
 from jax import lax
+from jax.experimental import pallas as pl
+from jax.experimental.pallas import tpu as pltpu
 from jax.sharding import PartitionSpec as P
 
 D = 1024
@@ -328,7 +330,7 @@
     return (grad_rows, grad_head, own_loss, jnp.sum(keep))
 
 
-def on_device(
+def on_device_any(
     frames,
     out_cotangent,
     lengths,
@@ -496,6 +498,505 @@
     )
 
 
+BF16 = jnp.bfloat16
+F32 = jnp.float32
+SCALE = HEAD_DIM ** (-0.5)
+CORE_PAIRS = [(0, 1), (1, 0), (2, 3), (3, 2)]
+CHIP_PAIRS = [(0, 2), (2, 0), (1, 3), (3, 1)]
+X_PAIRS = [(0, 1), (1, 0), (2, 3), (3, 2), (4, 5), (5, 4), (6, 7), (7, 6)]
+Z_NEAR_PAIRS = [(0, 2), (2, 0), (1, 3), (3, 1), (4, 6), (6, 4), (5, 7), (7, 5)]
+Z_FAR_PAIRS = [(0, 4), (4, 0), (1, 5), (5, 1), (2, 6), (6, 2), (3, 7), (7, 3)]
+
+
+def swap(values):
+    return lax.ppermute(values, "mp", CORE_PAIRS)
+
+
+def cross(values):
+    return lax.ppermute(values, "mp", CHIP_PAIRS)
+
+
+def sum_over_dp(values):
+    for pairs in (X_PAIRS, Z_NEAR_PAIRS, Z_FAR_PAIRS):
+        values = values + lax.ppermute(values, "dp", pairs)
+    return values
+
+
+def sum_over_all(values):
+    values = values + swap(values)
+    values = values + cross(values)
+    return sum_over_dp(values)
+
+
+def sum_channels(values):
+    other = cross(values)
+    half = values.shape[-1] // 2
+    turned = jnp.concatenate([other[..., half:], other[..., :half]], axis=-1)
+    return sum_over_dp(values + turned)
+
+
+def norm_forward(values, gain):
+    center = values - jnp.mean(values, axis=-1, keepdims=True)
+    spread = jnp.mean(center * center, axis=-1, keepdims=True)
+    inverse = lax.rsqrt(spread + NORM_EPSILON)
+    unit = center * inverse
+    return (unit * gain, (unit, inverse))
+
+
+def norm_backward(kept, gain, grad):
+    unit, inverse = kept
+    grad_gain = jnp.sum(grad * unit, axis=0, keepdims=True)
+    scaled = grad * gain
+    inner = jnp.mean(scaled * unit, axis=-1, keepdims=True)
+    return (inverse * (scaled - jnp.mean(scaled, axis=-1, keepdims=True) - unit * inner), grad_gain)
+
+
+def on_chip(values):
+    return jnp.concatenate([values, swap(values)], axis=0)
+
+
+def on_chip_sum(values):
+    half = values.shape[0] // 2
+    return values[:half].astype(F32) + swap(values[half:]).astype(F32)
+
+
+def gather_parts(values, number):
+    step = values.shape[0] // number
+    far = [cross(values[k * step : (k + 1) * step]) for k in range(number)]
+    near = on_chip(values)
+    return [on_chip(part) for part in far] + [near]
+
+
+def scatter_parts(parts):
+    far = [cross(on_chip_sum(part).astype(BF16)) for part in parts[:-1]]
+    far = far[0] if len(far) == 1 else jnp.concatenate(far, axis=0)
+    return on_chip_sum(parts[-1]) + far.astype(F32)
+
+
+def dot(left, right, kind=F32):
+    return jnp.dot(left, right, preferred_element_type=F32).astype(kind)
+
+
+def dot_t(left, right, kind=F32):
+    return matmul_t(left, right).astype(kind)
+
+
+def dot_rows(lefts, rights):
+    total = weight_term(lefts, rights)
+    return total.astype(BF16)
+
+
+def branch_forward(resid, gain, expand, project, number):
+    normed, norm_kept = norm_forward(resid, gain)
+    parts = gather_parts(normed.astype(BF16), number)
+    inners, actives, results = [], [], []
+    for part in parts:
+        inner = dot(part, expand)
+        inners.append(inner.astype(BF16))
+        active = swish(inner).astype(BF16)
+        actives.append(active)
+        results.append(dot(active, project, BF16))
+    return (scatter_parts(results), (norm_kept, parts, inners, actives))
+
+
+def branch_backward(gain, expand, project, kept, grad_branch, number):
+    norm_kept, parts, inners, actives = kept
+    grads = gather_parts(grad_branch.astype(BF16), number)
+    grad_inners, results = [], []
+    for grad, inner in zip(grads, inners):
+        grad_inner = (matmul_t(grad, project) * swish_slope(inner.astype(F32))).astype(BF16)
+        grad_inners.append(grad_inner)
+        results.append(dot_t(grad_inner, expand, BF16))
+    grad_resid, grad_gain = norm_backward(norm_kept, gain, scatter_parts(results))
+    whole = lambda pieces: jnp.concatenate(pieces, axis=0)
+    grad_project = dot_rows(whole(grads), whole(actives))
+    grad_expand = dot_rows(whole(parts), whole(grad_inners))
+    return (grad_resid, grad_gain, grad_expand, grad_project)
+
+
+def attend_kernel(live_ref, query_ref, keys_ref, values_ref, mixed_ref, total_ref):
+    scores = matmul_t(keys_ref[...], query_ref[...]) * SCALE
+    scores = jnp.where(live_ref[...] > 0, scores, MASKED_SCORE)
+    top = jnp.max(scores, axis=0, keepdims=True)
+    lifted = jnp.exp(scores - top)
+    total = jnp.sum(lifted, axis=0, keepdims=True)
+    mixed = weight_term(values_ref[...], lifted.astype(BF16)) * (1.0 / total)
+    mixed_ref[...] = mixed.T.astype(BF16)
+    total_ref[0] = top + jnp.log(total)
+
+
+def head_column(head, kind):
+    return (head // 2) * 6 + kind * 2 + head % 2
+
+
+def attend_forward_call(qkv, live_column):
+    length = qkv.shape[0]
+    heads = qkv.shape[1] // (3 * HEAD_DIM)
+    block = length // 2
+
+    def whole(kind):
+        return pl.BlockSpec((length, HEAD_DIM), lambda h, b: (0, head_column(h, kind)))
+
+    return pl.pallas_call(
+        attend_kernel,
+        grid=(heads, length // block),
+        in_specs=[
+            pl.BlockSpec((length, 1), lambda h, b: (0, 0)),
+            pl.BlockSpec((block, HEAD_DIM), lambda h, b: (b, head_column(h, 0))),
+            whole(1),
+            whole(2),
+        ],
+        out_specs=[
+            pl.BlockSpec((block, HEAD_DIM), lambda h, b: (b, h)),
+            pl.BlockSpec((1, 1, block), lambda h, b: (h, 0, b)),
+        ],
+        out_shape=[
+            jax.ShapeDtypeStruct((length, heads * HEAD_DIM), BF16),
+            jax.ShapeDtypeStruct((heads, 1, length), F32),
+        ],
+        compiler_params=pltpu.CompilerParams(vmem_limit_bytes=32 << 20),
+        cost_estimate=pl.CostEstimate(
+            flops=4 * heads * length * length * HEAD_DIM,
+            bytes_accessed=8 * length * heads * HEAD_DIM,
+            transcendentals=heads * length * length,
+        ),
+        name="attend_forward",
+    )(live_column, qkv, qkv, qkv)
+
+
+def attend_back_kernel(
+    live_ref, query_ref, keys_ref, values_ref, grad_ref, total_ref, out_ref, keys_sum, values_sum
+):
+    head, block = pl.program_id(0), pl.program_id(1)
+    rows = query_ref.shape[0]
+    query, keys, grad = query_ref[...], keys_ref[...], grad_ref[...]
+    scores = matmul_t(keys, query) * SCALE
+    scores = jnp.where(live_ref[...] > 0, scores, MASKED_SCORE)
+    shares = jnp.exp(scores - total_ref[0])
+    grad_shares = matmul_t(values_ref[...], grad)
+    inner = jnp.sum(shares * grad_shares, axis=0, keepdims=True)
+    grad_scores = (shares * (grad_shares - inner)).astype(BF16)
+    grad_values = dot(shares.astype(BF16), grad)
+    grad_keys = dot(grad_scores, query) * SCALE
+    grad_query = (weight_term(keys, grad_scores) * SCALE).T.astype(BF16)
+
+    def columns(kind):
+        start = head_column(head, kind) * HEAD_DIM
+        return pl.ds(pl.multiple_of(start, HEAD_DIM), HEAD_DIM)
+
+    out_ref[pl.ds(pl.multiple_of(block * rows, rows), rows), columns(0)] = grad_query
+
+    @pl.when(block == 0)
+    def _():
+        keys_sum[...] = grad_keys
+        values_sum[...] = grad_values
+
+    @pl.when(block > 0)
+    def _():
+        keys_sum[...] += grad_keys
+        values_sum[...] += grad_values
+
+    @pl.when(block == pl.num_programs(1) - 1)
+    def _():
+        out_ref[:, columns(1)] = keys_sum[...].astype(BF16)
+        out_ref[:, columns(2)] = values_sum[...].astype(BF16)
+
+
+def attend_backward_call(qkv, live_column, grad_mixed, log_total):
+    length = qkv.shape[0]
+    heads = qkv.shape[1] // (3 * HEAD_DIM)
+    block = length // 2
+
+    def whole(kind):
+        return pl.BlockSpec((length, HEAD_DIM), lambda h, b: (0, head_column(h, kind)))
+
+    return pl.pallas_call(
+        attend_back_kernel,
+        grid=(heads, length // block),
+        in_specs=[
+            pl.BlockSpec((length, 1), lambda h, b: (0, 0)),
+            pl.BlockSpec((block, HEAD_DIM), lambda h, b: (b, head_column(h, 0))),
+            whole(1),
+            whole(2),
+            pl.BlockSpec((block, HEAD_DIM), lambda h, b: (b, h)),
+            pl.BlockSpec((1, 1, block), lambda h, b: (h, 0, b)),
+        ],
+        out_specs=pl.BlockSpec(qkv.shape, lambda h, b: (0, 0)),
+        out_shape=jax.ShapeDtypeStruct(qkv.shape, BF16),
+        scratch_shapes=[pltpu.VMEM((length, HEAD_DIM), F32), pltpu.VMEM((length, HEAD_DIM), F32)],
+        compiler_params=pltpu.CompilerParams(vmem_limit_bytes=40 << 20),
+        cost_estimate=pl.CostEstimate(
+            flops=10 * heads * length * length * HEAD_DIM,
+            bytes_accessed=16 * length * heads * HEAD_DIM,
+            transcendentals=heads * length * length,
+        ),
+        name="attend_backward",
+    )(live_column, qkv, qkv, qkv, grad_mixed, log_total)
+
+
+def shifted(values, offset, position):
+    if offset == 0:
+        return values
+    moved = jnp.roll(values, -offset, axis=0)
+    place = position + offset
+    return jnp.where((place >= 0) & (place < LEN), moved, 0.0)
+
+
+def fetch_other(packed):
+    number = lax.axis_size("dp")
+    rows = packed.shape[0] // number
+    piece = lax.dynamic_slice_in_dim(packed, lax.axis_index("dp") * rows, rows)
+    return lax.all_gather(cross(piece), "dp", axis=0, tiled=True)
+
+
+def reduce_weights(grads):
+    sizes = [grad.shape[1] for grad in grads]
+    packed = grads[0] if len(grads) == 1 else jnp.concatenate(grads, axis=1)
+    reduced = lax.psum_scatter(packed, "dp", scatter_dimension=0, tiled=True).astype(F32)
+    results, start = [], 0
+    for size in sizes:
+        results.append(reduced[:, start : start + size])
+        start += size
+    return results
+
+
+def on_device_block(
+    frames,
+    out_cotangent,
+    lengths,
+    masked_rows,
+    targets,
+    head_device,
+    first_gain,
+    first_in,
+    first_out,
+    attend_gain,
+    query_weight,
+    key_weight,
+    value_weight,
+    attend_out,
+    mixer_gain,
+    mixer_value,
+    mixer_gate,
+    mixer_depth,
+    batch_scale,
+    batch_shift,
+    mixer_out,
+    second_gain,
+    second_in,
+    second_out,
+    final_gain,
+    head_weight,
+):
+    rows = frames.shape[0]
+    own = lax.axis_index("mp")
+    core, chip = own % 2, own // 2
+    length = lax.dynamic_index_in_dim(lengths, chip, 0, keepdims=False)
+    position = (jnp.arange(LEN) + core * rows) % LEN
+    live = (position < length).astype(F32)
+    live_column = live[:, None]
+    place = position[:, None]
+
+    attend_pack = jnp.concatenate(
+        [query_weight, key_weight, value_weight, attend_out.reshape(D, -1)], axis=1
+    )
+    mixer_pack = jnp.concatenate([mixer_value, mixer_gate, mixer_out.reshape(D, -1)], axis=1)
+    width = query_weight.shape[1]
+    attend_other = fetch_other(attend_pack)
+    mixer_other = fetch_other(mixer_pack)
+
+    start = frames.astype(F32)
+    branch, first_kept = branch_forward(start, first_gain, first_in, first_out, 2)
+    after_first = start + 0.5 * branch
+
+    qkv_weight = jnp.concatenate([attend_pack[:, : 3 * width], attend_other[:, : 3 * width]], axis=1)
+    attend_out_both = jnp.concatenate(
+        [attend_out, attend_other[:, 3 * width :].reshape(width, D)], axis=0
+    )
+    normed, attend_norm = norm_forward(after_first, attend_gain)
+    attend_in = on_chip(normed.astype(BF16))
+    qkv = dot(attend_in, qkv_weight, BF16)
+    mixed, log_total = attend_forward_call(qkv, live_column)
+    after_attend = after_first + on_chip_sum(dot(mixed, attend_out_both, BF16))
+
+    value_both = jnp.concatenate([mixer_value, mixer_other[:, :width]], axis=1)
+    gate_both = jnp.concatenate([mixer_gate, mixer_other[:, width : 2 * width]], axis=1)
+    mixer_out_both = jnp.concatenate(
+        [mixer_out, mixer_other[:, 2 * width :].reshape(width, D)], axis=0
+    )
+    channels = jnp.concatenate([mixer_depth, batch_scale[None], batch_shift[None]], axis=0)
+    channels = jnp.concatenate([channels, cross(channels)], axis=1)
+    depth, scale_both, shift_both = channels[:KERNEL], channels[KERNEL], channels[KERNEL + 1]
+    normed, mixer_norm = norm_forward(after_attend, mixer_gain)
+    mixer_in = on_chip(normed.astype(BF16))
+    value_in = dot(mixer_in, value_both)
+    gate_in = dot(mixer_in, gate_both)
+    gate = jax.nn.sigmoid(gate_in)
+    glu = value_in * gate * live_column
+    half = KERNEL // 2
+    convolved = sum(shifted(glu, j - half, place) * depth[j] for j in range(KERNEL))
+    weighted = convolved * live_column
+    sums = jnp.stack(
+        [
+            jnp.sum(weighted, axis=0),
+            jnp.sum(weighted * convolved, axis=0),
+            jnp.broadcast_to(jnp.sum(live), (2 * width,)),
+        ]
+    )
+    sums = sum_channels(sums)
+    count = sums[2]
+    bn_mean = sums[0] / count
+    inverse = lax.rsqrt(sums[1] / count - bn_mean * bn_mean + NORM_EPSILON)
+    normal = (convolved - bn_mean) * inverse
+    shaped = normal * scale_both + shift_both
+    mixer_active = swish(shaped).astype(BF16)
+    after_mixer = after_attend + on_chip_sum(dot(mixer_active, mixer_out_both, BF16))
+
+    branch, second_kept = branch_forward(after_mixer, second_gain, second_in, second_out, 2)
+    after_second = after_mixer + 0.5 * branch
+    output, final_norm = norm_forward(after_second, final_gain)
+
+    own_live = live[:rows]
+    picker = (masked_rows[:, None] == jnp.arange(rows)[None, :]).astype(BF16)
+    keep = jnp.sum(picker.astype(F32) * own_live[None, :], axis=1)
+    chosen = dot(picker, output.astype(BF16), BF16)
+    labels = (targets + 1) * (keep > 0).astype(jnp.int32)
+    codes = on_chip(labels[None, :])
+    codes = jnp.concatenate([cross(codes), codes], axis=0)
+    slots = masked_rows.shape[0]
+    vocab = head_weight.shape[1]
+    head_parts = gather_parts(chosen, 1)
+    logits = [dot(part, head_weight) for part in head_parts]
+    top = [jnp.max(part, axis=1) for part in logits]
+    total = [jnp.sum(jnp.exp(part - peak[:, None]), axis=1) for part, peak in zip(logits, top)]
+    pair = jnp.stack([jnp.concatenate(top), jnp.concatenate(total)]).reshape(2, 4, slots)
+
+    def merge(first, second):
+        peak = jnp.maximum(first[0], second[0])
+        return jnp.stack(
+            [peak, first[1] * jnp.exp(first[0] - peak) + second[1] * jnp.exp(second[0] - peak)]
+        )
+
+    other = swap(pair)
+    pair = merge(pair, jnp.stack([other[:, 1], other[:, 0], other[:, 3], other[:, 2]], axis=1))
+    other = cross(pair)
+    pair = merge(pair, jnp.concatenate([other[:, 2:], other[:, :2]], axis=1))
+    log_totals = (pair[0] + jnp.log(pair[1])).reshape(2, 2 * slots)
+    codes = codes.reshape(2, 2 * slots)
+    own_loss = jnp.sum((codes[1, :slots] > 0).astype(F32) * log_totals[1, :slots])
+    grad_logits, head_results = [], []
+    for k in range(2):
+        hits = (codes[k] - 1 - own * vocab)[:, None] == jnp.arange(vocab)[None, :]
+        counted = (codes[k] > 0).astype(F32)
+        own_loss = own_loss - jnp.sum(jnp.where(hits, logits[k], 0.0))
+        shares = jnp.exp(logits[k] - log_totals[k][:, None])
+        grad = (counted[:, None] * (shares - hits.astype(F32))).astype(BF16)
+        grad_logits.append(grad)
+        head_results.append(dot_t(grad, head_weight, BF16))
+    grad_head = dot_rows(jnp.concatenate(head_parts), jnp.concatenate(grad_logits))
+    grad_chosen = scatter_parts(head_results).astype(BF16)
+    grad_output = out_cotangent.astype(F32) + weight_term(picker, grad_chosen)
+    (grad_head,) = reduce_weights([grad_head])
+    grad_second, final_gain_grad = norm_backward(final_norm, final_gain, grad_output)
+
+    back, second_gain_grad, grad_second_in, grad_second_out = branch_backward(
+        second_gain, second_in, second_out, second_kept, 0.5 * grad_second, 2
+    )
+    grad_mixer = grad_second + back
+    grad_second_in, grad_second_out = reduce_weights([grad_second_in, grad_second_out])
+
+    grad_full = on_chip(grad_mixer.astype(BF16))
+    grad_shaped = dot_t(grad_full, mixer_out_both) * swish_slope(shaped)
+    sums = sum_channels(
+        jnp.stack([jnp.sum(grad_shaped, axis=0), jnp.sum(grad_shaped * normal, axis=0)])
+    )
+    batch_shift_grad, batch_scale_grad = sums[0], sums[1]
+    grad_conv = (
+        scale_both
+        * inverse
+        * (grad_shaped - live_column / count * (batch_shift_grad + normal * batch_scale_grad))
+    )
+    depth_grad = jnp.stack(
+        [jnp.sum(grad_conv * shifted(glu, j - half, place), axis=0) for j in range(KERNEL)]
+    )
+    grad_glu = sum(shifted(grad_conv, half - j, place) * depth[j] for j in range(KERNEL))
+    grad_glu = grad_glu * live_column
+    grad_value = (grad_glu * gate).astype(BF16)
+    grad_gate = (grad_glu * value_in * gate * (1.0 - gate)).astype(BF16)
+    summed = matmul_t(grad_value, value_both) + matmul_t(grad_gate, gate_both)
+    back, mixer_gain_grad = norm_backward(mixer_norm, mixer_gain, on_chip_sum(summed.astype(BF16)))
+    grad_attend = grad_mixer + back
+    mixer_grads = [
+        dot_rows(mixer_in, grad_value),
+        dot_rows(mixer_in, grad_gate),
+        dot_rows(grad_full, mixer_active),
+    ]
+    mixer_grads = [
+        jnp.concatenate([grad[:, :width] for grad in mixer_grads], axis=1),
+        jnp.concatenate([grad[:, width:] for grad in mixer_grads], axis=1),
+    ]
+    mixer_grads = (mixer_grads[0].astype(F32) + cross(mixer_grads[1]).astype(F32)).astype(BF16)
+    depth_grad = sum_channels(depth_grad)
+
+    grad_full = on_chip(grad_attend.astype(BF16))
+    grad_mixed = dot_t(grad_full, attend_out_both, BF16)
+    grad_qkv = attend_backward_call(qkv, live_column, grad_mixed, log_total)
+    summed = dot_t(grad_qkv, qkv_weight, BF16)
+    back, attend_gain_grad = norm_backward(attend_norm, attend_gain, on_chip_sum(summed))
+    grad_first = grad_attend + back
+    qkv_grad = dot_rows(attend_in, grad_qkv)
+    out_grad = dot_rows(grad_full, mixed)
+    attend_grads = [
+        jnp.concatenate([qkv_grad[:, : 3 * width], out_grad[:, :width]], axis=1),
+        jnp.concatenate([qkv_grad[:, 3 * width :], out_grad[:, width:]], axis=1),
+    ]
+    attend_grads = (attend_grads[0].astype(F32) + cross(attend_grads[1]).astype(F32)).astype(BF16)
+    (middle,) = reduce_weights([jnp.concatenate([mixer_grads, attend_grads], axis=1)])
+    grad_mixer_value, grad_mixer_gate, grad_mixer_out, grad_query, grad_key, grad_value, grad_out = (
+        jnp.split(middle, 7, axis=1)
+    )
+
+    back, first_gain_grad, grad_first_in, grad_first_out = branch_backward(
+        first_gain, first_in, first_out, first_kept, 0.5 * grad_first, 2
+    )
+    input_grad = grad_first + back
+    grad_first_out, grad_first_in = reduce_weights([grad_first_out, grad_first_in])
+
+    counts = jnp.stack([own_loss, jnp.sum(keep)])
+    counts = jnp.concatenate([counts, jnp.zeros((D - 2,), F32)])[None]
+    gains = jnp.concatenate(
+        [attend_gain_grad, mixer_gain_grad, second_gain_grad, final_gain_grad, counts], axis=0
+    )
+    gains = sum_over_all(gains)
+    first_gain_grad = sum_over_all(first_gain_grad)[0]
+    loss = gains[4, 0] / gains[4, 1]
+    return (
+        output,
+        loss,
+        input_grad,
+        first_gain_grad,
+        grad_first_in,
+        grad_first_out.T,
+        gains[0],
+        grad_query,
+        grad_key,
+        grad_value,
+        grad_out.T,
+        gains[1],
+        grad_mixer_value,
+        grad_mixer_gate,
+        depth_grad[:, :width],
+        batch_scale_grad[:width],
+        batch_shift_grad[:width],
+        grad_mixer_out.T,
+        gains[2],
+        grad_second_in,
+        grad_second_out.T,
+        gains[3],
+        grad_head,
+    )
+
+
 def solution(mesh):
     in_specs = (
         P(("dp", "mp"), None),
@@ -550,6 +1051,8 @@
         P(),
         P("dp", "mp"),
     )
+    small = mesh.shape["dp"] == 8 and mesh.shape["mp"] == 4
+    on_device = on_device_block if small else on_device_any
     return jax.shard_map(
         on_device, mesh=mesh, in_specs=in_specs, out_specs=out_specs, check_vma=False
     )

time: 2420 us -> 792 us (0.33)
  waiting for transfers between devices: 1740 us -> 333 us
  blocking collectives: 166 us -> 0 us
  matrix products: 297 us -> 151 us
  starting transfers between devices: 6.92 us -> 64.6 us
  Pallas kernels: 0 us -> 29.1 us
    reduce_scatter x21 -> x2, waiting for transfers between devices: 1460 us -> 0.02 us  [reduce_weights(): lax.psum_scatter(packed, 'dp', scatter_dimension=0, tiled=True).astype(F32)]
    ppermute x0 -> x85, waiting for transfers between devices: none -> 254 us  [the longest x30 221 us: cross(): return lax.ppermute(values, 'mp', CHIP_PAIRS)]
    all_gather x9 -> x2, waiting for transfers between devices: 267 us -> 36.4 us  [fetch_other(): return lax.all_gather(cross(piece), 'dp', axis=0, tiled=True)]
    psum x3 -> x0, blocking collectives: 87.6 us -> none  [the longest x1 44.3 us: on_device(): lax.psum((first_gain_grad, attend_gain_grad, mixer_gain_grad, second_gain...]
    dot_general x26 -> x20, matrix products: 127 us -> 62.1 us  [dot(): return jnp.dot(left, right, preferred_element_type=F32).astype(kind)]
    ppermute x0 -> x85, starting transfers between devices: none -> 64.1 us  [the longest x30 38.3 us: cross(): return lax.ppermute(values, 'mp', CHIP_PAIRS)]
    all_to_all x2 -> x0, blocking collectives: 62.2 us -> none  [the longest x1 31.2 us: masked_head(): lax.all_to_all(packed, 'dp', split_axis=0, concat_axis=0, tiled=True)]
    dot_general x14 -> x11, matrix products: 93.9 us -> 46.3 us  [weight_term(): lax.dot_general(left, right, (((0,), (0,)), ((), ())), preferred_element_...]
  transfers between devices with their start and end apart: 31 -> 91, of which waited for: 30 -> 40; matrix products, arithmetic and copies ran while one was open for 5% -> 32% of each run, Pallas kernels for 0% -> 2%
where the time goes in v1:
time: 792 us; the launch traced here: 780 us
  waiting for transfers between devices  333 us (42%)
  matrix products  151 us (19%)
  other arithmetic  98 us (12%)
  local copies, waits for them, and re-layouts  82.1 us (10%)
  starting transfers between devices  64.6 us (8%)
  Pallas kernels  29.1 us (4%)
  between operations  22.1 us (3%)
    ppermute x30, waiting for transfers between devices, cross(): return lax.ppermute(values, 'mp', CHIP_PAIRS)  221 us
    dot_general x20, matrix products, dot(): return jnp.dot(left, right, preferred_element_type=F32).astype(kind)  62.1 us
    unnamed x461, local copies, waits for them, and re-layouts  50.2 us
    dot_general x11, matrix products, weight_term(): lax.dot_general(left, right, (((0,), (0,)), ((), ())), preferred_element_...  46.3 us
    dot_general x19, matrix products, matmul_t(): lax.dot_general(left, right, (((1,), (1,)), ((), ())), preferred_element_...  42.5 us
    unnamed x8, waiting for transfers between devices  42.2 us
    ppermute x30, starting transfers between devices, cross(): return lax.ppermute(values, 'mp', CHIP_PAIRS)  38.3 us
    all_gather x2, waiting for transfers between devices, fetch_other(): return lax.all_gather(cross(piece), 'dp', axis=0, tiled=True)  36.4 us
  transfers between devices with their start and end apart: 91, of which 40 were waited for; matrix products, arithmetic and copies ran while one was open for 32% of the time, Pallas kernels for 2%

profile of v1, /device:TPU:0, one launch (start us, length us, event | category | flops | bytes accessed | tf_op | source)
XLA Modules:
  0.0 779.7 jit_solution(399005492399227347)
XLA Ops:
  17.5 12.8 %collective-permute-done.2 = bf16[256,1024]{1,0:T(8,128)(2,1)} collective-permute-done((bf16[256,1024]{1,0:T(8,128)(2,1)S(1)}, bf16[256,1024]{1,0:T(8,128)(2,1)}, u32[]{:S(2)}, u32[]{:S(2)}) %collective-permute-start.2) | collective-permute-done | bytes 524320 | tf_op jit(solution)/shard_map/ppermute | solution.py:516
  34.0 12.3 %collective-permute-done.11 = bf16[128,1024]{1,0:T(8,128)(2,1)S(1)} collective-permute-done((bf16[128,1024]{1,0:T(8,128)(2,1)S(1)}, bf16[128,1024]{1,0:T(8,128)(2,1)S(1)}, u32[]{:S(2)}, u32[]{:S(2)}) %collective-permute-start.11) | collective-permute-done | bytes 262176 | tf_op jit(solution)/shard_map/ppermute | solution.py:516
  69.8 12.4 %collective-permute-done.5 = bf16[256,1024]{1,0:T(8,128)(2,1)S(1)} collective-permute-done((bf16[256,1024]{1,0:T(8,128)(2,1)S(1)}, bf16[256,1024]{1,0:T(8,128)(2,1)S(1)}, u32[]{:S(2)}, u32[]{:S(2)}) %collective-permute-start.5) | collective-permute-done | bytes 524320 | tf_op jit(solution)/shard_map/ppermute | solution.py:516
  82.2 10.7 %collective-permute-done.9 = bf16[256,1024]{1,0:T(8,128)(2,1)S(1)} collective-permute-done((bf16[256,1024]{1,0:T(8,128)(2,1)S(1)}, bf16[256,1024]{1,0:T(8,128)(2,1)S(1)}, u32[]{:S(2)}, u32[]{:S(2)}) %collective-permute-start.9) | collective-permute-done | bytes 524320 | tf_op jit(solution)/shard_map/ppermute | solution.py:516
  108.9 10.6 %attend_forward.1 = (bf16[1024,512]{1,0:T(8,128)(2,1)S(1)}, f32[4,1,1024]{2,1,0:T(1,128)S(1)}) custom-call(f32[1024,1]{1,0:T(8,128)S(1)} %fusion.183.live_ref, bf16[1024,1536]{1,0:T(8,128)(2,1)S(1)} %convolution_convert_fusion.1.query_ref.keys_ref.values_ref, bf16[1024,1536]{1,0:T(8,128)(2,1)S(1)} %convolution_convert_fusion.1.query_ref.keys_ref.values_ref, ...), custom_call_target="tpu_custom_call" | custom-call | flops 2147483648 | bytes 4194304 | tf_op jit(solution)/shard_map/attend_forward/pallas_call | solution.py:640
  142.2 36.4 %all-gather.5.cloned.1.call-done = bf16[1024,768]{1,0:T(8,128)(2,1)} async-done(((bf16[128,768]{1,0:T(8,128)(2,1)}), bf16[1024,768]{1,0:T(8,128)(2,1)}) %all-gather.5.cloned.1.call-update) | async-done | bytes 1572880 | tf_op jit(solution)/shard_map/all_gather | solution.py:749
  223.2 12.7 %collective-permute-done.23 = bf16[256,1024]{1,0:T(8,128)(2,1)S(1)} collective-permute-done((bf16[256,1024]{1,0:T(8,128)(2,1)S(1)}, bf16[256,1024]{1,0:T(8,128)(2,1)S(1)}, u32[]{:S(2)}, u32[]{:S(2)}) %collective-permute-start.23) | collective-permute-done | bytes 524320 | tf_op jit(solution)/shard_map/ppermute | solution.py:516
  236.0 10.7 %collective-permute-done.27 = bf16[256,1024]{1,0:T(8,128)(2,1)S(1)} collective-permute-done((bf16[256,1024]{1,0:T(8,128)(2,1)S(1)}, bf16[256,1024]{1,0:T(8,128)(2,1)S(1)}, u32[]{:S(2)}, u32[]{:S(2)}) %collective-permute-start.27) | collective-permute-done | bytes 524320 | tf_op jit(solution)/shard_map/ppermute | solution.py:516
  265.9 11.7 %collective-permute-done.26 = bf16[256,1024]{1,0:T(8,128)(2,1)S(1)} collective-permute-done((bf16[256,1024]{1,0:T(8,128)(2,1)S(1)}, bf16[256,1024]{1,0:T(8,128)(2,1)S(1)}, u32[]{:S(2)}, u32[]{:S(2)}) %collective-permute-start.26) | collective-permute-done | bytes 524320 | tf_op jit(solution)/shard_map/ppermute | solution.py:516
  277.5 10.3 %collective-permute-done.30 = bf16[256,1024]{1,0:T(8,128)(2,1)S(1)} collective-permute-done((bf16[256,1024]{1,0:T(8,128)(2,1)S(1)}, bf16[256,1024]{1,0:T(8,128)(2,1)S(1)}, u32[]{:S(2)}, u32[]{:S(2)}) %collective-permute-start.30) | collective-permute-done | bytes 524320 | tf_op jit(solution)/shard_map/ppermute | solution.py:516
  294.6 11.0 %collective-permute-done.38 = s32[2,256]{1,0:T(2,128)S(1)} collective-permute-done((s32[2,256]{1,0:T(2,128)S(1)}, s32[2,256]{1,0:T(2,128)S(1)}, u32[]{:S(2)}, u32[]{:S(2)}) %collective-permute-start.38) | collective-permute-done | bytes 2080 | tf_op jit(solution)/shard_map/ppermute | solution.py:516
  344.0 12.3 %collective-permute-done.40 = bf16[256,1024]{1,0:T(8,128)(2,1)S(1)} collective-permute-done((bf16[256,1024]{1,0:T(8,128)(2,1)S(1)}, bf16[256,1024]{1,0:T(8,128)(2,1)S(1)}, u32[]{:S(2)}, u32[]{:S(2)}) %collective-permute-start.40) | collective-permute-done | bytes 524320 | tf_op jit(solution)/shard_map/ppermute | solution.py:516
  363.3 11.8 %collective-permute-done.43 = bf16[256,1024]{1,0:T(8,128)(2,1)S(1)} collective-permute-done((bf16[256,1024]{1,0:T(8,128)(2,1)S(1)}, bf16[256,1024]{1,0:T(8,128)(2,1)S(1)}, u32[]{:S(2)}, u32[]{:S(2)}) %collective-permute-start.43) | collective-permute-done | bytes 524320 | tf_op jit(solution)/shard_map/ppermute | solution.py:516
  375.1 10.8 %collective-permute-done.47 = bf16[256,1024]{1,0:T(8,128)(2,1)S(1)} collective-permute-done((bf16[256,1024]{1,0:T(8,128)(2,1)S(1)}, bf16[256,1024]{1,0:T(8,128)(2,1)S(1)}, u32[]{:S(2)}, u32[]{:S(2)}) %collective-permute-start.47) | collective-permute-done | bytes 524320 | tf_op jit(solution)/shard_map/ppermute | solution.py:516
  406.4 7.4 fusion.42
  418.4 10.5 %collective-permute-done.50 = bf16[256,1024]{1,0:T(8,128)(2,1)} collective-permute-done((bf16[256,1024]{1,0:T(8,128)(2,1)}, bf16[256,1024]{1,0:T(8,128)(2,1)}, u32[]{:S(2)}, u32[]{:S(2)}) %collective-permute-start.50) | collective-permute-done | bytes 524320 | tf_op jit(solution)/shard_map/ppermute | solution.py:516
  457.3 7.3 fusion.121
  483.2 6.5 copy.73
  515.4 18.5 %attend_backward.1 = bf16[1024,1536]{1,0:T(8,128)(2,1)S(1)} custom-call(f32[1024,1]{1,0:T(8,128)S(1)} %fusion.183.live_ref, bf16[1024,1536]{1,0:T(8,128)(2,1)S(1)} %copy-done.3, bf16[1024,1536]{1,0:T(8,128)(2,1)S(1)} %copy-done.3, bf16[1024,1536]{1,0:T(8,128)(2,1)S(1)} %copy-done.3, bf16[1024,512]{1,0:T(8,128)(2,1)S(1)} %convolution_convert_fusion.15.grad_ref, ...), custom_call_target="tpu_custom_call" | custom-call | flops 5368709120 | bytes 8388608 | tf_op jit(solution)/shard_map/attend_backward/pallas_call | solution.py:713
  556.0 34.9 %collective-permute-done.80 = bf16[1024,1024]{1,0:T(8,128)(2,1)} collective-permute-done((bf16[1024,1024]{1,0:T(8,128)(2,1)}, bf16[1024,1024]{1,0:T(8,128)(2,1)}, u32[]{:S(2)}, u32[]{:S(2)}) %collective-permute-start.80) | collective-permute-done | bytes 2097184 | tf_op jit(solution)/shard_map/ppermute | solution.py:516
  605.9 9.4 %collective-permute-done.66 = bf16[256,1024]{1,0:T(8,128)(2,1)S(1)} collective-permute-done((bf16[256,1024]{1,0:T(8,128)(2,1)S(1)}, bf16[256,1024]{1,0:T(8,128)(2,1)S(1)}, u32[]{:S(2)}, u32[]{:S(2)}) %collective-permute-start.66) | collective-permute-done | bytes 524320 | tf_op jit(solution)/shard_map/ppermute | solution.py:516
  615.3 9.4 %collective-permute-done.70 = bf16[256,1024]{1,0:T(8,128)(2,1)S(1)} collective-permute-done((bf16[256,1024]{1,0:T(8,128)(2,1)S(1)}, bf16[256,1024]{1,0:T(8,128)(2,1)S(1)}, u32[]{:S(2)}, u32[]{:S(2)}) %collective-permute-start.70) | collective-permute-done | bytes 524320 | tf_op jit(solution)/shard_map/ppermute | solution.py:516
  649.2 6.6 copy.71
  726.0 42.1 %reduce-scatter.13.cloned.1.call-done = bf16[128,2048]{1,0:T(8,128)(2,1)} async-done(((bf16[1024,2048]{1,0:T(8,128)(2,1)}), bf16[128,2048]{1,0:T(8,128)(2,1)}) %reduce-scatter.13.cloned.1.call-update) | async-done | bytes 524304
  (889 shorter events, 418.4 us)
Async XLA Ops:
  7.2 90.8 %all-gather.3.cloned.1.call-start = ((), (), s32[]{:S(2)}) async-start(), calls=%async_computation.4 | async-start | bytes 2359296 | tf_op jit(solution)/shard_map/all_gather | solution.py:749
  17.5 29.6 %collective-permute-start.6 = (bf16[256,1024]{1,0:T(8,128)(2,1)}, bf16[256,1024]{1,0:T(8,128)(2,1)}, u32[]{:S(2)}, u32[]{:S(2)}) collective-permute-start(bf16[256,1024]{1,0:T(8,128)(2,1)} %get-tuple-element.191), channel_id=1, source_target_pairs={{0,2},{2,0},{1,3},{3,1},{4,6},{6,4},{5,7},{7,5},{8,10},{10,8},{9,1... | collective-permute-start | bytes 1572872 | tf_op jit(solution)/shard_map/ppermute | solution.py:516
  33.8 25.3 %collective-permute-start = (bf16[512,1024]{1,0:T(8,128)(2,1)}, bf16[512,1024]{1,0:T(8,128)(2,1)}, u32[]{:S(2)}, u32[]{:S(2)}) collective-permute-start(bf16[512,1024]{1,0:T(8,128)(2,1)} %fusion.53), channel_id=1, source_target_pairs={{0,1},{1,0},{2,3},{3,2},{4,5},{5,4},{6,7},{7,6},{8,9},{9,8},{10,11... | collective-permute-start | bytes 3145736 | tf_op jit(solution)/shard_map/ppermute | solution.py:512
  47.0 131.6 %all-gather.5.cloned.1.call-start = ((), (), s32[]{:S(2)}) async-start(), calls=%async_computation.5 | async-start | bytes 1769472 | tf_op jit(solution)/shard_map/all_gather | solution.py:749
  67.0 25.9 %collective-permute-start.1 = (bf16[512,1024]{1,0:T(8,128)(2,1)S(1)}, bf16[512,1024]{1,0:T(8,128)(2,1)S(1)}, u32[]{:S(2)}, u32[]{:S(2)}) collective-permute-start(bf16[512,1024]{1,0:T(8,128)(2,1)S(1)} %slice.540), channel_id=1, source_target_pairs={{0,1},{1,0},{2,3},{3,2},{4,5},{5,4},{6,7},{7,6},{8,9},{9,8},{10,11... | collective-permute-start | bytes 3145736 | tf_op jit(solution)/shard_map/ppermute | solution.py:512
  69.4 23.5 %collective-permute-start.9 = (bf16[256,1024]{1,0:T(8,128)(2,1)S(1)}, bf16[256,1024]{1,0:T(8,128)(2,1)S(1)}, u32[]{:S(2)}, u32[]{:S(2)}) collective-permute-start(bf16[256,1024]{1,0:T(8,128)(2,1)S(1)} %add_convert_fusion.11), channel_id=1, source_target_pairs={{0,2},{2,0},{1,3},{3,1},{4,6},{6,4},{5,7},{7,5},{8,10},{10,8},{9,1... | collective-permute-start | bytes 1572872 | tf_op jit(solution)/shard_map/ppermute | solution.py:516
  132.8 570.7 %reduce-scatter.11.cloned.1.call-start = ((), (), s32[]{:S(2)}) async-start(), calls=%async_computation.7 | async-start | bytes 4718592 | tf_op jit(solution)/shard_map/reduce_scatter | solution.py:755
  137.5 43.4 %collective-permute-start.13 = (bf16[512,1024]{1,0:T(8,128)(2,1)}, bf16[512,1024]{1,0:T(8,128)(2,1)}, u32[]{:S(2)}, u32[]{:S(2)}) collective-permute-start(bf16[512,1024]{1,0:T(8,128)(2,1)} %multiply_convert_fusion.12), channel_id=1, source_target_pairs={{0,1},{1,0},{2,3},{3,2},{4,5},{5,4},{6,7},{7,6},{8,9},{9,8},{10,11... | collective-permute-start | bytes 3145736 | tf_op jit(solution)/shard_map/ppermute | solution.py:512
  220.8 25.8 %collective-permute-start.21 = (bf16[512,1024]{1,0:T(8,128)(2,1)S(1)}, bf16[512,1024]{1,0:T(8,128)(2,1)S(1)}, u32[]{:S(2)}, u32[]{:S(2)}) collective-permute-start(bf16[512,1024]{1,0:T(8,128)(2,1)S(1)} %multiply_convert_fusion.10), channel_id=1, source_target_pairs={{0,1},{1,0},{2,3},{3,2},{4,5},{5,4},{6,7},{7,6},{8,9},{9,8},{10,11... | collective-permute-start | bytes 3145736 | tf_op jit(solution)/shard_map/ppermute | solution.py:512
  222.7 24.0 %collective-permute-start.27 = (bf16[256,1024]{1,0:T(8,128)(2,1)S(1)}, bf16[256,1024]{1,0:T(8,128)(2,1)S(1)}, u32[]{:S(2)}, u32[]{:S(2)}) collective-permute-start(bf16[256,1024]{1,0:T(8,128)(2,1)S(1)} %get-tuple-element.189), channel_id=1, source_target_pairs={{0,2},{2,0},{1,3},{3,1},{4,6},{6,4},{5,7},{7,5},{8,10},{10,8},{9,1... | collective-permute-start | bytes 1572872 | tf_op jit(solution)/shard_map/ppermute | solution.py:516
  264.4 23.4 %collective-permute-start.30 = (bf16[256,1024]{1,0:T(8,128)(2,1)S(1)}, bf16[256,1024]{1,0:T(8,128)(2,1)S(1)}, u32[]{:S(2)}, u32[]{:S(2)}) collective-permute-start(bf16[256,1024]{1,0:T(8,128)(2,1)S(1)} %add_convert_fusion.9), channel_id=1, source_target_pairs={{0,2},{2,0},{1,3},{3,1},{4,6},{6,4},{5,7},{7,5},{8,10},{10,8},{9,1... | collective-permute-start | bytes 1572872 | tf_op jit(solution)/shard_map/ppermute | solution.py:516
  360.1 25.8 %collective-permute-start.41 = (bf16[512,1024]{1,0:T(8,128)(2,1)S(1)}, bf16[512,1024]{1,0:T(8,128)(2,1)S(1)}, u32[]{:S(2)}, u32[]{:S(2)}) collective-permute-start(bf16[512,1024]{1,0:T(8,128)(2,1)S(1)} %get-tuple-element.141), channel_id=1, source_target_pairs={{0,1},{1,0},{2,3},{3,2},{4,5},{5,4},{6,7},{7,6},{8,9},{9,8},{10,11... | collective-permute-start | bytes 3145736 | tf_op jit(solution)/shard_map/ppermute | solution.py:512
  361.9 24.1 %collective-permute-start.47 = (bf16[256,1024]{1,0:T(8,128)(2,1)S(1)}, bf16[256,1024]{1,0:T(8,128)(2,1)S(1)}, u32[]{:S(2)}, u32[]{:S(2)}) collective-permute-start(bf16[256,1024]{1,0:T(8,128)(2,1)S(1)} %get-tuple-element.187), channel_id=1, source_target_pairs={{0,2},{2,0},{1,3},{3,1},{4,6},{6,4},{5,7},{7,5},{8,10},{10,8},{9,1... | collective-permute-start | bytes 1572872 | tf_op jit(solution)/shard_map/ppermute | solution.py:516
  405.9 23.0 %collective-permute-start.50 = (bf16[256,1024]{1,0:T(8,128)(2,1)}, bf16[256,1024]{1,0:T(8,128)(2,1)}, u32[]{:S(2)}, u32[]{:S(2)}) collective-permute-start(bf16[256,1024]{1,0:T(8,128)(2,1)} %add_convert_fusion.5), channel_id=1, source_target_pairs={{0,2},{2,0},{1,3},{3,1},{4,6},{6,4},{5,7},{7,5},{8,10},{10,8},{9,1... | collective-permute-start | bytes 1572872 | tf_op jit(solution)/shard_map/ppermute | solution.py:516
  413.8 305.4 %reduce-scatter.15.cloned.1.call-start = ((), (), s32[]{:S(2)}) async-start(), calls=%async_computation.9 | async-start | bytes 4718592
  489.7 232.8 %reduce-scatter.9.cloned.1.call-start = ((), (), s32[]{:S(2)}) async-start(), calls=%async_computation.6 | async-start | bytes 4128768 | tf_op jit(solution)/shard_map/reduce_scatter | solution.py:755
  509.4 38.7 %collective-permute-start.79 = (bf16[1024,768]{0,1:T(8,128)(2,1)S(1)}, bf16[1024,768]{0,1:T(8,128)(2,1)S(1)}, u32[]{:S(2)}, u32[]{:S(2)}) collective-permute-start(bf16[1024,768]{0,1:T(8,128)(2,1)S(1)} %pad_maximum_fusion.9), channel_id=1, source_target_pairs={{0,2},{2,0},{1,3},{3,1},{4,6},{6,4},{5,7},{7,5},{8,10},{10,8},{9,1... | collective-permute-start | bytes 4718600 | tf_op jit(solution)/shard_map/ppermute | solution.py:516
  542.3 48.6 %collective-permute-start.80 = (bf16[1024,1024]{1,0:T(8,128)(2,1)}, bf16[1024,1024]{1,0:T(8,128)(2,1)}, u32[]{:S(2)}, u32[]{:S(2)}) collective-permute-start(bf16[1024,1024]{1,0:T(8,128)(2,1)} %pad_maximum_fusion.8), channel_id=1, source_target_pairs={{0,2},{2,0},{1,3},{3,1},{4,6},{6,4},{5,7},{7,5},{8,10},{10,8},{9,1... | collective-permute-start | bytes 6291464 | tf_op jit(solution)/shard_map/ppermute | solution.py:516
  595.5 172.6 %reduce-scatter.13.cloned.1.call-start = ((), (), s32[]{:S(2)}) async-start(), calls=%async_computation.8 | async-start | bytes 4718592
  601.9 22.7 %collective-permute-start.70 = (bf16[256,1024]{1,0:T(8,128)(2,1)S(1)}, bf16[256,1024]{1,0:T(8,128)(2,1)S(1)}, u32[]{:S(2)}, u32[]{:S(2)}) collective-permute-start(bf16[256,1024]{1,0:T(8,128)(2,1)S(1)} %get-tuple-element.185), channel_id=1, source_target_pairs={{0,2},{2,0},{1,3},{3,1},{4,6},{6,4},{5,7},{7,5},{8,10},{10,8},{9,1... | collective-permute-start | bytes 1572872 | tf_op jit(solution)/shard_map/ppermute | solution.py:516
  605.8 20.9 %collective-permute-start.64 = (bf16[512,1024]{1,0:T(8,128)(2,1)S(1)}, bf16[512,1024]{1,0:T(8,128)(2,1)S(1)}, u32[]{:S(2)}, u32[]{:S(2)}) collective-permute-start(bf16[512,1024]{1,0:T(8,128)(2,1)S(1)} %get-tuple-element.127), channel_id=1, source_target_pairs={{0,1},{1,0},{2,3},{3,2},{4,5},{5,4},{6,7},{7,6},{8,9},{9,8},{10,11... | collective-permute-start | bytes 3145736 | tf_op jit(solution)/shard_map/ppermute | solution.py:512
  672.3 22.1 %collective-permute-start.65 = (bf16[512,1024]{1,0:T(8,128)(2,1)S(1)}, bf16[512,1024]{1,0:T(8,128)(2,1)S(1)}, u32[]{:S(2)}, u32[]{:S(2)}) collective-permute-start(bf16[512,1024]{1,0:T(8,128)(2,1)S(1)} %slice.629), channel_id=1, source_target_pairs={{0,1},{1,0},{2,3},{3,2},{4,5},{5,4},{6,7},{7,6},{8,9},{9,8},{10,11... | collective-permute-start | bytes 3145736 | tf_op jit(solution)/shard_map/ppermute | solution.py:512
  672.6 21.8 %collective-permute-start.69 = (bf16[256,1024]{1,0:T(8,128)(2,1)S(1)}, bf16[256,1024]{1,0:T(8,128)(2,1)S(1)}, u32[]{:S(2)}, u32[]{:S(2)}) collective-permute-start(bf16[256,1024]{1,0:T(8,128)(2,1)S(1)} %add_convert_fusion.4), channel_id=1, source_target_pairs={{0,2},{2,0},{1,3},{3,1},{4,6},{6,4},{5,7},{7,5},{8,10},{10,8},{9,1... | collective-permute-start | bytes 1572872 | tf_op jit(solution)/shard_map/ppermute | solution.py:516
  673.8 24.5 %collective-permute-start.73 = (bf16[256,1024]{1,0:T(8,128)(2,1)S(1)}, bf16[256,1024]{1,0:T(8,128)(2,1)S(1)}, u32[]{:S(2)}, u32[]{:S(2)}) collective-permute-start(bf16[256,1024]{1,0:T(8,128)(2,1)S(1)} %add_convert_fusion.3), channel_id=1, source_target_pairs={{0,2},{2,0},{1,3},{3,1},{4,6},{6,4},{5,7},{7,5},{8,10},{10,8},{9,1... | collective-permute-start | bytes 1572872 | tf_op jit(solution)/shard_map/ppermute | solution.py:516
  (280 other events, 2471.6 us)
Sparse Core Ops, SparseCore 0:
  47.1 50.7 all-gather.2
  132.9 45.6 all-gather.4
  413.9 86.2 reduce-scatter.10
  504.2 87.8 reduce-scatter.14
  595.6 80.4 reduce-scatter.8
  679.6 88.4 reduce-scatter.12

commit v2 on v1

--- a/solution.py
+++ b/solution.py
@@ -586,32 +586,148 @@
     return total.astype(BF16)
 
 
-def branch_forward(resid, gain, expand, project, number):
+def after(values, *earlier):
+    return lax.optimization_barrier((values, *earlier))[0]
+
+
+def early(flops, size):
+    return pl.CostEstimate(flops=flops // 1000, bytes_accessed=size // 1000, transcendentals=0)
+
+
+BLOCK = 256
+
+
+def pieces_call(body, pieces, row_inputs, weights, row_outputs, held, start, total, name):
+    rows, width = pieces[0].shape
+    block = min(BLOCK, rows)
+    half, first = rows // block, start // block
+    steps = 2 * half
+
+    def kernel(*refs):
+        refs = list(refs)
+        inputs, refs = refs[: 2 + len(row_inputs) + len(weights)], refs[2 + len(row_inputs) + len(weights) :]
+        if held is not None:
+            refs = refs[len(held) :]
+        step = pl.program_id(0)
+        piece = jnp.where(step < half, inputs[0][...], inputs[1][...])
+        result = body(piece, inputs[2:], refs[: len(row_outputs)])
+
+        @pl.when(step < half)
+        def _():
+            refs[-2][...] = result
+
+        @pl.when(step >= half)
+        def _():
+            refs[-1][...] = result
+
+    def kept(array):
+        return pl.BlockSpec(array.shape, lambda i: (0,) * array.ndim)
+
+    def placed(size):
+        return pl.BlockSpec((block, size), lambda i: (i + first, 0))
+
+    two = [
+        pl.BlockSpec((block, width), lambda i: (jnp.minimum(i, half - 1), 0)),
+        pl.BlockSpec((block, width), lambda i: (jnp.maximum(i - half, 0), 0)),
+    ]
+    row_inputs = [pltpu.with_memory_space_constraint(array, pltpu.HBM) for array in row_inputs]
+    operands = [*pieces, *row_inputs, *weights]
+    in_specs = two + [placed(array.shape[1]) for array in row_inputs] + [kept(w) for w in weights]
+    aliases = {}
+    if held is not None:
+        aliases = {len(operands) + k: k for k in range(len(held))}
+        operands += held
+        in_specs += [pl.BlockSpec(memory_space=pl.ANY)] * len(held)
+    flops = 2 * 2 * rows * sum(w.size for w in weights if w.ndim == 2 and w.shape[0] > 1)
+    return pl.pallas_call(
+        kernel,
+        grid=(steps,),
+        in_specs=in_specs,
+        out_specs=[placed(size) for size in row_outputs] + two,
+        out_shape=[pltpu.HBM((total, size), BF16) for size in row_outputs]
+        + [jax.ShapeDtypeStruct((rows, width), BF16)] * 2,
+        input_output_aliases=aliases,
+        compiler_params=pltpu.CompilerParams(vmem_limit_bytes=32 << 20),
+        cost_estimate=early(flops, 2 * sum(w.size for w in weights)),
+        name=name,
+    )(*operands)
+
+
+def expand_body(piece, inputs, outputs):
+    expand_ref, project_ref = inputs
+    held_ref, inner_ref, active_ref = outputs
+    inner = matmul(piece, expand_ref[...])
+    active = swish(inner).astype(BF16)
+    held_ref[...] = piece
+    inner_ref[...] = inner.astype(BF16)
+    active_ref[...] = active
+    return matmul(active, project_ref[...]).astype(BF16)
+
+
+def expand_back_body(piece, inputs, outputs):
+    inner_ref, expand_ref, project_ref = inputs
+    held_ref, grad_ref = outputs
+    slope = swish_slope(inner_ref[...].astype(F32))
+    grad = (matmul_t(piece, project_ref[...]) * slope).astype(BF16)
+    held_ref[...] = piece
+    grad_ref[...] = grad
+    return matmul_t(grad, expand_ref[...]).astype(BF16)
+
+
+def swap_halves(values):
+    half = values.shape[0] // 2
+    return jnp.concatenate([swap(values[:half]), swap(values[half:])], axis=0)
+
+
+def branch_over(values, number, call, beside=None):
+    rows = values.shape[0]
+    step = rows // number
+    far = [cross(values[k * step : (k + 1) * step]) for k in range(number)]
+    held, (own, other) = call((values, swap(values)), None, 0)
+    near = own.astype(F32) + swap(other).astype(F32)
+    done, back = own, []
+    for k in range(number):
+        part = after(far[k], done) if beside is None else after(far[k], done, *beside[k]())
+        held, (own, other) = call((part, swap_halves(part)), held, 2 * rows + 2 * step * k)
+        result = (own.astype(F32) + swap_halves(other).astype(F32)).astype(BF16)
+        result = after(result, *back)
+        back.append(cross(result))
+        done = own
+    return (near + jnp.concatenate(back, axis=0).astype(F32), held, result)
+
+
+def branch_forward(resid, gain, expand, project, number, beside=None):
     normed, norm_kept = norm_forward(resid, gain)
-    parts = gather_parts(normed.astype(BF16), number)
-    inners, actives, results = [], [], []
-    for part in parts:
-        inner = dot(part, expand)
-        inners.append(inner.astype(BF16))
-        active = swish(inner).astype(BF16)
-        actives.append(active)
-        results.append(dot(active, project, BF16))
-    return (scatter_parts(results), (norm_kept, parts, inners, actives))
-
-
-def branch_backward(gain, expand, project, kept, grad_branch, number):
-    norm_kept, parts, inners, actives = kept
-    grads = gather_parts(grad_branch.astype(BF16), number)
-    grad_inners, results = [], []
-    for grad, inner in zip(grads, inners):
-        grad_inner = (matmul_t(grad, project) * swish_slope(inner.astype(F32))).astype(BF16)
-        grad_inners.append(grad_inner)
-        results.append(dot_t(grad_inner, expand, BF16))
-    grad_resid, grad_gain = norm_backward(norm_kept, gain, scatter_parts(results))
-    whole = lambda pieces: jnp.concatenate(pieces, axis=0)
-    grad_project = dot_rows(whole(grads), whole(actives))
-    grad_expand = dot_rows(whole(parts), whole(grad_inners))
-    return (grad_resid, grad_gain, grad_expand, grad_project)
+    total = 4 * resid.shape[0]
+    sizes = [resid.shape[1], expand.shape[1], expand.shape[1]]
+
+    def call(pieces, held, start):
+        *held, own, other = pieces_call(
+            expand_body, pieces, [], [expand, project], sizes, held, start, total, "branch_forward"
+        )
+        return (held, (own, other))
+
+    result, held, _ = branch_over(normed.astype(BF16), number, call, beside)
+    return (result, (norm_kept, *held))
+
+
+def branch_backward(gain, expand, project, kept, grad_branch, number, beside=None):
+    norm_kept, normed, inner, active = kept
+    total = 4 * grad_branch.shape[0]
+    sizes = [grad_branch.shape[1], expand.shape[1]]
+
+    def call(pieces, held, start):
+        *held, own, other = pieces_call(
+            expand_back_body, pieces, [inner], [expand, project], sizes, held, start, total,
+            "branch_backward",
+        )
+        return (held, (own, other))
+
+    result, (grads, grad_inner), sent = branch_over(grad_branch.astype(BF16), number, call, beside)
+
+    held = (grads, active, normed, grad_inner, sent)
+    grad_resid, grad_gain = norm_backward(norm_kept, gain, result)
+    return (grad_resid, grad_gain, held, result)
 
 
 def attend_kernel(live_ref, query_ref, keys_ref, values_ref, mixed_ref, total_ref):
@@ -632,7 +748,7 @@
 def attend_forward_call(qkv, live_column):
     length = qkv.shape[0]
     heads = qkv.shape[1] // (3 * HEAD_DIM)
-    block = length // 2
+    block = length
 
     def whole(kind):
         return pl.BlockSpec((length, HEAD_DIM), lambda h, b: (0, head_column(h, kind)))
@@ -655,11 +771,7 @@
             jax.ShapeDtypeStruct((heads, 1, length), F32),
         ],
         compiler_params=pltpu.CompilerParams(vmem_limit_bytes=32 << 20),
-        cost_estimate=pl.CostEstimate(
-            flops=4 * heads * length * length * HEAD_DIM,
-            bytes_accessed=8 * length * heads * HEAD_DIM,
-            transcendentals=heads * length * length,
-        ),
+        cost_estimate=early(4 * heads * length * length * HEAD_DIM, 8 * qkv.size),
         name="attend_forward",
     )(live_column, qkv, qkv, qkv)
 
@@ -725,11 +837,7 @@
         out_shape=jax.ShapeDtypeStruct(qkv.shape, BF16),
         scratch_shapes=[pltpu.VMEM((length, HEAD_DIM), F32), pltpu.VMEM((length, HEAD_DIM), F32)],
         compiler_params=pltpu.CompilerParams(vmem_limit_bytes=40 << 20),
-        cost_estimate=pl.CostEstimate(
-            flops=10 * heads * length * length * HEAD_DIM,
-            bytes_accessed=16 * length * heads * HEAD_DIM,
-            transcendentals=heads * length * length,
-        ),
+        cost_estimate=early(10 * heads * length * length * HEAD_DIM, 8 * qkv.size),
         name="attend_backward",
     )(live_column, qkv, qkv, qkv, grad_mixed, log_total)
 
@@ -742,22 +850,129 @@
     return jnp.where((place >= 0) & (place < LEN), moved, 0.0)
 
 
+def weights_kernel(number, *refs):
+    out_ref = refs[-1]
+    start = 0
+    for k in range(number):
+        left_ref, right_ref = refs[2 * k], refs[2 * k + 1]
+        size = right_ref.shape[1]
+        out_ref[:, start : start + size] = weight_term(left_ref[...], right_ref[...]).astype(BF16)
+        start += size
+
+
+def weights_turn_kernel(number, *refs):
+    out_ref = refs[-1]
+    for k in range(number):
+
+        @pl.when(pl.program_id(0) == k)
+        def _(left_ref=refs[2 * k], right_ref=refs[2 * k + 1]):
+            out_ref[...] = weight_term(left_ref[...], right_ref[...]).astype(BF16)
+
+
+def weights_call(lefts, rights, name):
+    rows, width = lefts[0].shape
+    number = len(lefts)
+    total = sum(right.shape[1] for right in rights)
+    block = 512
+    steps = width // block
+    turns = len({right.shape[1] for right in rights}) == 1
+    operands, in_specs = [], []
+    for k in range(number):
+        left_rows, size = rights[k].shape
+        if turns:
+            place = lambda i, j, k=k: (0, jnp.clip((i - k) * steps + j, 0, steps - 1))
+            held = lambda i, j: (0, 0)
+        else:
+            place = lambda j: (0, j)
+            held = lambda j: (0, 0)
+        in_specs.append(pl.BlockSpec((left_rows, block), place))
+        in_specs.append(pl.BlockSpec((left_rows, size), held))
+        operands += [lefts[k], rights[k]]
+    if turns:
+        grid, kernel = (number, steps), weights_turn_kernel
+        out_spec = pl.BlockSpec((block, rights[0].shape[1]), lambda i, j: (j, i))
+    else:
+        grid, kernel = (steps,), weights_kernel
+        out_spec = pl.BlockSpec((block, total), lambda j: (j, 0))
+    return pl.pallas_call(
+        lambda *refs: kernel(number, *refs),
+        grid=grid,
+        in_specs=in_specs,
+        out_specs=out_spec,
+        out_shape=jax.ShapeDtypeStruct((width, total), BF16),
+        compiler_params=pltpu.CompilerParams(vmem_limit_bytes=48 << 20),
+        cost_estimate=early(2 * rows * width * total, 2 * width * total),
+        name=name,
+    )(*operands)
+
+
 def fetch_other(packed):
-    number = lax.axis_size("dp")
-    rows = packed.shape[0] // number
-    piece = lax.dynamic_slice_in_dim(packed, lax.axis_index("dp") * rows, rows)
-    return lax.all_gather(cross(piece), "dp", axis=0, tiled=True)
-
-
-def reduce_weights(grads):
-    sizes = [grad.shape[1] for grad in grads]
-    packed = grads[0] if len(grads) == 1 else jnp.concatenate(grads, axis=1)
-    reduced = lax.psum_scatter(packed, "dp", scatter_dimension=0, tiled=True).astype(F32)
-    results, start = [], 0
-    for size in sizes:
-        results.append(reduced[:, start : start + size])
-        start += size
-    return results
+    place = lax.axis_index("dp")
+    x, z = place % 2, (place // 2) % 2
+    rows = packed.shape[0] // 4
+
+    def over_x(values):
+        return lax.ppermute(values, "dp", X_PAIRS)
+
+    def over_z(values):
+        return lax.ppermute(values, "dp", Z_NEAR_PAIRS)
+
+    def first():
+        return cross(lax.dynamic_slice_in_dim(packed, (2 * z + x) * rows, rows))
+
+    def second(piece):
+        return (over_x(piece), over_z(piece))
+
+    def third(beside, above):
+        return (over_z(beside[: rows // 2]), over_x(above[rows // 2 :]))
+
+    def whole(piece, beside, above, corner):
+        corner = jnp.concatenate(corner, axis=0)
+        pieces = ((x, z, piece), (1 - x, z, beside), (x, 1 - z, above), (1 - x, 1 - z, corner))
+        result = jnp.zeros_like(packed)
+        for at_x, at_z, part in pieces:
+            result = lax.dynamic_update_slice_in_dim(result, part, (2 * at_z + at_x) * rows, 0)
+        return result
+
+    return (first, second, third, whole)
+
+
+def reduce_weights(grad):
+    return lax.psum_scatter(grad, "dp", scatter_dimension=0, tiled=True)
+
+
+def sum_steps(values):
+    for axis, pairs in (
+        ("mp", CORE_PAIRS),
+        ("mp", CHIP_PAIRS),
+        ("dp", X_PAIRS),
+        ("dp", Z_NEAR_PAIRS),
+        ("dp", Z_FAR_PAIRS),
+    ):
+        arrived = lax.ppermute(values, axis, pairs)
+        earlier = yield arrived
+        values = values + after(arrived, *earlier)
+    yield values
+
+
+def reduce_by_steps(grad):
+    place = lax.axis_index("dp")
+    size = grad.shape[0] // 8
+    x, near, far = place % 2, (place // 2) % 2, place // 4
+    steps = (
+        ((4, 2, size, -1), 1, x, X_PAIRS),
+        ((2, 2, size, -1), 1, near, Z_NEAR_PAIRS),
+        ((2, size, -1), 0, far, Z_FAR_PAIRS),
+    )
+    for shape, axis, at, pairs in steps:
+        parts = grad.reshape(shape)
+        keep = lax.dynamic_index_in_dim(parts, at, axis, keepdims=False)
+        send = lax.dynamic_index_in_dim(parts, 1 - at, axis, keepdims=False)
+        arrived = lax.ppermute(send, "dp", pairs)
+        earlier = yield arrived
+        total = keep.astype(F32) + after(arrived, *earlier).astype(F32)
+        grad = total.astype(BF16)
+    yield total
 
 
 def on_device_block(
@@ -800,13 +1015,31 @@
     attend_pack = jnp.concatenate(
         [query_weight, key_weight, value_weight, attend_out.reshape(D, -1)], axis=1
     )
-    mixer_pack = jnp.concatenate([mixer_value, mixer_gate, mixer_out.reshape(D, -1)], axis=1)
+    mixer_pack = jnp.concatenate([mixer_value, mixer_gate], axis=1)
     width = query_weight.shape[1]
-    attend_other = fetch_other(attend_pack)
-    mixer_other = fetch_other(mixer_pack)
+    channels = jnp.concatenate([mixer_depth, batch_scale[None], batch_shift[None]], axis=0)
+    own_live = live[:rows]
+    picker = (masked_rows[:, None] == jnp.arange(rows)[None, :]).astype(BF16)
+    keep = jnp.sum(picker.astype(F32) * own_live[None, :], axis=1)
+    labels = (targets + 1) * (keep > 0).astype(jnp.int32)
+    codes = on_chip(labels[None, :])
+
+    first, second, third, whole = fetch_other(attend_pack)
+    fetched = []
+
+    def fetch_first():
+        fetched.append(first())
+        return fetched
 
     start = frames.astype(F32)
-    branch, first_kept = branch_forward(start, first_gain, first_in, first_out, 2)
+    branch, first_kept = branch_forward(
+        start, first_gain, first_in, first_out, 2, (lambda: [], fetch_first)
+    )
+    piece = fetched[0]
+    beside, above = second(piece)
+    channels_other, codes_other = cross(channels), cross(codes)
+    branch = after(branch, beside, above, channels_other, codes_other)
+    attend_other = whole(piece, beside, above, third(beside, above))
     after_first = start + 0.5 * branch
 
     qkv_weight = jnp.concatenate([attend_pack[:, : 3 * width], attend_other[:, : 3 * width]], axis=1)
@@ -814,23 +1047,26 @@
         [attend_out, attend_other[:, 3 * width :].reshape(width, D)], axis=0
     )
     normed, attend_norm = norm_forward(after_first, attend_gain)
+    mixer_other, mixer_out_other = cross(mixer_pack), cross(mixer_out)
     attend_in = on_chip(normed.astype(BF16))
     qkv = dot(attend_in, qkv_weight, BF16)
-    mixed, log_total = attend_forward_call(qkv, live_column)
+    mixed, log_total = attend_forward_call(after(qkv, mixer_other), live_column)
+    mixed = after(mixed, mixer_out_other)
     after_attend = after_first + on_chip_sum(dot(mixed, attend_out_both, BF16))
 
-    value_both = jnp.concatenate([mixer_value, mixer_other[:, :width]], axis=1)
-    gate_both = jnp.concatenate([mixer_gate, mixer_other[:, width : 2 * width]], axis=1)
-    mixer_out_both = jnp.concatenate(
-        [mixer_out, mixer_other[:, 2 * width :].reshape(width, D)], axis=0
-    )
-    channels = jnp.concatenate([mixer_depth, batch_scale[None], batch_shift[None]], axis=0)
-    channels = jnp.concatenate([channels, cross(channels)], axis=1)
+    mixer_both = jnp.concatenate([mixer_pack, mixer_other], axis=1)
+    mixer_out_both = jnp.concatenate([mixer_out, mixer_out_other], axis=0)
+    channels = jnp.concatenate([channels, channels_other], axis=1)
     depth, scale_both, shift_both = channels[:KERNEL], channels[KERNEL], channels[KERNEL + 1]
     normed, mixer_norm = norm_forward(after_attend, mixer_gain)
     mixer_in = on_chip(normed.astype(BF16))
-    value_in = dot(mixer_in, value_both)
-    gate_in = dot(mixer_in, gate_both)
+    both_in = dot(mixer_in, mixer_both)
+
+    def sides(first, second):
+        return jnp.concatenate([first, second], axis=1)
+
+    value_in = sides(both_in[:, :width], both_in[:, 2 * width : 3 * width])
+    gate_in = sides(both_in[:, width : 2 * width], both_in[:, 3 * width :])
     gate = jax.nn.sigmoid(gate_in)
     glu = value_in * gate * live_column
     half = KERNEL // 2
@@ -856,19 +1092,23 @@
     after_second = after_mixer + 0.5 * branch
     output, final_norm = norm_forward(after_second, final_gain)
 
-    own_live = live[:rows]
-    picker = (masked_rows[:, None] == jnp.arange(rows)[None, :]).astype(BF16)
-    keep = jnp.sum(picker.astype(F32) * own_live[None, :], axis=1)
     chosen = dot(picker, output.astype(BF16), BF16)
-    labels = (targets + 1) * (keep > 0).astype(jnp.int32)
-    codes = on_chip(labels[None, :])
-    codes = jnp.concatenate([cross(codes), codes], axis=0)
+    codes = jnp.concatenate([codes_other, codes], axis=0)
     slots = masked_rows.shape[0]
     vocab = head_weight.shape[1]
-    head_parts = gather_parts(chosen, 1)
-    logits = [dot(part, head_weight) for part in head_parts]
-    top = [jnp.max(part, axis=1) for part in logits]
-    total = [jnp.sum(jnp.exp(part - peak[:, None]), axis=1) for part, peak in zip(logits, top)]
+    near = on_chip(chosen)
+    far = cross(chosen)
+
+    def evaluate(part):
+        logits = dot(part, head_weight)
+        top = jnp.max(logits, axis=1)
+        return (logits, top, jnp.sum(jnp.exp(logits - top[:, None]), axis=1))
+
+    near_values = evaluate(near)
+    far = on_chip(after(far, near_values[2]))
+    far_values = evaluate(far)
+    head_parts = [far, near]
+    logits, top, total = zip(far_values, near_values)
     pair = jnp.stack([jnp.concatenate(top), jnp.concatenate(total)]).reshape(2, 4, slots)
 
     def merge(first, second):
@@ -896,16 +1136,26 @@
     grad_head = dot_rows(jnp.concatenate(head_parts), jnp.concatenate(grad_logits))
     grad_chosen = scatter_parts(head_results).astype(BF16)
     grad_output = out_cotangent.astype(F32) + weight_term(picker, grad_chosen)
-    (grad_head,) = reduce_weights([grad_head])
     grad_second, final_gain_grad = norm_backward(final_norm, final_gain, grad_output)
 
-    back, second_gain_grad, grad_second_in, grad_second_out = branch_backward(
-        second_gain, second_in, second_out, second_kept, 0.5 * grad_second, 2
-    )
+    back, second_gain_grad, second_held, _ = branch_backward(
+        second_gain,
+        second_in,
+        second_out,
+        second_kept,
+        0.5 * grad_second,
+        2,
+        (lambda: [grad_head], lambda: []),
+    )
+    grad_head = reduce_weights(grad_head)
     grad_mixer = grad_second + back
-    grad_second_in, grad_second_out = reduce_weights([grad_second_in, grad_second_out])
 
     grad_full = on_chip(grad_mixer.astype(BF16))
+    grads, active, normed, grad_inner, _ = second_held
+    grad_second_both = weights_call(
+        [after(grads, grad_full), normed], [active, grad_inner], "second_weights"
+    )
+    grad_second_both = reduce_weights(grad_second_both)
     grad_shaped = dot_t(grad_full, mixer_out_both) * swish_slope(shaped)
     sums = sum_channels(
         jnp.stack([jnp.sum(grad_shaped, axis=0), jnp.sum(grad_shaped * normal, axis=0)])
@@ -923,76 +1173,107 @@
     grad_glu = grad_glu * live_column
     grad_value = (grad_glu * gate).astype(BF16)
     grad_gate = (grad_glu * value_in * gate * (1.0 - gate)).astype(BF16)
-    summed = matmul_t(grad_value, value_both) + matmul_t(grad_gate, gate_both)
-    back, mixer_gain_grad = norm_backward(mixer_norm, mixer_gain, on_chip_sum(summed.astype(BF16)))
+    grad_both = jnp.concatenate(
+        [grad_value[:, :width], grad_gate[:, :width], grad_value[:, width:], grad_gate[:, width:]],
+        axis=1,
+    )
+    summed = dot_t(grad_both, mixer_both, BF16)
+    back, mixer_gain_grad = norm_backward(mixer_norm, mixer_gain, on_chip_sum(summed))
     grad_attend = grad_mixer + back
-    mixer_grads = [
-        dot_rows(mixer_in, grad_value),
-        dot_rows(mixer_in, grad_gate),
-        dot_rows(grad_full, mixer_active),
+    mixer_grads = weights_call([mixer_in, grad_full], [grad_both, mixer_active], "mixer_weights")
+    counts = jnp.stack([own_loss, jnp.sum(keep)])
+    counts = jnp.concatenate([counts, jnp.zeros((D - 2,), F32)])[None]
+    depth_full = jnp.zeros((KERNEL, D), F32)
+    for side, at in ((0, own), (1, (own + 2) % 4)):
+        depth_full = lax.dynamic_update_slice_in_dim(
+            depth_full, depth_grad[:, side * width : (side + 1) * width], at * width, 1
+        )
+    gains = jnp.concatenate(
+        [mixer_gain_grad, second_gain_grad, final_gain_grad, counts, depth_full], axis=0
+    )
+    gain_run = sum_steps(gains)
+    next(gain_run)
+    gain_run.send(())
+    gain_crossed = gain_run.send(())
+    mixer_crossed = [
+        cross(after(part, gain_crossed))
+        for part in (mixer_grads[:, 2 * width : 4 * width], mixer_grads[:, 5 * width :])
     ]
-    mixer_grads = [
-        jnp.concatenate([grad[:, :width] for grad in mixer_grads], axis=1),
-        jnp.concatenate([grad[:, width:] for grad in mixer_grads], axis=1),
-    ]
-    mixer_grads = (mixer_grads[0].astype(F32) + cross(mixer_grads[1]).astype(F32)).astype(BF16)
-    depth_grad = sum_channels(depth_grad)
+    gain_run.send(())
+    gain_run.send(())
+    gains = gain_run.send(())
+    loss = gains[3, 0] / gains[3, 1]
+    depth_grad = lax.dynamic_slice_in_dim(gains[4:], own * width, width, 1)
 
     grad_full = on_chip(grad_attend.astype(BF16))
     grad_mixed = dot_t(grad_full, attend_out_both, BF16)
     grad_qkv = attend_backward_call(qkv, live_column, grad_mixed, log_total)
+    mixer_crossed = after(jnp.concatenate(mixer_crossed, axis=1), grad_qkv)
     summed = dot_t(grad_qkv, qkv_weight, BF16)
     back, attend_gain_grad = norm_backward(attend_norm, attend_gain, on_chip_sum(summed))
     grad_first = grad_attend + back
-    qkv_grad = dot_rows(attend_in, grad_qkv)
-    out_grad = dot_rows(grad_full, mixed)
-    attend_grads = [
-        jnp.concatenate([qkv_grad[:, : 3 * width], out_grad[:, :width]], axis=1),
-        jnp.concatenate([qkv_grad[:, 3 * width :], out_grad[:, width:]], axis=1),
-    ]
-    attend_grads = (attend_grads[0].astype(F32) + cross(attend_grads[1]).astype(F32)).astype(BF16)
-    (middle,) = reduce_weights([jnp.concatenate([mixer_grads, attend_grads], axis=1)])
-    grad_mixer_value, grad_mixer_gate, grad_mixer_out, grad_query, grad_key, grad_value, grad_out = (
-        jnp.split(middle, 7, axis=1)
-    )
-
-    back, first_gain_grad, grad_first_in, grad_first_out = branch_backward(
-        first_gain, first_in, first_out, first_kept, 0.5 * grad_first, 2
+    middle = weights_call([attend_in, grad_full], [grad_qkv, mixed], "attend_weights")
+    mixer_sum = sides(mixer_grads[:, : 2 * width], mixer_grads[:, 4 * width : 5 * width])
+    mixer_sum = (mixer_sum.astype(F32) + mixer_crossed.astype(F32)).astype(BF16)
+    middle = reduce_weights(jnp.concatenate([middle, mixer_sum], axis=1))
+
+    back, first_gain_grad, (grads, active, normed, grad_inner, sent), result = branch_backward(
+        first_gain, first_in, first_out, first_kept, after(0.5 * grad_first, gains), 2
     )
     input_grad = grad_first + back
-    grad_first_out, grad_first_in = reduce_weights([grad_first_out, grad_first_in])
-
-    counts = jnp.stack([own_loss, jnp.sum(keep)])
-    counts = jnp.concatenate([counts, jnp.zeros((D - 2,), F32)])[None]
-    gains = jnp.concatenate(
-        [attend_gain_grad, mixer_gain_grad, second_gain_grad, final_gain_grad, counts], axis=0
-    )
-    gains = sum_over_all(gains)
-    first_gain_grad = sum_over_all(first_gain_grad)[0]
-    loss = gains[4, 0] / gains[4, 1]
+    gain_run = sum_steps(jnp.concatenate([attend_gain_grad, first_gain_grad], axis=0))
+    next(gain_run)
+    gain_run.send(())
+    gain_run.send(())
+    grad_out = dot_rows(after(grads, sent), active)
+    run_out = reduce_by_steps(grad_out)
+    next(run_out)
+    grad_in = dot_rows(normed, after(grad_inner, grad_out))
+    run_in = reduce_by_steps(grad_in)
+    next(run_in)
+    grad_head = after(grad_head, grad_in).astype(F32)
+    grad_second_both = after(grad_second_both, grad_in).astype(F32)
+    arrived = run_out.send((grad_in,))
+    arrived = run_in.send((arrived,))
+    gain_run.send((arrived,))
+    run_out.send((arrived,))
+    arrived = run_in.send(())
+    gain_run.send((arrived,))
+    grad_first_out = run_out.send(())
+    grad_first_in = run_in.send(())
+    first_gain_grad = gain_run.send((grad_first_in,))
+    grad_second_out, grad_second_in = jnp.split(grad_second_both, 2, axis=1)
+    middle = after(middle, grad_first_in).astype(F32)
+    crossed = cross(
+        jnp.concatenate([middle[:, 3 * width : 6 * width], middle[:, 7 * width : 8 * width]], axis=1).astype(BF16)
+    )
+    own_part = jnp.concatenate([middle[:, : 3 * width], middle[:, 6 * width : 7 * width]], axis=1)
+    attend_grads = own_part + crossed.astype(F32)
+    grad_query, grad_key, grad_value, grad_out = jnp.split(attend_grads, 4, axis=1)
+    grad_mixer_value, grad_mixer_gate, grad_mixer_out = jnp.split(middle[:, 8 * width :], 3, axis=1)
     return (
         output,
         loss,
         input_grad,
-        first_gain_grad,
+        first_gain_grad[1],
         grad_first_in,
         grad_first_out.T,
-        gains[0],
+        first_gain_grad[0],
         grad_query,
         grad_key,
         grad_value,
         grad_out.T,
-        gains[1],
+        gains[0],
         grad_mixer_value,
         grad_mixer_gate,
-        depth_grad[:, :width],
+        depth_grad,
         batch_scale_grad[:width],
         batch_shift_grad[:width],
         grad_mixer_out.T,
-        gains[2],
+        gains[1],
         grad_second_in,
         grad_second_out.T,
-        gains[3],
+        gains[2],
         grad_head,
     )
 

time: 792 us -> 704 us (0.89)
  Pallas kernels: 29.1 us -> 125 us
  matrix products: 151 us -> 56.6 us
  waiting for transfers between devices: 333 us -> 262 us
  other arithmetic: 98 us -> 87.5 us
  local copies, waits for them, and re-layouts: 82.1 us -> 72.2 us
    pallas_call x0 -> x15, Pallas kernels: none -> 97.4 us  [the longest x12 68.6 us: pieces_call(): pl.pallas_call(kernel, grid=(steps,), in_specs=in_specs, out_specs=[place...]
    ppermute x0 -> x20, waiting for transfers between devices: none -> 84.4 us  [the longest x6 60.8 us: reduce_by_steps(): arrived = lax.ppermute(send, 'dp', pairs)]
    ppermute x30 -> x29, waiting for transfers between devices: 221 us -> 146 us  [cross(): return lax.ppermute(values, 'mp', CHIP_PAIRS)]
    dot_general x20 -> x7, matrix products: 62.1 us -> 18 us  [dot(): return jnp.dot(left, right, preferred_element_type=F32).astype(kind)]
    unnamed x8 -> x3, waiting for transfers between devices: 42.2 us -> 0.05 us
    all_gather x2 -> x0, waiting for transfers between devices: 36.4 us -> none  [fetch_other(): return lax.all_gather(cross(piece), 'dp', axis=0, tiled=True)]
    dot_general x19 -> x6, matrix products: 42.5 us -> 15.7 us  [matmul_t(): lax.dot_general(left, right, (((1,), (1,)), ((), ())), preferred_element_...]
    dot_general x11 -> x4, matrix products: 46.3 us -> 22.9 us  [weight_term(): lax.dot_general(left, right, (((0,), (0,)), ((), ())), preferred_element_...]
  transfers between devices with their start and end apart: 91 -> 112, of which waited for: 40 -> 66; matrix products, arithmetic and copies ran while one was open for 32% -> 21% of each run, Pallas kernels for 2% -> 18%
where the time goes in v2:
time: 704 us; the launch traced here: 692 us
  waiting for transfers between devices  262 us (37%)
  Pallas kernels  125 us (18%)
  other arithmetic  87.5 us (12%)
  local copies, waits for them, and re-layouts  72.2 us (10%)
  starting transfers between devices  68.3 us (10%)
  matrix products  56.6 us (8%)
  between operations  21.1 us (3%)
    ppermute x29, waiting for transfers between devices, cross(): return lax.ppermute(values, 'mp', CHIP_PAIRS)  146 us
    pallas_call x12, Pallas kernels, pieces_call(): pl.pallas_call(kernel, grid=(steps,), in_specs=in_specs, out_specs=[place...  68.6 us
    ppermute x6, waiting for transfers between devices, reduce_by_steps(): arrived = lax.ppermute(send, 'dp', pairs)  60.8 us
    unnamed x277, local copies, waits for them, and re-layouts  35.3 us
    pallas_call x3, Pallas kernels, weights_call(): pl.pallas_call(lambda *refs: kernel(number, *refs), grid=grid, in_specs=i...  28.8 us
    ppermute x29, starting transfers between devices, cross(): return lax.ppermute(values, 'mp', CHIP_PAIRS)  27.5 us
    dot_general x4, matrix products, weight_term(): lax.dot_general(left, right, (((0,), (0,)), ((), ())), preferred_element_...  22.9 us
    ppermute x54, waiting for transfers between devices, swap(): return lax.ppermute(values, 'mp', CORE_PAIRS)  22.8 us
  transfers between devices with their start and end apart: 112, of which 66 were waited for; matrix products, arithmetic and copies ran while one was open for 21% of the time, Pallas kernels for 18%

profile of v2, /device:TPU:0, one launch (start us, length us, event | category | flops | bytes accessed | tf_op | source)
XLA Modules:
  0.0 692.2 jit_solution(2372229283011030408)
XLA Ops:
  18.7 8.0 %branch_forward.6 = (bf16[2048,1024]{1,0:T(8,128)(2,1)}, bf16[2048,1024]{1,0:T(8,128)(2,1)}, bf16[2048,1024]{1,0:T(8,128)(2,1)}, bf16[512,1024]{1,0:T(8,128)(2,1)S(1)}, bf16[512,1024]{1,0:T(8,128)(2,1)}) custom-call(bf16[512,1024]{1,0:T(8,128)(2,1)S(1)} %fusion.15.refs_0_, bf16[512,1024]{1,0:T(8,128)(2,1)} %collective-permute-done.refs_1_, ...), custom_call_target="tpu_custom_call" | custom-call | flops 4294967 | bytes 4194 | tf_op jit(solution)/shard_map/branch_forward/pallas_call | solution.py:642
  37.2 7.2 %collective-permute-done.9 = bf16[256,1024]{1,0:T(8,128)(2,1)S(1)} collective-permute-done((bf16[256,1024]{1,0:T(8,128)(2,1)S(1)}, bf16[256,1024]{1,0:T(8,128)(2,1)S(1)}, u32[]{:S(2)}, u32[]{:S(2)}) %collective-permute-start.9) | collective-permute-done | bytes 524320 | tf_op jit(solution)/shard_map/ppermute | solution.py:516
  44.4 10.4 %collective-permute-done.8.refs_0_ = bf16[256,1024]{1,0:T(8,128)(2,1)S(1)} collective-permute-done((bf16[256,1024]{1,0:T(8,128)(2,1)S(1)}, bf16[256,1024]{1,0:T(8,128)(2,1)S(1)}, u32[]{:S(2)}, u32[]{:S(2)}) %collective-permute-start.8) | collective-permute-done | bytes 524320 | tf_op jit(solution)/shard_map/ppermute | solution.py:516
  118.1 10.5 %collective-permute-done.23 = bf16[1024,512]{1,0:T(8,128)(2,1)} collective-permute-done((bf16[1024,512]{1,0:T(8,128)(2,1)}, bf16[1024,512]{1,0:T(8,128)(2,1)}, u32[]{:S(2)}, u32[]{:S(2)}) %collective-permute-start.23) | collective-permute-done | bytes 1048608 | tf_op jit(solution)/shard_map/ppermute | solution.py:516
  128.5 8.8 %attend_forward.1 = (bf16[1024,512]{1,0:T(8,128)(2,1)S(1)}, f32[4,1,1024]{2,1,0:T(1,128)S(1)}) custom-call(f32[1024,1]{1,0:T(8,128)S(1)} %fusion.72.live_ref, bf16[1024,1536]{1,0:T(8,128)(2,1)S(1)} %convolution_convert_fusion.query_ref.keys_ref.values_ref, bf16[1024,1536]{1,0:T(8,128)(2,1)S(1)} %convolution_convert_fusion.query_ref.keys_ref.values_ref, ...), custom_call_target="tpu_custom_call" | custom-call | flops 2147483 | bytes 12582 | tf_op jit(solution)/shard_map/attend_forward/pallas_call | solution.py:756
  203.3 8.0 %collective-permute-done.40.refs_0_ = bf16[256,1024]{1,0:T(8,128)(2,1)S(1)} collective-permute-done((bf16[256,1024]{1,0:T(8,128)(2,1)S(1)}, bf16[256,1024]{1,0:T(8,128)(2,1)S(1)}, u32[]{:S(2)}, u32[]{:S(2)}) %collective-permute-start.40) | collective-permute-done | bytes 524320 | tf_op jit(solution)/shard_map/ppermute | solution.py:516
  219.6 6.9 %collective-permute-done.39 = bf16[256,1024]{1,0:T(8,128)(2,1)S(1)} collective-permute-done((bf16[256,1024]{1,0:T(8,128)(2,1)S(1)}, bf16[256,1024]{1,0:T(8,128)(2,1)S(1)}, u32[]{:S(2)}, u32[]{:S(2)}) %collective-permute-start.39) | collective-permute-done | bytes 524320 | tf_op jit(solution)/shard_map/ppermute | solution.py:516
  227.1 13.0 %collective-permute-done.45 = bf16[256,1024]{1,0:T(8,128)(2,1)S(1)} collective-permute-done((bf16[256,1024]{1,0:T(8,128)(2,1)S(1)}, bf16[256,1024]{1,0:T(8,128)(2,1)S(1)}, u32[]{:S(2)}, u32[]{:S(2)}) %collective-permute-start.45) | collective-permute-done | bytes 524320 | tf_op jit(solution)/shard_map/ppermute | solution.py:516
  249.9 7.0 %collective-permute-done.47 = bf16[256,1024]{1,0:T(8,128)(2,1)S(1)} collective-permute-done((bf16[256,1024]{1,0:T(8,128)(2,1)S(1)}, bf16[256,1024]{1,0:T(8,128)(2,1)S(1)}, u32[]{:S(2)}, u32[]{:S(2)}) %collective-permute-start.47) | collective-permute-done | bytes 524320 | tf_op jit(solution)/shard_map/ppermute | solution.py:516
  292.8 7.4 %collective-permute-done.53 = bf16[256,1024]{1,0:T(8,128)(2,1)} collective-permute-done((bf16[256,1024]{1,0:T(8,128)(2,1)}, bf16[256,1024]{1,0:T(8,128)(2,1)}, u32[]{:S(2)}, u32[]{:S(2)}) %collective-permute-start.53) | collective-permute-done | bytes 524320 | tf_op jit(solution)/shard_map/ppermute | solution.py:516
  307.3 8.4 %branch_backward.6 = (bf16[2048,1024]{1,0:T(8,128)(2,1)}, bf16[2048,1024]{1,0:T(8,128)(2,1)}, bf16[512,1024]{1,0:T(8,128)(2,1)S(1)}, bf16[512,1024]{1,0:T(8,128)(2,1)S(1)}) custom-call(bf16[512,1024]{1,0:T(8,128)(2,1)S(1)} %get-tuple-element.313.refs_0_, bf16[512,1024]{1,0:T(8,128)(2,1)S(1)} %collective-permute-done.54.refs_1_, ...), custom_call_target="tpu_custom_call" | custom-call | flops 4294967 | bytes 4194 | tf_op jit(solution)/shard_map/branch_backward/pallas_call | solution.py:642
  326.9 6.8 collective-permute-done.62.refs_0_
  349.6 12.9 %collective-permute-done.67 = bf16[256,1024]{1,0:T(8,128)(2,1)S(1)} collective-permute-done((bf16[256,1024]{1,0:T(8,128)(2,1)S(1)}, bf16[256,1024]{1,0:T(8,128)(2,1)S(1)}, u32[]{:S(2)}, u32[]{:S(2)}) %collective-permute-start.67) | collective-permute-done | bytes 524320 | tf_op jit(solution)/shard_map/ppermute | solution.py:516
  387.4 14.6 %second_weights.1 = bf16[1024,2048]{1,0:T(8,128)(2,1)S(1)} custom-call(bf16[2048,1024]{1,0:T(8,128)(2,1)} %get-tuple-element.193.refs_0_, bf16[2048,1024]{1,0:T(8,128)(2,1)} %get-tuple-element.194.refs_1_, bf16[2048,1024]{1,0:T(8,128)(2,1)} %get-tuple-element.195.refs_2_, bf16[2048,1024]{1,0:T(8,128)(2,1)} %get-tuple-element.196.refs_3_), custom_call_target="tpu_custom_call" | custom-call | flops 8589934 | bytes 4194 | tf_op jit(solution)/shard_map/second_weights/pallas_call | solution.py:897
  405.5 7.1 %multiply_reduce_fusion.4 = (f32[512]{0:T(512)S(1)}, f32[512]{0:T(512)S(1)}, f32[512]{0:T(512)S(1)}, f32[512]{0:T(512)S(1)}, f32[512]{0:T(512)S(1)}, /*index=5*/f32[1024,512]{1,0:T(8,128)S(1)}) fusion(f32[2,512]{1,0:T(2,128)S(1)} %get-tuple-element.344, f32[1022,512]{1,0:T(8,128)} %copy-done.38, pred[1024]{0:T(1024)(128)(4,1)S(1)} %get-tuple-element.446, ...), kind=kLoop, calls=%fused_computation.88 | loop fusion | flops 13628928 | bytes 16807936 | tf_op jit(solution)/shard_map/reduce_sum | solution.py:1170
  465.5 18.5 %attend_backward.1.refs_1_ = bf16[1024,1536]{1,0:T(8,128)(2,1)S(1)} custom-call(f32[1024,1]{1,0:T(8,128)S(1)} %copy-done.13, bf16[1024,1536]{1,0:T(8,128)(2,1)S(1)} %copy-done.1, bf16[1024,1536]{1,0:T(8,128)(2,1)S(1)} %copy-done.1, bf16[1024,1536]{1,0:T(8,128)(2,1)S(1)} %copy-done.1, bf16[1024,512]{1,0:T(8,128)(2,1)S(1)} %convolution_convert_fusion.7.grad_ref, ...), custom_call_target="tpu_custom_call" | custom-call | flops 5368709 | bytes 12582 | tf_op jit(solution)/shard_map/attend_backward/pallas_call | solution.py:825
  490.7 8.1 %attend_weights.1 = bf16[1024,2048]{1,0:T(8,128)(2,1)} custom-call(bf16[1024,1024]{1,0:T(8,128)(2,1)S(1)} %pad_maximum_fusion.2.refs_0_, bf16[1024,1536]{1,0:T(8,128)(2,1)} %copy-done.11, bf16[1024,1024]{1,0:T(8,128)(2,1)S(1)} %pad_maximum_fusion.7.refs_2_, bf16[1024,512]{1,0:T(8,128)(2,1)S(1)} %copy-done.17), custom_call_target="tpu_custom_call" | custom-call | flops 4294967 | bytes 4194 | tf_op jit(solution)/shard_map/attend_weights/pallas_call | solution.py:897
  513.4 8.3 %branch_backward.9 = (bf16[2048,1024]{1,0:T(8,128)(2,1)}, bf16[2048,1024]{1,0:T(8,128)(2,1)}, bf16[512,1024]{1,0:T(8,128)(2,1)S(1)}, bf16[512,1024]{1,0:T(8,128)(2,1)}) custom-call(bf16[512,1024]{1,0:T(8,128)(2,1)S(1)} %get-tuple-element.161.refs_0_, bf16[512,1024]{1,0:T(8,128)(2,1)S(1)} %collective-permute-done.81.refs_1_, ...), custom_call_target="tpu_custom_call" | custom-call | flops 4294967 | bytes 4194 | tf_op jit(solution)/shard_map/branch_backward/pallas_call | solution.py:642
  552.9 9.7 %collective-permute-done.88 = bf16[256,1024]{1,0:T(8,128)(2,1)S(1)} collective-permute-done((bf16[256,1024]{1,0:T(8,128)(2,1)S(1)}, bf16[256,1024]{1,0:T(8,128)(2,1)S(1)}, u32[]{:S(2)}, u32[]{:S(2)}) %collective-permute-start.88) | collective-permute-done | bytes 524320 | tf_op jit(solution)/shard_map/ppermute | solution.py:516
  563.4 7.2 %convolution_convert_fusion.2 = bf16[1024,1024]{1,0:T(8,128)(2,1)S(1)} fusion(bf16[2048,1024]{1,0:T(8,128)(2,1)} %get-tuple-element.179, bf16[2048,1024]{1,0:T(8,128)(2,1)S(1)} %copy-done.41), kind=kOutput, calls=%fused_computation.132 | convolution fusion | flops 4296015872 | bytes 10485760 | tf_op jit(solution)/shard_map/dot_general | solution.py:66
  584.7 22.6 %collective-permute-done.99 = bf16[4,128,1024]{2,1,0:T(8,128)(2,1)} collective-permute-done((bf16[4,128,1024]{2,1,0:T(8,128)(2,1)}, bf16[4,128,1024]{2,1,0:T(8,128)(2,1)}, u32[]{:S(2)}, u32[]{:S(2)}) %collective-permute-start.99) | collective-permute-done | bytes 1048608 | tf_op jit(solution)/shard_map/ppermute | solution.py:971
  611.7 16.2 %collective-permute-done.98 = bf16[4,128,1024]{2,1,0:T(8,128)(2,1)S(1)} collective-permute-done((bf16[4,128,1024]{2,1,0:T(8,128)(2,1)S(1)}, bf16[4,128,1024]{2,1,0:T(8,128)(2,1)S(1)}, u32[]{:S(2)}, u32[]{:S(2)}) %collective-permute-start.98) | collective-permute-done | bytes 1048608 | tf_op jit(solution)/shard_map/ppermute | solution.py:971
  633.1 8.3 %collective-permute-done.101 = bf16[2,128,1024]{2,1,0:T(8,128)(2,1)S(1)} collective-permute-done((bf16[2,128,1024]{2,1,0:T(8,128)(2,1)S(1)}, bf16[2,128,1024]{2,1,0:T(8,128)(2,1)S(1)}, u32[]{:S(2)}, u32[]{:S(2)}) %collective-permute-start.101) | collective-permute-done | bytes 524320 | tf_op jit(solution)/shard_map/ppermute | solution.py:971
  652.6 8.1 %collective-permute-done.103 = bf16[128,1024]{1,0:T(8,128)(2,1)S(1)} collective-permute-done((bf16[128,1024]{1,0:T(8,128)(2,1)S(1)}, bf16[128,1024]{1,0:T(8,128)(2,1)S(1)}, u32[]{:S(2)}, u32[]{:S(2)}) %collective-permute-start.103) | collective-permute-done | bytes 262176 | tf_op jit(solution)/shard_map/ppermute | solution.py:971
  (759 shorter events, 427.0 us)
Async XLA Ops:
  7.2 572.3 %reduce-scatter.8.cloned.1.call-start = ((), (), s32[]{:S(2)}) async-start(), calls=%async_computation.5 | async-start | bytes 4718592 | tf_op jit(solution)/shard_map/reduce_scatter | solution.py:941
  12.4 15.4 %collective-permute-start.2 = (bf16[256,1024]{1,0:T(8,128)(2,1)}, bf16[256,1024]{1,0:T(8,128)(2,1)}, u32[]{:S(2)}, u32[]{:S(2)}) collective-permute-start(bf16[256,1024]{1,0:T(8,128)(2,1)} %get-tuple-element.361), channel_id=1, source_target_pairs={{0,2},{2,0},{1,3},{3,1},{4,6},{6,4},{5,7},{7,5},{8,10},{10,8},{9,1... | collective-permute-start | bytes 1572872 | tf_op jit(solution)/shard_map/ppermute | solution.py:516
  31.4 23.4 %collective-permute-start.8 = (bf16[256,1024]{1,0:T(8,128)(2,1)S(1)}, bf16[256,1024]{1,0:T(8,128)(2,1)S(1)}, u32[]{:S(2)}, u32[]{:S(2)}) collective-permute-start(bf16[256,1024]{1,0:T(8,128)(2,1)S(1)} %copy-done.94), channel_id=1, source_target_pairs={{0,2},{2,0},{1,3},{3,1},{4,6},{6,4},{5,7},{7,5},{8,10},{10,8},{9,1... | collective-permute-start | bytes 1572872 | tf_op jit(solution)/shard_map/ppermute | solution.py:516
  36.6 18.8 %collective-permute-start.5 = (bf16[128,1024]{1,0:T(8,128)(2,1)S(1)}, bf16[128,1024]{1,0:T(8,128)(2,1)S(1)}, u32[]{:S(2)}, u32[]{:S(2)}) collective-permute-start(bf16[128,1024]{1,0:T(8,128)(2,1)S(1)} %get-tuple-element.394), channel_id=1, source_target_pairs={{0,1},{1,0},{2,3},{3,2},{4,5},{5,4},{6,7},{7,6},{8,9},{9,8},{10,11... | collective-permute-start | bytes 786440 | tf_op jit(solution)/shard_map/ppermute | solution.py:512
  36.7 18.7 %collective-permute-start.6 = (bf16[128,1024]{1,0:T(8,128)(2,1)S(1)}, bf16[128,1024]{1,0:T(8,128)(2,1)S(1)}, u32[]{:S(2)}, u32[]{:S(2)}) collective-permute-start(bf16[128,1024]{1,0:T(8,128)(2,1)S(1)} %get-tuple-element.395), channel_id=1, source_target_pairs={{0,1},{1,0},{2,3},{3,2},{4,5},{5,4},{6,7},{7,6},{8,9},{9,8},{10,11... | collective-permute-start | bytes 786440 | tf_op jit(solution)/shard_map/ppermute | solution.py:512
  91.4 20.8 %collective-permute-start.20 = (bf16[512,1024]{1,0:T(8,128)(2,1)}, bf16[512,1024]{1,0:T(8,128)(2,1)}, u32[]{:S(2)}, u32[]{:S(2)}) collective-permute-start(bf16[512,1024]{1,0:T(8,128)(2,1)} %multiply_convert_fusion.8), channel_id=1, source_target_pairs={{0,1},{1,0},{2,3},{3,2},{4,5},{5,4},{6,7},{7,6},{8,9},{9,8},{10,11... | collective-permute-start | bytes 3145736 | tf_op jit(solution)/shard_map/ppermute | solution.py:512
  91.4 46.0 %collective-permute-start.24 = (bf16[256,1024]{1,0:T(8,128)(2,1)}, bf16[256,1024]{1,0:T(8,128)(2,1)}, u32[]{:S(2)}, u32[]{:S(2)}) collective-permute-start(bf16[256,1024]{1,0:T(8,128)(2,1)} %param.45), channel_id=1, source_target_pairs={{0,2},{2,0},{1,3},{3,1},{4,6},{6,4},{5,7},{7,5},{8,10},{10,8},{9,1... | collective-permute-start | bytes 1572872 | tf_op jit(solution)/shard_map/ppermute | solution.py:516
  93.0 35.5 %collective-permute-start.23 = (bf16[1024,512]{1,0:T(8,128)(2,1)}, bf16[1024,512]{1,0:T(8,128)(2,1)}, u32[]{:S(2)}, u32[]{:S(2)}) collective-permute-start(bf16[1024,512]{1,0:T(8,128)(2,1)} %pad_maximum_fusion.9), channel_id=1, source_target_pairs={{0,2},{2,0},{1,3},{3,1},{4,6},{6,4},{5,7},{7,5},{8,10},{10,8},{9,1... | collective-permute-start | bytes 3145736 | tf_op jit(solution)/shard_map/ppermute | solution.py:516
  211.9 15.1 %collective-permute-start.33 = (bf16[512,1024]{1,0:T(8,128)(2,1)S(1)}, bf16[512,1024]{1,0:T(8,128)(2,1)S(1)}, u32[]{:S(2)}, u32[]{:S(2)}) collective-permute-start(bf16[512,1024]{1,0:T(8,128)(2,1)S(1)} %get-tuple-element.131), channel_id=1, source_target_pairs={{0,1},{1,0},{2,3},{3,2},{4,5},{5,4},{6,7},{7,6},{8,9},{9,8},{10,11... | collective-permute-start | bytes 3145736 | tf_op jit(solution)/shard_map/ppermute | solution.py:512
  292.7 376.3 %reduce-scatter.6.cloned.1.call-start = ((), (), s32[]{:S(2)}) async-start(), calls=%async_computation.4 | async-start | bytes 4718592 | tf_op jit(solution)/shard_map/reduce_scatter | solution.py:941
  334.3 15.3 %collective-permute-start.55 = (bf16[512,1024]{1,0:T(8,128)(2,1)S(1)}, bf16[512,1024]{1,0:T(8,128)(2,1)S(1)}, u32[]{:S(2)}, u32[]{:S(2)}) collective-permute-start(bf16[512,1024]{1,0:T(8,128)(2,1)S(1)} %get-tuple-element.148), channel_id=1, source_target_pairs={{0,1},{1,0},{2,3},{3,2},{4,5},{5,4},{6,7},{7,6},{8,9},{9,8},{10,11... | collective-permute-start | bytes 3145736 | tf_op jit(solution)/shard_map/ppermute | solution.py:512
  383.2 20.8 %collective-permute-start.72 = (f32[2,512]{1,0:T(2,128)S(1)}, f32[2,512]{1,0:T(2,128)S(1)}, u32[]{:S(2)}, u32[]{:S(2)}) collective-permute-start(f32[2,512]{1,0:T(2,128)S(1)} %add.583), channel_id=1, source_target_pairs={{0,16},{16,0},{4,20},{20,4},{8,24},{24,8},{12,28},{28,12},{1,17},{... | collective-permute-start | bytes 12296 | tf_op jit(solution)/shard_map/ppermute | solution.py:521
  403.9 269.0 %reduce-scatter.4.cloned.1.call-start = ((), (), s32[]{:S(2)}) async-start(), calls=%async_computation.3 | async-start | bytes 6488064 | tf_op jit(solution)/shard_map/reduce_scatter | solution.py:941
  438.5 25.0 %collective-permute-start.79 = (bf16[512,1024]{1,0:T(8,128)(2,1)S(1)}, bf16[512,1024]{1,0:T(8,128)(2,1)S(1)}, u32[]{:S(2)}, u32[]{:S(2)}) collective-permute-start(bf16[512,1024]{1,0:T(8,128)(2,1)S(1)} %get-tuple-element.300), channel_id=1, source_target_pairs={{0,1},{1,0},{2,3},{3,2},{4,5},{5,4},{6,7},{7,6},{8,9},{9,8},{10,11... | collective-permute-start | bytes 3145736 | tf_op jit(solution)/shard_map/ppermute | solution.py:512
  459.1 39.7 %collective-permute-start.107 = (bf16[1024,256]{1,0:T(8,128)(2,1)S(1)}, bf16[1024,256]{1,0:T(8,128)(2,1)S(1)}, u32[]{:S(2)}, u32[]{:S(2)}) collective-permute-start(bf16[1024,256]{1,0:T(8,128)(2,1)S(1)} %get-tuple-element.189), channel_id=1, source_target_pairs={{0,2},{2,0},{1,3},{3,1},{4,6},{6,4},{5,7},{7,5},{8,10},{10,8},{9,1... | collective-permute-start | bytes 1572872 | tf_op jit(solution)/shard_map/ppermute | solution.py:516
  459.8 39.1 %collective-permute-start.106 = (bf16[1024,512]{1,0:T(8,128)(2,1)S(1)}, bf16[1024,512]{1,0:T(8,128)(2,1)S(1)}, u32[]{:S(2)}, u32[]{:S(2)}) collective-permute-start(bf16[1024,512]{1,0:T(8,128)(2,1)S(1)} %get-tuple-element.188), channel_id=1, source_target_pairs={{0,2},{2,0},{1,3},{3,1},{4,6},{6,4},{5,7},{7,5},{8,10},{10,8},{9,1... | collective-permute-start | bytes 3145736 | tf_op jit(solution)/shard_map/ppermute | solution.py:516
  512.1 26.8 %collective-permute-start.89 = (bf16[256,1024]{1,0:T(8,128)(2,1)}, bf16[256,1024]{1,0:T(8,128)(2,1)}, u32[]{:S(2)}, u32[]{:S(2)}) collective-permute-start(bf16[256,1024]{1,0:T(8,128)(2,1)} %get-tuple-element.352), channel_id=1, source_target_pairs={{0,2},{2,0},{1,3},{3,1},{4,6},{6,4},{5,7},{7,5},{8,10},{10,8},{9,1... | collective-permute-start | bytes 1572872 | tf_op jit(solution)/shard_map/ppermute | solution.py:516
  551.9 57.4 %collective-permute-start.82 = (bf16[512,1024]{1,0:T(8,128)(2,1)}, bf16[512,1024]{1,0:T(8,128)(2,1)S(1)}, u32[]{:S(2)}, u32[]{:S(2)}) collective-permute-start(bf16[512,1024]{1,0:T(8,128)(2,1)} %get-tuple-element.164), channel_id=1, source_target_pairs={{0,1},{1,0},{2,3},{3,2},{4,5},{5,4},{6,7},{7,6},{8,9},{9,8},{10,11... | collective-permute-start | bytes 3145736 | tf_op jit(solution)/shard_map/ppermute | solution.py:512
  562.6 46.6 %collective-permute-start.94 = (bf16[256,1024]{1,0:T(8,128)(2,1)}, bf16[256,1024]{1,0:T(8,128)(2,1)S(1)}, u32[]{:S(2)}, u32[]{:S(2)}) collective-permute-start(bf16[256,1024]{1,0:T(8,128)(2,1)} %add_convert_fusion.1), channel_id=1, source_target_pairs={{0,2},{2,0},{1,3},{3,1},{4,6},{6,4},{5,7},{7,5},{8,10},{10,8},{9,1... | collective-permute-start | bytes 1572872 | tf_op jit(solution)/shard_map/ppermute | solution.py:516
  573.1 34.1 %collective-permute-start.99 = (bf16[4,128,1024]{2,1,0:T(8,128)(2,1)}, bf16[4,128,1024]{2,1,0:T(8,128)(2,1)}, u32[]{:S(2)}, u32[]{:S(2)}) collective-permute-start(bf16[4,128,1024]{2,1,0:T(8,128)(2,1)} %dynamic-slice_bitcast_fusion), channel_id=1, source_target_pairs={{0,4},{4,0},{8,12},{12,8},{16,20},{20,16},{24,28},{28,24},{1,5},{5... | collective-permute-start | bytes 3145736 | tf_op jit(solution)/shard_map/ppermute | solution.py:971
  583.2 44.7 %collective-permute-start.98 = (bf16[4,128,1024]{2,1,0:T(8,128)(2,1)S(1)}, bf16[4,128,1024]{2,1,0:T(8,128)(2,1)S(1)}, u32[]{:S(2)}, u32[]{:S(2)}) collective-permute-start(bf16[4,128,1024]{2,1,0:T(8,128)(2,1)S(1)} %dynamic-slice_bitcast_fusion.1), channel_id=1, source_target_pairs={{0,4},{4,0},{8,12},{12,8},{16,20},{20,16},{24,28},{28,24},{1,5},{5... | collective-permute-start | bytes 3145736 | tf_op jit(solution)/shard_map/ppermute | solution.py:971
  609.0 18.9 %collective-permute-start.100 = (bf16[2,128,1024]{2,1,0:T(8,128)(2,1)S(1)}, bf16[2,128,1024]{2,1,0:T(8,128)(2,1)S(1)}, u32[]{:S(2)}, u32[]{:S(2)}) collective-permute-start(bf16[2,128,1024]{2,1,0:T(8,128)(2,1)S(1)} %dynamic-slice_bitcast_fusion.3), channel_id=1, source_target_pairs={{0,8},{8,0},{4,12},{12,4},{16,24},{24,16},{20,28},{28,20},{1,9},{9... | collective-permute-start | bytes 1572872 | tf_op jit(solution)/shard_map/ppermute | solution.py:971
  641.9 18.9 %collective-permute-start.103 = (bf16[128,1024]{1,0:T(8,128)(2,1)S(1)}, bf16[128,1024]{1,0:T(8,128)(2,1)S(1)}, u32[]{:S(2)}, u32[]{:S(2)}) collective-permute-start(bf16[128,1024]{1,0:T(8,128)(2,1)S(1)} %dynamic-slice_bitcast_fusion.5), channel_id=1, source_target_pairs={{0,16},{16,0},{4,20},{20,4},{8,24},{24,8},{12,28},{28,12},{1,17},{... | collective-permute-start | bytes 786440 | tf_op jit(solution)/shard_map/ppermute | solution.py:971
  643.4 23.1 %collective-permute-start.105 = (bf16[128,1024]{1,0:T(8,128)(2,1)S(1)}, bf16[128,1024]{1,0:T(8,128)(2,1)S(1)}, u32[]{:S(2)}, u32[]{:S(2)}) collective-permute-start(bf16[128,1024]{1,0:T(8,128)(2,1)S(1)} %dynamic-slice_bitcast_fusion.4), channel_id=1, source_target_pairs={{0,16},{16,0},{4,20},{20,4},{8,24},{24,8},{12,28},{28,12},{1,17},{... | collective-permute-start | bytes 786440 | tf_op jit(solution)/shard_map/ppermute | solution.py:971
  (221 other events, 1546.1 us)
Sparse Core Ops, SparseCore 0:
  292.8 88.5 reduce-scatter.7
  404.1 87.1 reduce-scatter.5
  504.3 119.0 reduce-scatter.3

commit v3 on v2

--- a/solution.py
+++ b/solution.py
@@ -528,49 +528,157 @@
     return sum_over_dp(values)
 
 
-def sum_channels(values):
+def sum_channels(values, *earlier):
     other = cross(values)
     half = values.shape[-1] // 2
     turned = jnp.concatenate([other[..., half:], other[..., :half]], axis=-1)
-    return sum_over_dp(values + turned)
-
-
-def norm_forward(values, gain):
+    return sum_over_dp(after(values + turned, *earlier))
+
+
+def clamped(block, width, first, last):
+    return pl.BlockSpec((block, width), lambda i: (jnp.clip(i, first, last) - first, 0))
+
+
+def part_specs(parts, block):
+    rows, width = parts[0].shape
+    specs, at = [], 0
+    for part in parts:
+        if part.shape[0] == rows:
+            specs.append(clamped(block, width, 0, rows // block - 1))
+            continue
+        steps = part.shape[0] // block
+        specs.append(clamped(block, width, at, at + steps - 1))
+        at += steps
+    return specs
+
+
+def part_total(refs, parts, block):
+    rows = parts[0].shape[0]
+    total, at = None, 0
+    for ref, part in zip(refs, parts):
+        value = ref[...].astype(F32)
+        if part.shape[0] != rows:
+            steps = part.shape[0] // block
+            step = pl.program_id(0)
+            value = jnp.where((step >= at) & (step < at + steps), value, 0.0)
+            at += steps
+        total = value if total is None else total + value
+    return total
+
+
+NORM_BLOCK = 256
+
+
+def center_of(values):
     center = values - jnp.mean(values, axis=-1, keepdims=True)
-    spread = jnp.mean(center * center, axis=-1, keepdims=True)
-    inverse = lax.rsqrt(spread + NORM_EPSILON)
-    unit = center * inverse
-    return (unit * gain, (unit, inverse))
-
-
-def norm_backward(kept, gain, grad):
-    unit, inverse = kept
-    grad_gain = jnp.sum(grad * unit, axis=0, keepdims=True)
-    scaled = grad * gain
-    inner = jnp.mean(scaled * unit, axis=-1, keepdims=True)
-    return (inverse * (scaled - jnp.mean(scaled, axis=-1, keepdims=True) - unit * inner), grad_gain)
+    inverse = lax.rsqrt(jnp.mean(center * center, axis=-1, keepdims=True) + NORM_EPSILON)
+    return (center * inverse, inverse)
+
+
+def streamed(array):
+    return pltpu.with_memory_space_constraint(array, pltpu.HBM)
+
+
+def norm_forward(base, parts, gain, scale, exact=False):
+    rows, width = base.shape
+    block = NORM_BLOCK
+    row = pl.BlockSpec((block, width), lambda i: (i, 0))
+    number = len(parts)
+
+    def kernel(base_ref, *refs):
+        parts_refs, gain_ref, outs = refs[:number], refs[number], list(refs[number + 1 :])
+        values = base_ref[...].astype(F32)
+        if parts:
+            values = values + scale * part_total(parts_refs, parts, block)
+            outs.pop(0)[...] = values
+        normed = center_of(values)[0] * gain_ref[...]
+        outs.pop(0)[...] = normed.astype(BF16)
+        if exact:
+            outs.pop(0)[...] = normed
+
+    kinds = ([F32] if parts else []) + [BF16] + ([F32] if exact else [])
+    results = pl.pallas_call(
+        kernel,
+        grid=(rows // block,),
+        in_specs=[row]
+        + (part_specs(parts, block) if parts else [])
+        + [pl.BlockSpec((1, width), lambda i: (0, 0))],
+        out_specs=[row] * len(kinds),
+        out_shape=[
+            jax.ShapeDtypeStruct((rows, width), kind) if kind == BF16 else pltpu.HBM((rows, width), kind)
+            for kind in kinds
+        ],
+        compiler_params=pltpu.CompilerParams(vmem_limit_bytes=24 << 20),
+        cost_estimate=cost(10 * base.size, 8 * base.size),
+        name="norm_forward",
+    )(streamed(base), *parts, gain[None])
+    return results if parts else [base, *results]
+
+
+def norm_backward(values, gain, parts, grad, scale, pick=None):
+    rows, width = values.shape
+    block = NORM_BLOCK
+    row = pl.BlockSpec((block, width), lambda i: (i, 0))
+    number = len(parts)
+    optional = list(pick) if pick is not None else []
+    optional_specs = []
+    if pick is not None:
+        slots = pick[0].shape[1]
+        optional_specs = [
+            pl.BlockSpec((block, slots), lambda i: (i, 0)),
+            pl.BlockSpec((slots, width), lambda i: (0, 0)),
+        ]
+    if grad is not None:
+        optional.append(streamed(grad))
+        optional_specs.append(row)
+
+    def kernel(values_ref, gain_ref, *refs):
+        parts_refs, refs = refs[:number], list(refs[number:])
+        total = part_total(parts_refs, parts, block)
+        if pick is not None:
+            total = total + matmul(refs.pop(0)[...], refs.pop(0)[...])
+        unit, inverse = center_of(values_ref[...].astype(F32))
+        scaled = total * gain_ref[...]
+        inner = jnp.mean(scaled * unit, axis=-1, keepdims=True)
+        result = inverse * (scaled - jnp.mean(scaled, axis=-1, keepdims=True) - unit * inner)
+        if grad is not None:
+            result = result + refs.pop(0)[...]
+        grad_ref, low_ref, gain_grad_ref = refs
+        grad_ref[...] = result
+        low_ref[...] = (scale * result).astype(BF16)
+        gain_grad = jnp.sum(total * unit, axis=0, keepdims=True)
+
+        @pl.when(pl.program_id(0) == 0)
+        def _():
+            gain_grad_ref[...] = gain_grad
+
+        @pl.when(pl.program_id(0) > 0)
+        def _():
+            gain_grad_ref[...] += gain_grad
+
+    one = pl.BlockSpec((1, width), lambda i: (0, 0))
+    return pl.pallas_call(
+        kernel,
+        grid=(rows // block,),
+        in_specs=[row, one] + part_specs(parts, block) + optional_specs,
+        out_specs=[row, row, one],
+        out_shape=[
+            pltpu.HBM((rows, width), F32),
+            jax.ShapeDtypeStruct((rows, width), BF16),
+            jax.ShapeDtypeStruct((1, width), F32),
+        ],
+        compiler_params=pltpu.CompilerParams(vmem_limit_bytes=24 << 20),
+        cost_estimate=cost(20 * values.size, 12 * values.size),
+        name="norm_backward",
+    )(streamed(values), gain[None], *parts, *optional)
 
 
 def on_chip(values):
     return jnp.concatenate([values, swap(values)], axis=0)
 
 
-def on_chip_sum(values):
-    half = values.shape[0] // 2
-    return values[:half].astype(F32) + swap(values[half:]).astype(F32)
-
-
-def gather_parts(values, number):
-    step = values.shape[0] // number
-    far = [cross(values[k * step : (k + 1) * step]) for k in range(number)]
-    near = on_chip(values)
-    return [on_chip(part) for part in far] + [near]
-
-
-def scatter_parts(parts):
-    far = [cross(on_chip_sum(part).astype(BF16)) for part in parts[:-1]]
-    far = far[0] if len(far) == 1 else jnp.concatenate(far, axis=0)
-    return on_chip_sum(parts[-1]) + far.astype(F32)
+def on_chip_sum(own, other):
+    return own.astype(F32) + swap(other).astype(F32)
 
 
 def dot(left, right, kind=F32):
@@ -592,6 +700,10 @@
 
 def early(flops, size):
     return pl.CostEstimate(flops=flops // 1000, bytes_accessed=size // 1000, transcendentals=0)
+
+
+def cost(flops, size):
+    return pl.CostEstimate(flops=flops, bytes_accessed=size, transcendentals=0)
 
 
 BLOCK = 256
@@ -679,27 +791,33 @@
     return jnp.concatenate([swap(values[:half]), swap(values[half:])], axis=0)
 
 
-def branch_over(values, number, call, beside=None):
+def branch_over(values, number, call, beside=None, last=None):
     rows = values.shape[0]
     step = rows // number
     far = [cross(values[k * step : (k + 1) * step]) for k in range(number)]
     held, (own, other) = call((values, swap(values)), None, 0)
-    near = own.astype(F32) + swap(other).astype(F32)
+    near = [own, swap(other)]
     done, back = own, []
     for k in range(number):
-        part = after(far[k], done) if beside is None else after(far[k], done, *beside[k]())
-        held, (own, other) = call((part, swap_halves(part)), held, 2 * rows + 2 * step * k)
+        part = after(far[k], done)
+        other = swap_halves(part)
+        if beside is not None:
+            other = after(other, *beside[k](done))
+        held, (own, other) = call((part, other), held, 2 * rows + 2 * step * k)
         result = (own.astype(F32) + swap_halves(other).astype(F32)).astype(BF16)
         result = after(result, *back)
         back.append(cross(result))
         done = own
-    return (near + jnp.concatenate(back, axis=0).astype(F32), held, result)
-
-
-def branch_forward(resid, gain, expand, project, number, beside=None):
-    normed, norm_kept = norm_forward(resid, gain)
-    total = 4 * resid.shape[0]
-    sizes = [resid.shape[1], expand.shape[1], expand.shape[1]]
+    extra = None
+    if last is not None:
+        extra = last(held, result)
+        back[-1] = after(back[-1], extra[0])
+    return (near + back, held, extra)
+
+
+def branch_forward(normed, expand, project, number, beside=None):
+    total = 4 * normed.shape[0]
+    sizes = [normed.shape[1], expand.shape[1], expand.shape[1]]
 
     def call(pieces, held, start):
         *held, own, other = pieces_call(
@@ -707,12 +825,12 @@
         )
         return (held, (own, other))
 
-    result, held, _ = branch_over(normed.astype(BF16), number, call, beside)
-    return (result, (norm_kept, *held))
-
-
-def branch_backward(gain, expand, project, kept, grad_branch, number, beside=None):
-    norm_kept, normed, inner, active = kept
+    parts, held, _ = branch_over(normed, number, call, beside)
+    return (parts, held)
+
+
+def branch_backward(expand, project, kept, grad_branch, number, beside, last):
+    normed, inner, active = kept
     total = 4 * grad_branch.shape[0]
     sizes = [grad_branch.shape[1], expand.shape[1]]
 
@@ -723,11 +841,12 @@
         )
         return (held, (own, other))
 
-    result, (grads, grad_inner), sent = branch_over(grad_branch.astype(BF16), number, call, beside)
-
-    held = (grads, active, normed, grad_inner, sent)
-    grad_resid, grad_gain = norm_backward(norm_kept, gain, result)
-    return (grad_resid, grad_gain, held, result)
+    def weights(held, sent):
+        grads, grad_inner = held
+        return last(after(grads, sent), active, normed, grad_inner)
+
+    parts, held, extra = branch_over(grad_branch, number, call, beside, weights)
+    return (parts, (*held, active, normed), extra)
 
 
 def attend_kernel(live_ref, query_ref, keys_ref, values_ref, mixed_ref, total_ref):
@@ -771,7 +890,7 @@
             jax.ShapeDtypeStruct((heads, 1, length), F32),
         ],
         compiler_params=pltpu.CompilerParams(vmem_limit_bytes=32 << 20),
-        cost_estimate=early(4 * heads * length * length * HEAD_DIM, 8 * qkv.size),
+        cost_estimate=cost(4 * heads * length * length * HEAD_DIM, 8 * qkv.size),
         name="attend_forward",
     )(live_column, qkv, qkv, qkv)
 
@@ -837,17 +956,437 @@
         out_shape=jax.ShapeDtypeStruct(qkv.shape, BF16),
         scratch_shapes=[pltpu.VMEM((length, HEAD_DIM), F32), pltpu.VMEM((length, HEAD_DIM), F32)],
         compiler_params=pltpu.CompilerParams(vmem_limit_bytes=40 << 20),
-        cost_estimate=early(10 * heads * length * length * HEAD_DIM, 8 * qkv.size),
+        cost_estimate=cost(10 * heads * length * length * HEAD_DIM, 8 * qkv.size),
         name="attend_backward",
     )(live_column, qkv, qkv, qkv, grad_mixed, log_total)
 
 
-def shifted(values, offset, position):
-    if offset == 0:
-        return values
-    moved = jnp.roll(values, -offset, axis=0)
-    place = position + offset
-    return jnp.where((place >= 0) & (place < LEN), moved, 0.0)
+def rows_call(
+    body, name, pieces, row_inputs, weights, row_outputs, result, sums=None, scalars=None, turned=True
+):
+    rows = 2 * pieces[0].shape[0] if pieces is not None else row_inputs[0].shape[0]
+    block = BLOCK
+    half = rows // 2 // block
+    steps = 2 * half
+    number, stay = len(row_inputs), len(weights)
+
+    def kernel(scalar_ref, *refs):
+        refs = list(refs)
+        step = pl.program_id(0)
+        piece = None
+        if pieces is not None:
+            piece = jnp.where(step < half, refs[0][...], refs[1][...])
+            refs = refs[2:]
+        inputs, refs = refs[:number], refs[number:]
+        held, refs = refs[:stay], refs[stay:]
+        outputs, refs = refs[: len(row_outputs)], refs[len(row_outputs) :]
+        sums_ref = refs[-1] if sums is not None else None
+        if sums is not None:
+
+            @pl.when(step == 0)
+            def _():
+                sums_ref[...] = jnp.zeros_like(sums_ref)
+
+        value = body(scalar_ref, piece, inputs, held, outputs, sums_ref)
+        if result is not None:
+
+            @pl.when(step < half)
+            def _():
+                refs[0][...] = value
+
+            @pl.when(step >= half)
+            def _():
+                refs[1][...] = value
+
+    def row(width):
+        if turned:
+            return pl.BlockSpec((block, width), lambda i, at: ((i + at[0] * half) % steps, 0))
+        return pl.BlockSpec((block, width), lambda i, at: (i, 0))
+
+    def two(width):
+        return [
+            pl.BlockSpec((block, width), lambda i, at: (jnp.minimum(i, half - 1), 0)),
+            pl.BlockSpec((block, width), lambda i, at: (jnp.maximum(i, half) - half, 0)),
+        ]
+
+    def kept(shape):
+        return pl.BlockSpec(shape, lambda i, at: (0,) * len(shape))
+
+    in_specs, operands = [], [scalars]
+    if pieces is not None:
+        in_specs += two(pieces[0].shape[1])
+        operands += pieces
+    in_specs += [row(array.shape[1]) for array in row_inputs] + [kept(w.shape) for w in weights]
+    operands += [*row_inputs, *(streamed(w) if w.shape[0] >= BLOCK else w for w in weights)]
+    out_specs = [row(width) for width, _ in row_outputs]
+    out_shape = [
+        pltpu.HBM((rows, width), BF16) if kind is None else jax.ShapeDtypeStruct((rows, width), kind)
+        for width, kind in row_outputs
+    ]
+    if result is not None:
+        out_specs += two(result)
+        out_shape += [jax.ShapeDtypeStruct((rows // 2, result), BF16)] * 2
+    if sums is not None:
+        out_specs.append(kept(sums))
+        out_shape.append(jax.ShapeDtypeStruct(sums, F32))
+    return pl.pallas_call(
+        kernel,
+        grid_spec=pltpu.PrefetchScalarGridSpec(
+            num_scalar_prefetch=1, grid=(steps,), in_specs=in_specs, out_specs=out_specs
+        ),
+        out_shape=out_shape,
+        compiler_params=pltpu.CompilerParams(vmem_limit_bytes=28 << 20),
+        cost_estimate=cost(2 * rows * sum(w.size for w in weights), 2 * sum(w.size for w in weights)),
+        name=name,
+    )(*operands)
+
+
+def quarter(scalar_ref, k):
+    rows = D // 4
+    at = scalar_ref[1] ^ k
+    return pl.ds(pl.multiple_of(at * rows, rows), rows)
+
+
+def qkv_body(scalar_ref, piece, inputs, held, outputs, sums_ref):
+    out_ref, held_ref = outputs
+    width = held[0].shape[1]
+    held_ref[...] = piece
+    for k in range(3):
+        out_ref[:, k * width : (k + 1) * width] = matmul(piece, held[k][...]).astype(BF16)
+    total = None
+    for k in range(4):
+        part = matmul(held_ref[:, quarter(scalar_ref, k)], held[3 + k][...])
+        total = part if total is None else total + part
+    out_ref[:, 3 * width :] = total.astype(BF16)
+
+
+def qkv_back_body(scalar_ref, piece, inputs, held, outputs, sums_ref):
+    width = held[0].shape[1]
+    grad_ref = inputs[0]
+    own = None
+    for k in range(3):
+        part = matmul_t(grad_ref[:, k * width : (k + 1) * width], held[k][...])
+        own = part if own is None else own + part
+    far = [matmul_t(grad_ref[:, 3 * width :], held[3 + k][...]) for k in range(4)]
+    at = scalar_ref[1]
+    near = [jnp.where(at % 2 == 0, far[k], far[k ^ 1]) for k in range(4)]
+    placed = [jnp.where(at // 2 == 0, near[k], near[k ^ 2]) for k in range(4)]
+    return (own + jnp.concatenate(placed, axis=1)).astype(BF16)
+
+
+def out_body(scalar_ref, piece, inputs, held, outputs, sums_ref):
+    width = held[0].shape[0]
+    values = inputs[0][...]
+    total = matmul(values[:, :width], held[0][...]) + matmul(values[:, width:], held[1][...])
+    return total.astype(BF16)
+
+
+def out_back_body(scalar_ref, piece, inputs, held, outputs, sums_ref):
+    width = held[0].shape[0]
+    outputs[0][:, :width] = matmul_t(piece, held[0][...]).astype(BF16)
+    outputs[0][:, width:] = matmul_t(piece, held[1][...]).astype(BF16)
+    outputs[1][...] = piece
+
+
+def shape_body(scalar_ref, piece, inputs, held, outputs, sums_ref):
+    stats_ref, *weights = held
+    stats = stats_ref[...]
+    normal = (inputs[0][...] - stats[0:1]) * stats[1:2]
+    shaped = normal * stats[2:3] + stats[3:4]
+    active = swish(shaped).astype(BF16)
+    outputs[0][...] = active
+    width = weights[0].shape[0]
+    total = matmul(active[:, :width], weights[0][...]) + matmul(active[:, width:], weights[1][...])
+    return total.astype(BF16)
+
+
+def shape_back_body(scalar_ref, piece, inputs, held, outputs, sums_ref):
+    stats_ref, *weights = held
+    stats = stats_ref[...]
+    width = weights[0].shape[0]
+    outputs[1][...] = piece
+    for side in range(2):
+        columns = slice(side * width, (side + 1) * width)
+        normal = (inputs[0][:, columns] - stats[0:1, columns]) * stats[1:2, columns]
+        shaped = normal * stats[2:3, columns] + stats[3:4, columns]
+        grad = matmul_t(piece, weights[side][...]) * swish_slope(shaped)
+        outputs[0][:, columns] = grad
+        sums_ref[0:1, columns] += jnp.sum(grad, axis=0, keepdims=True)
+        sums_ref[1:2, columns] += jnp.sum(grad * normal, axis=0, keepdims=True)
+
+
+EDGE = 8
+
+
+def set_padded(padded_ref, values):
+    rows = values.shape[0]
+    zeros = jnp.zeros((EDGE, values.shape[1]), F32)
+    padded_ref[:EDGE] = zeros
+    padded_ref[EDGE + rows :] = zeros
+    padded_ref[EDGE : EDGE + rows] = values
+
+
+def moved(padded_ref, offset):
+    rows = padded_ref.shape[0] - 2 * EDGE
+    return padded_ref[EDGE + offset : EDGE + offset + rows]
+
+
+def live_rows(scalar_ref, rows):
+    return (lax.broadcasted_iota(jnp.int32, (rows, 1), 0) < scalar_ref[1]).astype(F32)
+
+
+def mixer_front_kernel(
+    scalar_ref, own_ref, other_ref, value_ref, gate_ref, value_far_ref, gate_far_ref, depth_ref,
+    held_ref, value_out, gate_out, conv_out, sums_ref, padded_ref,
+):
+    side = pl.program_id(0)
+    half = own_ref.shape[0]
+    rows = 2 * half
+    core = scalar_ref[0]
+    value_weight = jnp.where(side == 0, value_ref[...], value_far_ref[...])
+    gate_weight = jnp.where(side == 0, gate_ref[...], gate_far_ref[...])
+    for at, ref in ((core, own_ref), (1 - core, other_ref)):
+        piece = ref[...]
+        place = pl.ds(pl.multiple_of(at * half, half), half)
+        value_out[place] = matmul(piece, value_weight)
+        gate_out[place] = jax.nn.sigmoid(matmul(piece, gate_weight))
+        held_ref[place] = piece
+    live = live_rows(scalar_ref, rows)
+    set_padded(padded_ref, value_out[...] * gate_out[...] * live)
+    middle = KERNEL // 2
+    conv = sum(moved(padded_ref, j - middle) * depth_ref[j : j + 1] for j in range(KERNEL))
+    conv_out[...] = conv
+    weighted = conv * live
+    sums_ref[0:1] = jnp.sum(weighted, axis=0, keepdims=True)
+    sums_ref[1:2] = jnp.sum(weighted * conv, axis=0, keepdims=True)
+    sums_ref[2:3] = jnp.broadcast_to(jnp.sum(live, axis=0, keepdims=True), (1, weighted.shape[1]))
+
+
+def mixer_front_call(scalars, own, other, weights, depth):
+    half, width = own.shape
+    rows, channels = 2 * half, weights[0].shape[1]
+
+    def kept(shape):
+        return pl.BlockSpec(shape, lambda i: (0,) * len(shape))
+
+    def side(height):
+        return pl.BlockSpec((height, channels), lambda i: (0, i))
+
+    return pl.pallas_call(
+        mixer_front_kernel,
+        grid=(2,),
+        in_specs=[pl.BlockSpec(memory_space=pltpu.SMEM), kept(own.shape), kept(other.shape)]
+        + [kept(w.shape) for w in weights]
+        + [side(depth.shape[0])],
+        out_specs=[kept((rows, width)), side(rows), side(rows), side(rows), side(3)],
+        out_shape=[pltpu.HBM((rows, width), BF16)]
+        + [pltpu.HBM((rows, 2 * channels), F32)] * 2
+        + [jax.ShapeDtypeStruct((rows, 2 * channels), F32)]
+        + [jax.ShapeDtypeStruct((3, 2 * channels), F32)],
+        scratch_shapes=[pltpu.VMEM((rows + 2 * EDGE, channels), F32)],
+        compiler_params=pltpu.CompilerParams(vmem_limit_bytes=36 << 20),
+        cost_estimate=cost(8 * rows * width * channels, 8 * width * channels),
+        name="mixer_front",
+    )(scalars, own, other, *map(streamed, weights), depth)
+
+
+def mixer_back_kernel(
+    scalar_ref, grad_ref, conv_ref, value_in, gate_in, stats_ref, sums_ref, depth_ref,
+    value_ref, gate_ref, value_far_ref, gate_far_ref,
+    both_ref, depth_out, own_ref, other_ref, total_ref, padded_ref, padded_glu_ref,
+):
+    side = pl.program_id(0)
+    rows, channels = grad_ref.shape
+    core = scalar_ref[0]
+    live = live_rows(scalar_ref, rows)
+    stats, sums = stats_ref[...], sums_ref[...]
+    normal = (conv_ref[...] - stats[0:1]) * stats[1:2]
+    share = live * stats[4:5, 0:1]
+    grad_conv = stats[2:3] * stats[1:2] * (grad_ref[...] - share * (sums[0:1] + normal * sums[1:2]))
+    set_padded(padded_ref, grad_conv)
+    set_padded(padded_glu_ref, value_in[...] * gate_in[...] * live)
+    middle = KERNEL // 2
+    for j in range(KERNEL):
+        term = padded_ref[EDGE : EDGE + rows] * moved(padded_glu_ref, j - middle)
+        depth_out[j : j + 1] = jnp.sum(term, axis=0, keepdims=True)
+    grad_glu = sum(moved(padded_ref, middle - j) * depth_ref[j : j + 1] for j in range(KERNEL))
+    grad_glu = grad_glu * live
+    value, gate = value_in[...], gate_in[...]
+    grad_value = (grad_glu * gate).astype(BF16)
+    grad_gate = (grad_glu * value * gate * (1.0 - gate)).astype(BF16)
+    both_ref[:, :channels] = grad_value
+    both_ref[:, channels:] = grad_gate
+    value_weight = jnp.where(side == 0, value_ref[...], value_far_ref[...])
+    gate_weight = jnp.where(side == 0, gate_ref[...], gate_far_ref[...])
+    total = matmul_t(grad_value, value_weight) + matmul_t(grad_gate, gate_weight)
+
+    @pl.when(side == 0)
+    def _():
+        total_ref[...] = total
+
+    @pl.when(side == 1)
+    def _():
+        total_ref[...] += total
+        half = rows // 2
+        for at, ref in ((core, own_ref), (1 - core, other_ref)):
+            ref[...] = total_ref[pl.ds(pl.multiple_of(at * half, half), half)].astype(BF16)
+
+
+def mixer_back_call(scalars, grad, conv, value, gate, stats, sums, depth, weights):
+    rows, both = grad.shape
+    width, channels = weights[0].shape
+
+    def kept(shape):
+        return pl.BlockSpec(shape, lambda i: (0,) * len(shape))
+
+    def side(height, size=channels):
+        return pl.BlockSpec((height, size), lambda i: (0, i))
+
+    return pl.pallas_call(
+        mixer_back_kernel,
+        grid=(2,),
+        in_specs=[pl.BlockSpec(memory_space=pltpu.SMEM)]
+        + [side(rows)] * 4
+        + [side(stats.shape[0]), side(sums.shape[0]), side(depth.shape[0])]
+        + [kept(w.shape) for w in weights],
+        out_specs=[side(rows, 2 * channels), side(KERNEL)] + [kept((rows // 2, width))] * 2,
+        out_shape=[
+            jax.ShapeDtypeStruct((rows, 2 * both), BF16),
+            jax.ShapeDtypeStruct((KERNEL, both), F32),
+        ]
+        + [jax.ShapeDtypeStruct((rows // 2, width), BF16)] * 2,
+        scratch_shapes=[pltpu.VMEM((rows, width), F32)]
+        + [pltpu.VMEM((rows + 2 * EDGE, channels), F32)] * 2,
+        compiler_params=pltpu.CompilerParams(vmem_limit_bytes=40 << 20),
+        cost_estimate=cost(8 * rows * width * channels, 8 * width * channels),
+        name="mixer_back",
+    )(scalars, *map(streamed, (grad, conv, value, gate)), stats, sums, depth, *map(streamed, weights))
+
+
+def row_of(column):
+    return jnp.broadcast_to(column, (column.shape[0], 128)).T[:1]
+
+
+def column_of(row):
+    return jnp.broadcast_to(row, (128, row.shape[1])).T[:, :1]
+
+
+def head_kernel(first_ref, second_ref, weight_ref, logits_ref, stats_ref):
+    step = pl.program_id(0)
+    piece = jnp.where(step == 0, first_ref[...], second_ref[...])
+    logits = matmul(piece, weight_ref[...])
+    logits_ref[...] = logits
+    top = jnp.max(logits, axis=1, keepdims=True)
+    stats_ref[0:1] = row_of(top)
+    stats_ref[1:2] = row_of(jnp.sum(jnp.exp(logits - top), axis=1, keepdims=True))
+
+
+def head_call(pieces, weight):
+    rows, width = pieces[0].shape
+    vocab = weight.shape[1]
+    piece = pl.BlockSpec((rows, width), lambda i: (0, 0))
+    return pl.pallas_call(
+        head_kernel,
+        grid=(2,),
+        in_specs=[piece, piece, pl.BlockSpec(weight.shape, lambda i: (0, 0))],
+        out_specs=[
+            pl.BlockSpec((rows, vocab), lambda i: (i, 0)),
+            pl.BlockSpec((2, rows), lambda i: (0, i)),
+        ],
+        out_shape=[
+            pltpu.HBM((2 * rows, vocab), F32),
+            jax.ShapeDtypeStruct((2, 2 * rows), F32),
+        ],
+        compiler_params=pltpu.CompilerParams(vmem_limit_bytes=28 << 20),
+        cost_estimate=cost(4 * rows * weight.size, 2 * weight.size),
+        name="head",
+    )(*pieces, weight)
+
+
+def merged(first, second):
+    top = jnp.maximum(first[0:1], second[0:1])
+    total = first[1:2] * jnp.exp(first[0:1] - top) + second[1:2] * jnp.exp(second[0:1] - top)
+    return (top, total)
+
+
+def merge_kernel(own_ref, other_ref, out_ref):
+    quarter = own_ref.shape[1] // 4
+    other = other_ref[...]
+    parts = [other[:, k * quarter : (k + 1) * quarter] for k in (1, 0, 3, 2)]
+    top, total = merged(own_ref[...], jnp.concatenate(parts, axis=1))
+    out_ref[0:1] = top
+    out_ref[1:2] = total
+
+
+def merge_call(own, other):
+    return pl.pallas_call(
+        merge_kernel, out_shape=jax.ShapeDtypeStruct(own.shape, F32), name="head_merge"
+    )(own, other)
+
+
+def head_back_kernel(
+    logits_ref, own_ref, far_ref, codes_ref, weight_ref, grad_ref, first_ref, second_ref, loss_ref
+):
+    step = pl.program_id(0)
+    top, total = merged(own_ref[...], far_ref[...])
+    log_total = top + jnp.log(total)
+    codes = codes_ref[...]
+    logits = logits_ref[...]
+    place = lax.broadcasted_iota(jnp.int32, logits.shape, 1)
+    target = column_of(codes[0:1])
+    hits = place == target.astype(jnp.int32)
+    shares = jnp.exp(logits - column_of(log_total))
+    grad = (column_of(codes[1:2]) * (shares - hits.astype(F32))).astype(BF16)
+    grad_ref[...] = grad
+    result = matmul_t(grad, weight_ref[...]).astype(BF16)
+    picked = jnp.sum(jnp.where(hits, logits, 0.0), axis=1, keepdims=True)
+    loss = jnp.sum(codes[2:3] * log_total, keepdims=True)
+    loss = loss - jnp.sum(column_of(codes[1:2]) * picked, keepdims=True)
+    loss = jnp.broadcast_to(loss, loss_ref.shape)
+
+    @pl.when(step == 0)
+    def _():
+        first_ref[...] = result
+        loss_ref[...] = loss
+
+    @pl.when(step == 1)
+    def _():
+        second_ref[...] = result
+        loss_ref[...] += loss
+
+
+def head_back_call(logits, own, far, codes, weight):
+    slots, vocab = logits.shape
+    rows = slots // 2
+    width = weight.shape[0]
+    piece = pl.BlockSpec((rows, width), lambda i: (0, 0))
+    stat = pl.BlockSpec((2, rows), lambda i: (0, i))
+    return pl.pallas_call(
+        head_back_kernel,
+        grid=(2,),
+        in_specs=[
+            pl.BlockSpec((rows, vocab), lambda i: (i, 0)),
+            stat,
+            stat,
+            pl.BlockSpec((3, rows), lambda i: (0, i)),
+            pl.BlockSpec(weight.shape, lambda i: (0, 0)),
+        ],
+        out_specs=[
+            pl.BlockSpec((rows, vocab), lambda i: (i, 0)),
+            piece,
+            piece,
+            pl.BlockSpec((1, 128), lambda i: (0, 0)),
+        ],
+        out_shape=[
+            jax.ShapeDtypeStruct((slots, vocab), BF16),
+            jax.ShapeDtypeStruct((rows, width), BF16),
+            jax.ShapeDtypeStruct((rows, width), BF16),
+            jax.ShapeDtypeStruct((1, 128), F32),
+        ],
+        compiler_params=pltpu.CompilerParams(vmem_limit_bytes=32 << 20),
+        cost_estimate=cost(2 * slots * weight.size, 2 * weight.size),
+        name="head_back",
+    )(streamed(logits), own, far, codes, weight)
 
 
 def weights_kernel(number, *refs):
@@ -869,7 +1408,33 @@
             out_ref[...] = weight_term(left_ref[...], right_ref[...]).astype(BF16)
 
 
-def weights_call(lefts, rights, name):
+def head_weights_kernel(*refs):
+    lefts, rights, out_ref = refs[:4], refs[4:6], refs[6]
+    total = None
+    for k in range(2):
+        left = jnp.concatenate([lefts[2 * k][...], lefts[2 * k + 1][...]], axis=0)
+        part = weight_term(left, rights[k][...])
+        total = part if total is None else total + part
+    out_ref[...] = total.astype(BF16)
+
+
+def head_weights_call(lefts, rights, total):
+    width, size = lefts[0].shape[1], rights[0].shape[1]
+    block = 256
+    return pl.pallas_call(
+        head_weights_kernel,
+        grid=(width // block,),
+        in_specs=[pl.BlockSpec((left.shape[0], block), lambda j: (0, j)) for left in lefts]
+        + [pl.BlockSpec(right.shape, lambda j: (0, 0)) for right in rights],
+        out_specs=pl.BlockSpec((block, size), lambda j: (j, 0)),
+        out_shape=pltpu.HBM((width, total), BF16),
+        compiler_params=pltpu.CompilerParams(vmem_limit_bytes=32 << 20),
+        cost_estimate=cost(4 * rights[0].size * width, 2 * width * size),
+        name="head_weights",
+    )(*lefts, *rights)
+
+
+def weights_call(lefts, rights, name, held=None):
     rows, width = lefts[0].shape
     number = len(lefts)
     total = sum(right.shape[1] for right in rights)
@@ -881,35 +1446,45 @@
         left_rows, size = rights[k].shape
         if turns:
             place = lambda i, j, k=k: (0, jnp.clip((i - k) * steps + j, 0, steps - 1))
-            held = lambda i, j: (0, 0)
+            whole = lambda i, j: (0, 0)
         else:
             place = lambda j: (0, j)
-            held = lambda j: (0, 0)
+            whole = lambda j: (0, 0)
         in_specs.append(pl.BlockSpec((left_rows, block), place))
-        in_specs.append(pl.BlockSpec((left_rows, size), held))
+        in_specs.append(pl.BlockSpec((left_rows, size), whole))
         operands += [lefts[k], rights[k]]
+    aliases = {}
+    if held is not None:
+        first = (held.shape[1] - total) // rights[0].shape[1]
+        total = held.shape[1]
+        aliases = {len(operands): 0}
+        operands.append(held)
+        in_specs.append(pl.BlockSpec(memory_space=pl.ANY))
+    else:
+        first = 0
     if turns:
         grid, kernel = (number, steps), weights_turn_kernel
-        out_spec = pl.BlockSpec((block, rights[0].shape[1]), lambda i, j: (j, i))
+        out_spec = pl.BlockSpec((block, rights[0].shape[1]), lambda i, j: (j, i + first))
     else:
         grid, kernel = (steps,), weights_kernel
         out_spec = pl.BlockSpec((block, total), lambda j: (j, 0))
     return pl.pallas_call(
-        lambda *refs: kernel(number, *refs),
+        lambda *refs: kernel(number, *refs[: 2 * number], refs[-1]),
         grid=grid,
         in_specs=in_specs,
         out_specs=out_spec,
-        out_shape=jax.ShapeDtypeStruct((width, total), BF16),
-        compiler_params=pltpu.CompilerParams(vmem_limit_bytes=48 << 20),
-        cost_estimate=early(2 * rows * width * total, 2 * width * total),
+        out_shape=pltpu.HBM((width, total), BF16),
+        input_output_aliases=aliases,
+        compiler_params=pltpu.CompilerParams(vmem_limit_bytes=40 << 20),
+        cost_estimate=cost(2 * rows * width * total, 2 * width * total),
         name=name,
     )(*operands)
 
 
 def fetch_other(packed):
-    place = lax.axis_index("dp")
-    x, z = place % 2, (place // 2) % 2
+    place = lax.axis_index("dp") % 4
     rows = packed.shape[0] // 4
+    piece = cross(lax.dynamic_slice_in_dim(packed, place * rows, rows))
 
     def over_x(values):
         return lax.ppermute(values, "dp", X_PAIRS)
@@ -917,24 +1492,11 @@
     def over_z(values):
         return lax.ppermute(values, "dp", Z_NEAR_PAIRS)
 
-    def first():
-        return cross(lax.dynamic_slice_in_dim(packed, (2 * z + x) * rows, rows))
-
-    def second(piece):
-        return (over_x(piece), over_z(piece))
-
-    def third(beside, above):
-        return (over_z(beside[: rows // 2]), over_x(above[rows // 2 :]))
-
-    def whole(piece, beside, above, corner):
-        corner = jnp.concatenate(corner, axis=0)
-        pieces = ((x, z, piece), (1 - x, z, beside), (x, 1 - z, above), (1 - x, 1 - z, corner))
-        result = jnp.zeros_like(packed)
-        for at_x, at_z, part in pieces:
-            result = lax.dynamic_update_slice_in_dim(result, part, (2 * at_z + at_x) * rows, 0)
-        return result
-
-    return (first, second, third, whole)
+    def rest():
+        beside, above = over_x(piece), over_z(piece)
+        return (beside, above, over_z(beside[: rows // 2]), over_x(above[rows // 2 :]))
+
+    return (piece, rest)
 
 
 def reduce_weights(grad):
@@ -1012,10 +1574,8 @@
     live_column = live[:, None]
     place = position[:, None]
 
-    attend_pack = jnp.concatenate(
-        [query_weight, key_weight, value_weight, attend_out.reshape(D, -1)], axis=1
-    )
-    mixer_pack = jnp.concatenate([mixer_value, mixer_gate], axis=1)
+    scalars = jnp.stack([core, length]).astype(jnp.int32)
+    attend_pack = jnp.concatenate([query_weight, key_weight, value_weight], axis=1)
     width = query_weight.shape[1]
     channels = jnp.concatenate([mixer_depth, batch_scale[None], batch_shift[None]], axis=0)
     own_live = live[:rows]
@@ -1024,163 +1584,139 @@
     labels = (targets + 1) * (keep > 0).astype(jnp.int32)
     codes = on_chip(labels[None, :])
 
-    first, second, third, whole = fetch_other(attend_pack)
     fetched = []
 
-    def fetch_first():
-        fetched.append(first())
-        return fetched
-
-    start = frames.astype(F32)
-    branch, first_kept = branch_forward(
-        start, first_gain, first_in, first_out, 2, (lambda: [], fetch_first)
-    )
-    piece = fetched[0]
-    beside, above = second(piece)
-    channels_other, codes_other = cross(channels), cross(codes)
-    branch = after(branch, beside, above, channels_other, codes_other)
-    attend_other = whole(piece, beside, above, third(beside, above))
-    after_first = start + 0.5 * branch
-
-    qkv_weight = jnp.concatenate([attend_pack[:, : 3 * width], attend_other[:, : 3 * width]], axis=1)
-    attend_out_both = jnp.concatenate(
-        [attend_out, attend_other[:, 3 * width :].reshape(width, D)], axis=0
-    )
-    normed, attend_norm = norm_forward(after_first, attend_gain)
-    mixer_other, mixer_out_other = cross(mixer_pack), cross(mixer_out)
-    attend_in = on_chip(normed.astype(BF16))
-    qkv = dot(attend_in, qkv_weight, BF16)
-    mixed, log_total = attend_forward_call(after(qkv, mixer_other), live_column)
-    mixed = after(mixed, mixer_out_other)
-    after_attend = after_first + on_chip_sum(dot(mixed, attend_out_both, BF16))
-
-    mixer_both = jnp.concatenate([mixer_pack, mixer_other], axis=1)
-    mixer_out_both = jnp.concatenate([mixer_out, mixer_out_other], axis=0)
+    def fetch(done):
+        fetched.append(fetch_other(attend_pack))
+        fetched.append((cross(channels), cross(codes)))
+        return [fetched[0][0], *fetched[1]]
+
+    _, normed = norm_forward(frames, [], first_gain, 1.0)
+    parts, first_kept = branch_forward(normed, first_in, first_out, 2, (lambda done: [], fetch))
+    piece, rest = fetched[0]
+    beside, above, *corner = rest()
+    channels_other, codes_other = fetched[1]
+    slots = masked_rows.shape[0]
+    vocab = head_weight.shape[1]
+
+    def slot_codes(codes, first):
+        codes = codes.reshape(1, 2 * slots)
+        counted = (codes > 0).astype(F32)
+        here = counted * (jnp.arange(2 * slots)[None, :] < first).astype(F32)
+        return jnp.concatenate([(codes - 1 - own * vocab).astype(F32), counted, here], axis=0)
+
+    codes_near, codes_far = slot_codes(codes, slots), slot_codes(codes_other, 0)
+    parts[0] = after(parts[0], beside, above, codes_near, codes_far)
+    after_first, normed = norm_forward(frames, parts, attend_gain, 0.5)
+
+    attend_out_other = cross(attend_out)
+    mixer_others = [cross(weight) for weight in (mixer_value, mixer_gate)]
+    mixer_out_other = cross(mixer_out)
+    quarters = [piece, beside, above, jnp.concatenate(corner, axis=0)]
+    place = jnp.stack([core, lax.axis_index("dp") % 4]).astype(jnp.int32)
+    qkv_weights = [query_weight, key_weight, value_weight, *quarters]
+    swapped = swap(normed)
+    swapped = after(swapped, attend_out_other)
+    qkv, attend_in = rows_call(
+        qkv_body, "qkv", (normed, swapped), [], qkv_weights,
+        [(6 * width, BF16), (D, None)], None, scalars=place, turned=False,
+    )
+    mixed, log_total = attend_forward_call(after(qkv, mixer_others[0]), live_column)
+    attend_outs = [attend_out, attend_out_other]
+    own_part, other_part = rows_call(
+        out_body, "attend_out", None, [after(mixed, mixer_others[1])], attend_outs, [], D,
+        scalars=place, turned=False,
+    )
+    parts = [own_part, swap(other_part)]
+    after_attend, normed = norm_forward(after_first, parts, mixer_gain, 1.0)
+
     channels = jnp.concatenate([channels, channels_other], axis=1)
     depth, scale_both, shift_both = channels[:KERNEL], channels[KERNEL], channels[KERNEL + 1]
-    normed, mixer_norm = norm_forward(after_attend, mixer_gain)
-    mixer_in = on_chip(normed.astype(BF16))
-    both_in = dot(mixer_in, mixer_both)
-
-    def sides(first, second):
-        return jnp.concatenate([first, second], axis=1)
-
-    value_in = sides(both_in[:, :width], both_in[:, 2 * width : 3 * width])
-    gate_in = sides(both_in[:, width : 2 * width], both_in[:, 3 * width :])
-    gate = jax.nn.sigmoid(gate_in)
-    glu = value_in * gate * live_column
-    half = KERNEL // 2
-    convolved = sum(shifted(glu, j - half, place) * depth[j] for j in range(KERNEL))
-    weighted = convolved * live_column
-    sums = jnp.stack(
-        [
-            jnp.sum(weighted, axis=0),
-            jnp.sum(weighted * convolved, axis=0),
-            jnp.broadcast_to(jnp.sum(live), (2 * width,)),
-        ]
-    )
-    sums = sum_channels(sums)
+    mixer_weights = [mixer_value, mixer_gate, *mixer_others]
+    mixer_outs = [mixer_out, mixer_out_other]
+    swapped = swap(normed)
+    mixer_in, value_in, gate, convolved, sums = mixer_front_call(
+        scalars, normed, swapped, mixer_weights, depth
+    )
+    sums = sum_channels(sums, mixer_out_other)
     count = sums[2]
     bn_mean = sums[0] / count
     inverse = lax.rsqrt(sums[1] / count - bn_mean * bn_mean + NORM_EPSILON)
-    normal = (convolved - bn_mean) * inverse
-    shaped = normal * scale_both + shift_both
-    mixer_active = swish(shaped).astype(BF16)
-    after_mixer = after_attend + on_chip_sum(dot(mixer_active, mixer_out_both, BF16))
-
-    branch, second_kept = branch_forward(after_mixer, second_gain, second_in, second_out, 2)
-    after_second = after_mixer + 0.5 * branch
-    output, final_norm = norm_forward(after_second, final_gain)
-
-    chosen = dot(picker, output.astype(BF16), BF16)
-    codes = jnp.concatenate([codes_other, codes], axis=0)
-    slots = masked_rows.shape[0]
+    stats = jnp.stack([bn_mean, inverse, scale_both, shift_both, 1.0 / count])
+    mixer_active, own_part, other_part = rows_call(
+        shape_body, "mixer_shape", None, [convolved], [stats, *mixer_outs],
+        [(2 * width, None)], D, scalars=scalars,
+    )
+    parts = [own_part, swap(other_part)]
+    after_mixer, normed = norm_forward(after_attend, parts, second_gain, 1.0)
+
+    parts, second_kept = branch_forward(normed, second_in, second_out, 2)
+    after_second, output_low, output = norm_forward(after_mixer, parts, final_gain, 0.5, True)
+
+    chosen = dot(picker, output_low, BF16)
     vocab = head_weight.shape[1]
-    near = on_chip(chosen)
     far = cross(chosen)
-
-    def evaluate(part):
-        logits = dot(part, head_weight)
-        top = jnp.max(logits, axis=1)
-        return (logits, top, jnp.sum(jnp.exp(logits - top[:, None]), axis=1))
-
-    near_values = evaluate(near)
-    far = on_chip(after(far, near_values[2]))
-    far_values = evaluate(far)
-    head_parts = [far, near]
-    logits, top, total = zip(far_values, near_values)
-    pair = jnp.stack([jnp.concatenate(top), jnp.concatenate(total)]).reshape(2, 4, slots)
-
-    def merge(first, second):
-        peak = jnp.maximum(first[0], second[0])
-        return jnp.stack(
-            [peak, first[1] * jnp.exp(first[0] - peak) + second[1] * jnp.exp(second[0] - peak)]
+    near_pieces = (chosen, swap(chosen))
+    near_logits, near_stats = head_call(near_pieces, head_weight)
+    far = after(far, near_stats)
+    far_pieces = (far, swap(far))
+    far_logits, far_stats = head_call(far_pieces, head_weight)
+    stats_own = jnp.concatenate([near_stats, far_stats], axis=1)
+    stats_own = merge_call(stats_own, swap(stats_own))
+    stats_far = cross(stats_own)
+    near, far = slice(0, 2 * slots), slice(2 * slots, 4 * slots)
+    far_grad, *far_results, far_loss = head_back_call(
+        far_logits, stats_own[:, far], stats_far[:, near], codes_far, head_weight
+    )
+    sent = on_chip_sum(*far_results).astype(BF16)
+    crossed = cross(sent)
+    near_grad, *near_results, near_loss = head_back_call(
+        near_logits, stats_own[:, near], stats_far[:, far], codes_near, head_weight
+    )
+    own_loss = near_loss[0, 0] + far_loss[0, 0]
+    grad_chosen = on_chip_sum(*near_results) + crossed.astype(F32)
+    grad_second, grad_low, final_gain_grad = norm_backward(
+        after_second, final_gain, [out_cotangent], None, 0.5, (picker.T, grad_chosen.astype(BF16))
+    )
+
+    grad_head = head_weights_call(
+        [*far_pieces, *near_pieces], [after(far_grad, grad_low), near_grad], vocab
+    )
+
+    def second_weights(grads, active, normed, grad_inner):
+        lefts, rights = [grads, normed], [active, grad_inner]
+        return (
+            weights_call(
+                [streamed(left) for left in lefts], [streamed(right) for right in rights],
+                "second_weights",
+            ),
         )
 
-    other = swap(pair)
-    pair = merge(pair, jnp.stack([other[:, 1], other[:, 0], other[:, 3], other[:, 2]], axis=1))
-    other = cross(pair)
-    pair = merge(pair, jnp.concatenate([other[:, 2:], other[:, :2]], axis=1))
-    log_totals = (pair[0] + jnp.log(pair[1])).reshape(2, 2 * slots)
-    codes = codes.reshape(2, 2 * slots)
-    own_loss = jnp.sum((codes[1, :slots] > 0).astype(F32) * log_totals[1, :slots])
-    grad_logits, head_results = [], []
-    for k in range(2):
-        hits = (codes[k] - 1 - own * vocab)[:, None] == jnp.arange(vocab)[None, :]
-        counted = (codes[k] > 0).astype(F32)
-        own_loss = own_loss - jnp.sum(jnp.where(hits, logits[k], 0.0))
-        shares = jnp.exp(logits[k] - log_totals[k][:, None])
-        grad = (counted[:, None] * (shares - hits.astype(F32))).astype(BF16)
-        grad_logits.append(grad)
-        head_results.append(dot_t(grad, head_weight, BF16))
-    grad_head = dot_rows(jnp.concatenate(head_parts), jnp.concatenate(grad_logits))
-    grad_chosen = scatter_parts(head_results).astype(BF16)
-    grad_output = out_cotangent.astype(F32) + weight_term(picker, grad_chosen)
-    grad_second, final_gain_grad = norm_backward(final_norm, final_gain, grad_output)
-
-    back, second_gain_grad, second_held, _ = branch_backward(
-        second_gain,
-        second_in,
-        second_out,
-        second_kept,
-        0.5 * grad_second,
-        2,
-        (lambda: [grad_head], lambda: []),
+    parts, _, (grad_second_both,) = branch_backward(
+        second_in, second_out, second_kept, grad_low, 2, (lambda done: [grad_head], lambda done: []),
+        second_weights,
     )
     grad_head = reduce_weights(grad_head)
-    grad_mixer = grad_second + back
-
-    grad_full = on_chip(grad_mixer.astype(BF16))
-    grads, active, normed, grad_inner, _ = second_held
-    grad_second_both = weights_call(
-        [after(grads, grad_full), normed], [active, grad_inner], "second_weights"
-    )
-    grad_second_both = reduce_weights(grad_second_both)
-    grad_shaped = dot_t(grad_full, mixer_out_both) * swish_slope(shaped)
-    sums = sum_channels(
-        jnp.stack([jnp.sum(grad_shaped, axis=0), jnp.sum(grad_shaped * normal, axis=0)])
-    )
+    grad_mixer, grad_low, second_gain_grad = norm_backward(
+        after_mixer, second_gain, parts, grad_second, 1.0
+    )
+
+    grad_shaped, grad_full, sums = rows_call(
+        shape_back_body, "mixer_shape_back", (grad_low, swap(grad_low)), [streamed(convolved)],
+        [stats, *mixer_outs], [(2 * width, F32), (D, None)], None, (2, 2 * width), scalars,
+    )
+    sums = sum_channels(sums)
     batch_shift_grad, batch_scale_grad = sums[0], sums[1]
-    grad_conv = (
-        scale_both
-        * inverse
-        * (grad_shaped - live_column / count * (batch_shift_grad + normal * batch_scale_grad))
-    )
-    depth_grad = jnp.stack(
-        [jnp.sum(grad_conv * shifted(glu, j - half, place), axis=0) for j in range(KERNEL)]
-    )
-    grad_glu = sum(shifted(grad_conv, half - j, place) * depth[j] for j in range(KERNEL))
-    grad_glu = grad_glu * live_column
-    grad_value = (grad_glu * gate).astype(BF16)
-    grad_gate = (grad_glu * value_in * gate * (1.0 - gate)).astype(BF16)
-    grad_both = jnp.concatenate(
-        [grad_value[:, :width], grad_gate[:, :width], grad_value[:, width:], grad_gate[:, width:]],
-        axis=1,
-    )
-    summed = dot_t(grad_both, mixer_both, BF16)
-    back, mixer_gain_grad = norm_backward(mixer_norm, mixer_gain, on_chip_sum(summed))
-    grad_attend = grad_mixer + back
-    mixer_grads = weights_call([mixer_in, grad_full], [grad_both, mixer_active], "mixer_weights")
+    grad_second_both = reduce_weights(after(grad_second_both, grad_head, sums))
+    grad_both, depth_grad, own_part, other_part = mixer_back_call(
+        scalars, grad_shaped, convolved, value_in, gate, stats, sums, depth, mixer_weights
+    )
+    grad_attend, grad_low, mixer_gain_grad = norm_backward(
+        after_attend, mixer_gain, [own_part, swap(other_part)], grad_mixer, 1.0
+    )
+    mixer_grads = weights_call(
+        [streamed(mixer_in), streamed(grad_full)], [grad_both, streamed(mixer_active)], "mixer_weights"
+    )
     counts = jnp.stack([own_loss, jnp.sum(keep)])
     counts = jnp.concatenate([counts, jnp.zeros((D - 2,), F32)])[None]
     depth_full = jnp.zeros((KERNEL, D), F32)
@@ -1191,66 +1727,80 @@
     gains = jnp.concatenate(
         [mixer_gain_grad, second_gain_grad, final_gain_grad, counts, depth_full], axis=0
     )
-    gain_run = sum_steps(gains)
-    next(gain_run)
-    gain_run.send(())
-    gain_crossed = gain_run.send(())
+    all_run = sum_steps(gains)
+    next(all_run)
+    all_run.send(())
+    gain_crossed = all_run.send(())
     mixer_crossed = [
         cross(after(part, gain_crossed))
         for part in (mixer_grads[:, 2 * width : 4 * width], mixer_grads[:, 5 * width :])
     ]
-    gain_run.send(())
-    gain_run.send(())
-    gains = gain_run.send(())
-    loss = gains[3, 0] / gains[3, 1]
-    depth_grad = lax.dynamic_slice_in_dim(gains[4:], own * width, width, 1)
-
-    grad_full = on_chip(grad_attend.astype(BF16))
-    grad_mixed = dot_t(grad_full, attend_out_both, BF16)
+
+    grad_mixed, grad_full = rows_call(
+        out_back_body, "attend_out_back", (grad_low, swap(grad_low)), [], attend_outs,
+        [(2 * width, BF16), (D, None)], None, scalars=place, turned=False,
+    )
+    grad_mixed = after(grad_mixed, mixer_grads, gain_crossed)
     grad_qkv = attend_backward_call(qkv, live_column, grad_mixed, log_total)
-    mixer_crossed = after(jnp.concatenate(mixer_crossed, axis=1), grad_qkv)
-    summed = dot_t(grad_qkv, qkv_weight, BF16)
-    back, attend_gain_grad = norm_backward(attend_norm, attend_gain, on_chip_sum(summed))
-    grad_first = grad_attend + back
-    middle = weights_call([attend_in, grad_full], [grad_qkv, mixed], "attend_weights")
+    own_part, other_part = rows_call(
+        qkv_back_body, "qkv_back", None, [after(grad_qkv, mixer_crossed[0])], qkv_weights, [], D, scalars=place,
+        turned=False,
+    )
+    grad_first, grad_low, attend_gain_grad = norm_backward(
+        after_first, attend_gain, [own_part, swap(other_part)], grad_attend, 0.5
+    )
+    attend_grads = weights_call(
+        [streamed(attend_in), streamed(grad_full)], [after(grad_qkv, grad_low), streamed(mixed)], "attend_weights"
+    )
+
+    def sides(first, second):
+        return jnp.concatenate([first, second], axis=1)
+
     mixer_sum = sides(mixer_grads[:, : 2 * width], mixer_grads[:, 4 * width : 5 * width])
+    mixer_crossed = sides(*after(mixer_crossed, attend_grads))
     mixer_sum = (mixer_sum.astype(F32) + mixer_crossed.astype(F32)).astype(BF16)
-    middle = reduce_weights(jnp.concatenate([middle, mixer_sum], axis=1))
-
-    back, first_gain_grad, (grads, active, normed, grad_inner, sent), result = branch_backward(
-        first_gain, first_in, first_out, first_kept, after(0.5 * grad_first, gains), 2
-    )
-    input_grad = grad_first + back
+    middle = reduce_weights(after(sides(attend_grads, mixer_sum), grad_second_both))
+
+    def first_weights(grads, active, normed, grad_inner):
+        grad_out = dot_rows(grads, active)
+        run_out = reduce_by_steps(grad_out)
+        return (grad_out, run_out, next(run_out))
+
+    parts, (grads, grad_inner, active, normed), (grad_out, run_out, _) = branch_backward(
+        first_in, first_out, first_kept, grad_low, 2, (lambda done: [attend_grads], lambda done: []), first_weights
+    )
+    grad_in = dot_rows(normed, after(grad_inner, grad_out))
+    run_in = reduce_by_steps(grad_in)
+    next(run_in)
+    all_run.send((grad_in,))
+    input_grad, _, first_gain_grad = norm_backward(frames, first_gain, parts, grad_first, 1.0)
     gain_run = sum_steps(jnp.concatenate([attend_gain_grad, first_gain_grad], axis=0))
     next(gain_run)
     gain_run.send(())
     gain_run.send(())
-    grad_out = dot_rows(after(grads, sent), active)
-    run_out = reduce_by_steps(grad_out)
-    next(run_out)
-    grad_in = dot_rows(normed, after(grad_inner, grad_out))
-    run_in = reduce_by_steps(grad_in)
-    next(run_in)
-    grad_head = after(grad_head, grad_in).astype(F32)
-    grad_second_both = after(grad_second_both, grad_in).astype(F32)
-    arrived = run_out.send((grad_in,))
+    all_run.send((input_grad,))
+    grad_head = after(grad_head, input_grad).astype(F32)
+    grad_second_both = after(grad_second_both, input_grad).astype(F32)
+    arrived = run_out.send((input_grad,))
+    gains = all_run.send((arrived,))
+    loss = gains[3, 0] / gains[3, 1]
+    depth_grad = lax.dynamic_slice_in_dim(gains[4:], own * width, width, 1)
     arrived = run_in.send((arrived,))
     gain_run.send((arrived,))
+    middle = after(middle, arrived).astype(F32)
+    attend_grads, mixer_sum = middle[:, : 8 * width], middle[:, 8 * width :]
+    crossed = cross(sides(attend_grads[:, 3 * width : 6 * width], attend_grads[:, 7 * width :]).astype(BF16))
+    own_part = sides(attend_grads[:, : 3 * width], attend_grads[:, 6 * width : 7 * width])
     run_out.send((arrived,))
-    arrived = run_in.send(())
+    arrived = run_in.send((own_part,))
+    attend_grads = own_part + after(crossed, arrived).astype(F32)
     gain_run.send((arrived,))
     grad_first_out = run_out.send(())
     grad_first_in = run_in.send(())
     first_gain_grad = gain_run.send((grad_first_in,))
     grad_second_out, grad_second_in = jnp.split(grad_second_both, 2, axis=1)
-    middle = after(middle, grad_first_in).astype(F32)
-    crossed = cross(
-        jnp.concatenate([middle[:, 3 * width : 6 * width], middle[:, 7 * width : 8 * width]], axis=1).astype(BF16)
-    )
-    own_part = jnp.concatenate([middle[:, : 3 * width], middle[:, 6 * width : 7 * width]], axis=1)
-    attend_grads = own_part + crossed.astype(F32)
     grad_query, grad_key, grad_value, grad_out = jnp.split(attend_grads, 4, axis=1)
-    grad_mixer_value, grad_mixer_gate, grad_mixer_out = jnp.split(middle[:, 8 * width :], 3, axis=1)
+    grad_mixer_value, grad_mixer_gate, grad_mixer_out = jnp.split(mixer_sum, 3, axis=1)
     return (
         output,
         loss,

time: 704 us -> 691 us (0.982)
  Pallas kernels: 125 us -> 243 us
  other arithmetic: 87.5 us -> 23.5 us
  matrix products: 56.6 us -> 13.6 us
  local copies, waits for them, and re-layouts: 72.2 us -> 36.4 us
  starting transfers between devices: 68.3 us -> 95.3 us
  waiting for transfers between devices: 262 us -> 251 us
    pallas_call x3 -> x27, Pallas kernels: 28.8 us -> 148 us  [the longest x6 31.9 us: rows_call(): pl.pallas_call(kernel, grid_spec=pltpu.PrefetchScalarGridSpec(num_scalar_...]
    reduce_sum x20 -> x0, other arithmetic: 34.2 us -> none  [the longest x2 7.86 us: on_device_block(): own_loss = own_loss - jnp.sum(jnp.where(hits, logits[k], 0.0))]
    convert_element_type x16 -> x6, other arithmetic: 25.7 us -> 2.89 us  [the longest x1 1.21 us: on_device_block(): middle = after(middle, arrived).astype(F32)]
    ppermute x29 -> x31, waiting for transfers between devices: 146 us -> 126 us  [cross(): return lax.ppermute(values, 'mp', CHIP_PAIRS)]
    ppermute x29 -> x31, starting transfers between devices: 27.5 us -> 46.9 us  [cross(): return lax.ppermute(values, 'mp', CHIP_PAIRS)]
    dot_general x7 -> x1, matrix products: 18 us -> 0.49 us  [dot(): return jnp.dot(left, right, preferred_element_type=F32).astype(kind)]
    unnamed x277 -> x154, local copies, waits for them, and re-layouts: 35.3 us -> 18.8 us
    dot_general x6 -> x0, matrix products: 15.7 us -> none  [matmul_t(): lax.dot_general(left, right, (((1,), (1,)), ((), ())), preferred_element_...]
  transfers between devices with their start and end apart: 112 -> 114, of which waited for: 66 -> 67; matrix products, arithmetic and copies ran while one was open for 21% -> 7% of each run, Pallas kernels for 18% -> 29%
where the time goes in v3:
time: 691 us; the launch traced here: 681 us
  waiting for transfers between devices  251 us (36%)
  Pallas kernels  243 us (35%)
  starting transfers between devices  95.3 us (14%)
  local copies, waits for them, and re-layouts  36.4 us (5%)
  other arithmetic  23.5 us (3%)
  between operations  18.1 us (3%)
  matrix products  13.6 us (2%)
    ppermute x31, waiting for transfers between devices, cross(): return lax.ppermute(values, 'mp', CHIP_PAIRS)  126 us
    pallas_call x12, Pallas kernels, pieces_call(): pl.pallas_call(kernel, grid=(steps,), in_specs=in_specs, out_specs=[place...  67.5 us
    ppermute x6, waiting for transfers between devices, reduce_by_steps(): arrived = lax.ppermute(send, 'dp', pairs)  64.1 us
    ppermute x31, starting transfers between devices, cross(): return lax.ppermute(values, 'mp', CHIP_PAIRS)  46.9 us
    pallas_call x6, Pallas kernels, rows_call(): pl.pallas_call(kernel, grid_spec=pltpu.PrefetchScalarGridSpec(num_scalar_...  31.9 us
    pallas_call x3, Pallas kernels, weights_call(): pl.pallas_call(lambda *refs: kernel(number, *refs[:2 * number], refs[-1])...  31 us
    ppermute x54, waiting for transfers between devices, swap(): return lax.ppermute(values, 'mp', CORE_PAIRS)  23.2 us
    pallas_call x5, Pallas kernels, norm_backward(): pl.pallas_call(kernel, grid=(rows // block,), in_specs=[row, one] + part_...  21.9 us
  transfers between devices with their start and end apart: 114, of which 67 were waited for; matrix products, arithmetic and copies ran while one was open for 7% of the time, Pallas kernels for 29%

profile of v3, /device:TPU:0, one launch (start us, length us, event | category | flops | bytes accessed | tf_op | source)
XLA Modules:
  0.0 680.9 jit_solution(11100536215547770849)
XLA Ops:
  17.7 7.7 %branch_forward.6 = (bf16[2048,1024]{1,0:T(8,128)(2,1)}, bf16[2048,1024]{1,0:T(8,128)(2,1)}, bf16[2048,1024]{1,0:T(8,128)(2,1)}, bf16[512,1024]{1,0:T(8,128)(2,1)S(1)}, bf16[512,1024]{1,0:T(8,128)(2,1)S(1)}) custom-call(bf16[512,1024]{1,0:T(8,128)(2,1)S(1)} %norm_forward.5.refs_0_, bf16[512,1024]{1,0:T(8,128)(2,1)} %collective-permute-done.refs_1_, ...), custom_call_target="tpu_custom_call" | custom-call | flops 4294967 | bytes 4194 | tf_op jit(solution)/shard_map/branch_forward/pallas_call | solution.py:754
  63.3 8.1 %collective-permute-done.12.refs_2_ = bf16[256,1024]{1,0:T(8,128)(2,1)S(1)} collective-permute-done((bf16[256,1024]{1,0:T(8,128)(2,1)S(1)}, bf16[256,1024]{1,0:T(8,128)(2,1)S(1)}, u32[]{:S(2)}, u32[]{:S(2)}) %collective-permute-start.12) | collective-permute-done | bytes 524320 | tf_op jit(solution)/shard_map/ppermute | solution.py:516
  73.2 11.2 %collective-permute-done.19.refs_3_ = bf16[256,1024]{1,0:T(8,128)(2,1)S(1)} collective-permute-done((bf16[256,1024]{1,0:T(8,128)(2,1)S(1)}, bf16[256,1024]{1,0:T(8,128)(2,1)S(1)}, u32[]{:S(2)}, u32[]{:S(2)}) %collective-permute-start.19) | collective-permute-done | bytes 524320 | tf_op jit(solution)/shard_map/ppermute | solution.py:516
  102.5 6.7 qkv.1
  113.7 8.6 %attend_forward.1 = (bf16[1024,512]{1,0:T(8,128)(2,1)S(1)}, f32[4,1,1024]{2,1,0:T(1,128)S(1)}) custom-call(f32[1024,1]{1,0:T(8,128)S(1)} %fusion.12.live_ref, bf16[1024,1536]{1,0:T(8,128)(2,1)S(1)} %get-tuple-element.208.query_ref.keys_ref.values_ref, bf16[1024,1536]{1,0:T(8,128)(2,1)S(1)} %get-tuple-element.208.query_ref.keys_ref.values_ref, ...), custom_call_target="tpu_custom_call" | custom-call | flops 2147483648 | bytes 12582912 | tf_op jit(solution)/shard_map/attend_forward/pallas_call | solution.py:875
  136.8 8.0 %mixer_front.1 = (bf16[1024,1024]{1,0:T(8,128)(2,1)}, f32[1024,512]{1,0:T(8,128)}, f32[1024,512]{1,0:T(8,128)}, f32[1024,512]{1,0:T(8,128)S(1)}, f32[3,512]{1,0:T(4,128)S(1)}) custom-call(s32[2]{0:T(128)S(1)} %pad_add_fusion.2.scalar_ref, bf16[512,1024]{1,0:T(8,128)(2,1)S(1)} %get-tuple-element.214.own_ref, ...), custom_call_target="tpu_custom_call" | custom-call | flops 2147483648 | bytes 2097152 | tf_op jit(solution)/shard_map/mixer_front/pallas_call | solution.py:1175
  174.0 6.5 branch_forward.9
  192.6 7.7 %collective-permute-done.42.refs_0_ = bf16[256,1024]{1,0:T(8,128)(2,1)S(1)} collective-permute-done((bf16[256,1024]{1,0:T(8,128)(2,1)S(1)}, bf16[256,1024]{1,0:T(8,128)(2,1)S(1)}, u32[]{:S(2)}, u32[]{:S(2)}) %collective-permute-start.42) | collective-permute-done | bytes 524320 | tf_op jit(solution)/shard_map/ppermute | solution.py:516
  217.3 11.8 %collective-permute-done.47.refs_3_ = bf16[256,1024]{1,0:T(8,128)(2,1)S(1)} collective-permute-done((bf16[256,1024]{1,0:T(8,128)(2,1)S(1)}, bf16[256,1024]{1,0:T(8,128)(2,1)S(1)}, u32[]{:S(2)}, u32[]{:S(2)}) %collective-permute-start.47) | collective-permute-done | bytes 524320 | tf_op jit(solution)/shard_map/ppermute | solution.py:516
  240.0 7.9 %collective-permute-done.49.first_ref.refs_0_ = bf16[256,1024]{1,0:T(8,128)(2,1)S(1)} collective-permute-done((bf16[256,1024]{1,0:T(8,128)(2,1)S(1)}, bf16[256,1024]{1,0:T(8,128)(2,1)S(1)}, u32[]{:S(2)}, u32[]{:S(2)}) %collective-permute-start.49) | collective-permute-done | bytes 524320 | tf_op jit(solution)/shard_map/ppermute | solution.py:516
  277.7 12.0 %collective-permute-done.55 = bf16[256,1024]{1,0:T(8,128)(2,1)S(1)} collective-permute-done((bf16[256,1024]{1,0:T(8,128)(2,1)S(1)}, bf16[256,1024]{1,0:T(8,128)(2,1)S(1)}, u32[]{:S(2)}, u32[]{:S(2)}) %collective-permute-start.55) | collective-permute-done | bytes 524320 | tf_op jit(solution)/shard_map/ppermute | solution.py:516
  303.2 8.6 %branch_backward.6 = (bf16[2048,1024]{1,0:T(8,128)(2,1)}, bf16[2048,1024]{1,0:T(8,128)(2,1)}, bf16[512,1024]{1,0:T(8,128)(2,1)S(1)}, bf16[512,1024]{1,0:T(8,128)(2,1)}) custom-call(bf16[512,1024]{1,0:T(8,128)(2,1)S(1)} %get-tuple-element.249.refs_0_, bf16[512,1024]{1,0:T(8,128)(2,1)S(1)} %collective-permute-done.56.refs_1_, ...), custom_call_target="tpu_custom_call" | custom-call | flops 4294967 | bytes 4194 | tf_op jit(solution)/shard_map/branch_backward/pallas_call | solution.py:754
  347.4 15.4 %second_weights.1 = bf16[1024,2048]{1,0:T(8,128)(2,1)} custom-call(bf16[2048,1024]{1,0:T(8,128)(2,1)} %get-tuple-element.269.refs_0_, bf16[2048,1024]{1,0:T(8,128)(2,1)} %get-tuple-element.270.refs_1_, bf16[2048,1024]{1,0:T(8,128)(2,1)} %get-tuple-element.271.refs_2_, bf16[2048,1024]{1,0:T(8,128)(2,1)} %get-tuple-element.272.refs_3_), custom_call_target="tpu_custom_call" | custom-call | flops 8589934592 | bytes 4194304 | tf_op jit(solution)/shard_map/second_weights/pallas_call | solution.py:1471
  392.8 12.1 %mixer_back.1 = (bf16[1024,1024]{1,0:T(8,128)(2,1)S(1)}, f32[5,512]{1,0:T(8,128)S(1)}, bf16[512,1024]{1,0:T(8,128)(2,1)S(1)}, bf16[512,1024]{1,0:T(8,128)(2,1)}) custom-call(s32[2]{0:T(128)S(1)} %pad_add_fusion.2.scalar_ref, f32[1024,512]{1,0:T(8,128)} %copy-done.13, f32[1024,512]{1,0:T(8,128)} %copy-done.12, f32[1024,512]{1,0:T(8,128)} %get-tuple-element.277.value_in, ...), custom_call_target="tpu_custom_call" | custom-call | flops 2147483648 | bytes 2097152 | tf_op jit(solution)/shard_map/mixer_back/pallas_call | solution.py:1245
  416.9 7.1 %mixer_weights.1 = bf16[1024,1536]{1,0:T(8,128)(2,1)} custom-call(bf16[1024,1024]{1,0:T(8,128)(2,1)} %get-tuple-element.292.refs_0_, bf16[1024,1024]{1,0:T(8,128)(2,1)S(1)} %copy-done.32, bf16[1024,1024]{1,0:T(8,128)(2,1)} %get-tuple-element.294.refs_2_, bf16[1024,512]{1,0:T(8,128)(2,1)} %get-tuple-element.295.refs_3_), custom_call_target="tpu_custom_call" | custom-call | flops 3221225472 | bytes 3145728 | tf_op jit(solution)/shard_map/mixer_weights/pallas_call | solution.py:1471
  434.5 18.3 %attend_backward.1.refs_0_.refs_1_ = bf16[1024,1536]{1,0:T(8,128)(2,1)S(1)} custom-call(f32[1024,1]{1,0:T(8,128)S(1)} %copy-done.15, bf16[1024,1536]{1,0:T(8,128)(2,1)S(1)} %copy-done.9, bf16[1024,1536]{1,0:T(8,128)(2,1)S(1)} %copy-done.9, bf16[1024,1536]{1,0:T(8,128)(2,1)S(1)} %copy-done.9, bf16[1024,512]{1,0:T(8,128)(2,1)S(1)} %get-tuple-element.296.grad_ref, ...), custom_call_target="tpu_custom_call" | custom-call | flops 5368709120 | bytes 12582912 | tf_op jit(solution)/shard_map/attend_backward/pallas_call | solution.py:944
  452.8 6.9 %qkv_back.1 = (bf16[512,1024]{1,0:T(8,128)(2,1)S(1)}, bf16[512,1024]{1,0:T(8,128)(2,1)S(1)}) custom-call(s32[2]{0:T(128)S(1)} %pad_add_fusion.1.scalar_ref, bf16[1024,1536]{1,0:T(8,128)(2,1)S(1)} %attend_backward.1.refs_0_.refs_1_, bf16[1024,256]{1,0:T(8,128)(2,1)} %refs_1_.3, bf16[1024,256]{1,0:T(8,128)(2,1)} %refs_2_.19, bf16[1024,256]{1,0:T(8,128)(2,1)} %refs_3_.24, ...), custom_call_target="tpu_custom_call" | custom-call | flops 3221225472 | bytes 3145728 | tf_op jit(solution)/shard_map/qkv_back/pallas_call | solution.py:1032
  466.7 8.5 %attend_weights.1 = bf16[1024,2048]{1,0:T(8,128)(2,1)} custom-call(bf16[1024,1024]{1,0:T(8,128)(2,1)} %get-tuple-element.307.refs_0_, bf16[1024,1536]{1,0:T(8,128)(2,1)S(1)} %attend_backward.1.refs_0_.refs_1_, bf16[1024,1024]{1,0:T(8,128)(2,1)} %get-tuple-element.309.refs_2_, bf16[1024,512]{1,0:T(8,128)(2,1)} %copy-done.33), custom_call_target="tpu_custom_call" | custom-call | flops 4294967296 | bytes 4194304 | tf_op jit(solution)/shard_map/attend_weights/pallas_call | solution.py:1471
  484.9 8.0 %branch_backward.9 = (bf16[2048,1024]{1,0:T(8,128)(2,1)}, bf16[2048,1024]{1,0:T(8,128)(2,1)}, bf16[512,1024]{1,0:T(8,128)(2,1)S(1)}, bf16[512,1024]{1,0:T(8,128)(2,1)S(1)}) custom-call(bf16[512,1024]{1,0:T(8,128)(2,1)S(1)} %get-tuple-element.303.refs_0_, bf16[512,1024]{1,0:T(8,128)(2,1)S(1)} %collective-permute-done.84.refs_1_, ...), custom_call_target="tpu_custom_call" | custom-call | flops 4294967 | bytes 4194 | tf_op jit(solution)/shard_map/branch_backward/pallas_call | solution.py:754
  527.4 8.3 %convolution_convert_fusion.1 = bf16[1024,1024]{1,0:T(8,128)(2,1)S(1)} fusion(bf16[2048,1024]{1,0:T(8,128)(2,1)} %get-tuple-element.323, bf16[2048,1024]{1,0:T(8,128)(2,1)} %get-tuple-element.324), kind=kOutput, calls=%fused_computation.7 | convolution fusion | flops 4296015872 | bytes 10485760 | tf_op jit(solution)/shard_map/dot_general | solution.py:66
  551.0 26.3 %collective-permute-done.98 = bf16[4,128,1024]{2,1,0:T(8,128)(2,1)} collective-permute-done((bf16[4,128,1024]{2,1,0:T(8,128)(2,1)}, bf16[4,128,1024]{2,1,0:T(8,128)(2,1)}, u32[]{:S(2)}, u32[]{:S(2)}) %collective-permute-start.98) | collective-permute-done | bytes 1048608 | tf_op jit(solution)/shard_map/ppermute | solution.py:1533
  581.3 25.1 %collective-permute-done.103 = bf16[4,128,1024]{2,1,0:T(8,128)(2,1)} collective-permute-done((bf16[4,128,1024]{2,1,0:T(8,128)(2,1)}, bf16[4,128,1024]{2,1,0:T(8,128)(2,1)}, u32[]{:S(2)}, u32[]{:S(2)}) %collective-permute-start.103) | collective-permute-done | bytes 1048608 | tf_op jit(solution)/shard_map/ppermute | solution.py:1533
  615.7 11.9 %collective-permute-done.97 = f32[9,1024]{1,0:T(8,128)S(1)} collective-permute-done((f32[9,1024]{1,0:T(8,128)S(1)}, f32[9,1024]{1,0:T(8,128)S(1)}, u32[]{:S(2)}, u32[]{:S(2)}) %collective-permute-start.97) | collective-permute-done | bytes 36896 | tf_op jit(solution)/shard_map/ppermute | solution.py:1514
  642.5 12.0 %collective-permute-done.107 = bf16[128,1024]{1,0:T(8,128)(2,1)S(1)} collective-permute-done((bf16[128,1024]{1,0:T(8,128)(2,1)S(1)}, bf16[128,1024]{1,0:T(8,128)(2,1)S(1)}, u32[]{:S(2)}, u32[]{:S(2)}) %collective-permute-start.107) | collective-permute-done | bytes 262176 | tf_op jit(solution)/shard_map/ppermute | solution.py:1533
  (532 shorter events, 398.2 us)
Async XLA Ops:
  7.2 385.5 %reduce-scatter.4.cloned.1.call-start = ((), (), s32[]{:S(2)}) async-start(), calls=%async_computation.3 | async-start | bytes 4718592 | tf_op jit(solution)/shard_map/reduce_scatter | solution.py:1503
  29.7 15.7 %collective-permute-start.4 = (s32[1,256]{1,0:T(1,128)}, s32[1,256]{1,0:T(1,128)}, u32[]{:S(2)}, u32[]{:S(2)}) collective-permute-start(s32[1,256]{1,0:T(1,128)} %bitcast.2), channel_id=1, source_target_pairs={{0,1},{1,0},{2,3},{3,2},{4,5},{5,4},{6,7},{7,6},{8,9},{9,8},{10,11... | collective-permute-start | bytes 3080 | tf_op jit(solution)/shard_map/ppermute | solution.py:512
  32.5 20.4 %collective-permute-start.1 = (bf16[256,768]{1,0:T(8,128)(2,1)S(1)}, bf16[256,768]{1,0:T(8,128)(2,1)}, u32[]{:S(2)}, u32[]{:S(2)}) collective-permute-start(bf16[256,768]{1,0:T(8,128)(2,1)S(1)} %fusion.16), channel_id=1, source_target_pairs={{0,2},{2,0},{1,3},{3,1},{4,6},{6,4},{5,7},{7,5},{8,10},{10,8},{9,1... | collective-permute-start | bytes 1179656 | tf_op jit(solution)/shard_map/ppermute | solution.py:516
  48.9 24.3 %collective-permute-start.6 = (bf16[512,1024]{1,0:T(8,128)(2,1)S(1)}, bf16[512,1024]{1,0:T(8,128)(2,1)S(1)}, u32[]{:S(2)}, u32[]{:S(2)}) collective-permute-start(bf16[512,1024]{1,0:T(8,128)(2,1)S(1)} %copy-done.35), channel_id=1, source_target_pairs={{0,1},{1,0},{2,3},{3,2},{4,5},{5,4},{6,7},{7,6},{8,9},{9,8},{10,11... | collective-permute-start | bytes 3145736 | tf_op jit(solution)/shard_map/ppermute | solution.py:512
  89.5 24.2 %collective-permute-start.24 = (bf16[1024,256]{1,0:T(8,128)(2,1)S(1)}, bf16[1024,256]{1,0:T(8,128)(2,1)S(1)}, u32[]{:S(2)}, u32[]{:S(2)}) collective-permute-start(bf16[1024,256]{1,0:T(8,128)(2,1)S(1)} %copy-done.51), channel_id=1, source_target_pairs={{0,2},{2,0},{1,3},{3,1},{4,6},{6,4},{5,7},{7,5},{8,10},{10,8},{9,1... | collective-permute-start | bytes 1572872 | tf_op jit(solution)/shard_map/ppermute | solution.py:516
  96.7 27.9 %collective-permute-start.25 = (bf16[1024,256]{1,0:T(8,128)(2,1)S(1)}, bf16[1024,256]{1,0:T(8,128)(2,1)S(1)}, u32[]{:S(2)}, u32[]{:S(2)}) collective-permute-start(bf16[1024,256]{1,0:T(8,128)(2,1)S(1)} %copy-done.52), channel_id=1, source_target_pairs={{0,2},{2,0},{1,3},{3,1},{4,6},{6,4},{5,7},{7,5},{8,10},{10,8},{9,1... | collective-permute-start | bytes 1572872 | tf_op jit(solution)/shard_map/ppermute | solution.py:516
  200.9 16.4 %collective-permute-start.35 = (bf16[512,1024]{1,0:T(8,128)(2,1)S(1)}, bf16[512,1024]{1,0:T(8,128)(2,1)S(1)}, u32[]{:S(2)}, u32[]{:S(2)}) collective-permute-start(bf16[512,1024]{1,0:T(8,128)(2,1)S(1)} %get-tuple-element.223), channel_id=1, source_target_pairs={{0,1},{1,0},{2,3},{3,2},{4,5},{5,4},{6,7},{7,6},{8,9},{9,8},{10,11... | collective-permute-start | bytes 3145736 | tf_op jit(solution)/shard_map/ppermute | solution.py:512
  300.4 181.7 %reduce-scatter.6.cloned.1.call-start = ((), (), s32[]{:S(2)}) async-start(), calls=%async_computation.4 | async-start | bytes 4718592 | tf_op jit(solution)/shard_map/reduce_scatter | solution.py:1503
  339.0 23.7 %collective-permute-start.57 = (bf16[512,1024]{1,0:T(8,128)(2,1)}, bf16[512,1024]{1,0:T(8,128)(2,1)S(1)}, u32[]{:S(2)}, u32[]{:S(2)}) collective-permute-start(bf16[512,1024]{1,0:T(8,128)(2,1)} %get-tuple-element.252), channel_id=1, source_target_pairs={{0,1},{1,0},{2,3},{3,2},{4,5},{5,4},{6,7},{7,6},{8,9},{9,8},{10,11... | collective-permute-start | bytes 3145736 | tf_op jit(solution)/shard_map/ppermute | solution.py:512
  345.6 17.1 %collective-permute-start.69 = (bf16[256,1024]{1,0:T(8,128)(2,1)}, bf16[256,1024]{1,0:T(8,128)(2,1)S(1)}, u32[]{:S(2)}, u32[]{:S(2)}) collective-permute-start(bf16[256,1024]{1,0:T(8,128)(2,1)} %add_convert_fusion.3), channel_id=1, source_target_pairs={{0,2},{2,0},{1,3},{3,1},{4,6},{6,4},{5,7},{7,5},{8,10},{10,8},{9,1... | collective-permute-start | bytes 1572872 | tf_op jit(solution)/shard_map/ppermute | solution.py:516
  392.8 268.9 %reduce-scatter.8.cloned.1.call-start = ((), (), s32[]{:S(2)}) async-start(), calls=%async_computation.5 | async-start | bytes 6488064 | tf_op jit(solution)/shard_map/reduce_scatter | solution.py:1503
  413.7 16.3 %collective-permute-start.79 = (bf16[512,1024]{1,0:T(8,128)(2,1)S(1)}, bf16[512,1024]{1,0:T(8,128)(2,1)S(1)}, u32[]{:S(2)}, u32[]{:S(2)}) collective-permute-start(bf16[512,1024]{1,0:T(8,128)(2,1)S(1)} %get-tuple-element.290.refs_0_), channel_id=1, source_target_pairs={{0,1},{1,0},{2,3},{3,2},{4,5},{5,4},{6,7},{7,6},{8,9},{9,8},{10,11... | collective-permute-start | bytes 3145736 | tf_op jit(solution)/shard_map/ppermute | solution.py:512
  428.4 24.4 %collective-permute-start.80 = (bf16[1024,512]{1,0:T(8,128)(2,1)S(1)}, bf16[1024,512]{1,0:T(8,128)(2,1)S(1)}, u32[]{:S(2)}, u32[]{:S(2)}) collective-permute-start(bf16[1024,512]{1,0:T(8,128)(2,1)S(1)} %get-tuple-element.298), channel_id=1, source_target_pairs={{0,2},{2,0},{1,3},{3,1},{4,6},{6,4},{5,7},{7,5},{8,10},{10,8},{9,1... | collective-permute-start | bytes 3145736 | tf_op jit(solution)/shard_map/ppermute | solution.py:516
  483.9 24.1 %collective-permute-start.82 = (bf16[256,1024]{1,0:T(8,128)(2,1)S(1)}, bf16[256,1024]{1,0:T(8,128)(2,1)S(1)}, u32[]{:S(2)}, u32[]{:S(2)}) collective-permute-start(bf16[256,1024]{1,0:T(8,128)(2,1)S(1)} %get-tuple-element.429), channel_id=1, source_target_pairs={{0,2},{2,0},{1,3},{3,1},{4,6},{6,4},{5,7},{7,5},{8,10},{10,8},{9,1... | collective-permute-start | bytes 1572872 | tf_op jit(solution)/shard_map/ppermute | solution.py:516
  519.1 27.0 %collective-permute-start.95 = (bf16[512,1024]{1,0:T(8,128)(2,1)}, bf16[512,1024]{1,0:T(8,128)(2,1)S(1)}, u32[]{:S(2)}, u32[]{:S(2)}) collective-permute-start(bf16[512,1024]{1,0:T(8,128)(2,1)} %copy-done.36), channel_id=1, source_target_pairs={{0,1},{1,0},{2,3},{3,2},{4,5},{5,4},{6,7},{7,6},{8,9},{9,8},{10,11... | collective-permute-start | bytes 3145736 | tf_op jit(solution)/shard_map/ppermute | solution.py:512
  525.9 20.2 %collective-permute-start.96 = (bf16[256,1024]{1,0:T(8,128)(2,1)}, bf16[256,1024]{1,0:T(8,128)(2,1)S(1)}, u32[]{:S(2)}, u32[]{:S(2)}) collective-permute-start(bf16[256,1024]{1,0:T(8,128)(2,1)} %add_convert_fusion.2), channel_id=1, source_target_pairs={{0,2},{2,0},{1,3},{3,1},{4,6},{6,4},{5,7},{7,5},{8,10},{10,8},{9,1... | collective-permute-start | bytes 1572872 | tf_op jit(solution)/shard_map/ppermute | solution.py:516
  536.9 40.4 %collective-permute-start.98 = (bf16[4,128,1024]{2,1,0:T(8,128)(2,1)}, bf16[4,128,1024]{2,1,0:T(8,128)(2,1)}, u32[]{:S(2)}, u32[]{:S(2)}) collective-permute-start(bf16[4,128,1024]{2,1,0:T(8,128)(2,1)} %dynamic-slice_bitcast_fusion.1), channel_id=1, source_target_pairs={{0,4},{4,0},{8,12},{12,8},{16,20},{20,16},{24,28},{28,24},{1,5},{5... | collective-permute-start | bytes 3145736 | tf_op jit(solution)/shard_map/ppermute | solution.py:1533
  545.5 60.9 %collective-permute-start.103 = (bf16[4,128,1024]{2,1,0:T(8,128)(2,1)}, bf16[4,128,1024]{2,1,0:T(8,128)(2,1)}, u32[]{:S(2)}, u32[]{:S(2)}) collective-permute-start(bf16[4,128,1024]{2,1,0:T(8,128)(2,1)} %dynamic-slice_bitcast_fusion), channel_id=1, source_target_pairs={{0,4},{4,0},{8,12},{12,8},{16,20},{20,16},{24,28},{28,24},{1,5},{5... | collective-permute-start | bytes 3145736 | tf_op jit(solution)/shard_map/ppermute | solution.py:1533
  579.0 27.5 %collective-permute-start.99 = (bf16[2,128,1024]{2,1,0:T(8,128)(2,1)S(1)}, bf16[2,128,1024]{2,1,0:T(8,128)(2,1)S(1)}, u32[]{:S(2)}, u32[]{:S(2)}) collective-permute-start(bf16[2,128,1024]{2,1,0:T(8,128)(2,1)S(1)} %dynamic-slice_bitcast_fusion.3), channel_id=1, source_target_pairs={{0,8},{8,0},{4,12},{12,4},{16,24},{24,16},{20,28},{28,20},{1,9},{9... | collective-permute-start | bytes 1572872 | tf_op jit(solution)/shard_map/ppermute | solution.py:1533
  580.2 31.9 %collective-permute-start.94 = (f32[9,1024]{1,0:T(8,128)S(1)}, f32[9,1024]{1,0:T(8,128)S(1)}, u32[]{:S(2)}, u32[]{:S(2)}) collective-permute-start(f32[9,1024]{1,0:T(8,128)S(1)} %add.295), channel_id=1, source_target_pairs={{0,8},{8,0},{4,12},{12,4},{16,24},{24,16},{20,28},{28,20},{1,9},{9... | collective-permute-start | bytes 110600 | tf_op jit(solution)/shard_map/ppermute | solution.py:1514
  608.5 19.9 %collective-permute-start.104 = (bf16[2,128,1024]{2,1,0:T(8,128)(2,1)S(1)}, bf16[2,128,1024]{2,1,0:T(8,128)(2,1)S(1)}, u32[]{:S(2)}, u32[]{:S(2)}) collective-permute-start(bf16[2,128,1024]{2,1,0:T(8,128)(2,1)S(1)} %dynamic-slice_bitcast_fusion.2), channel_id=1, source_target_pairs={{0,8},{8,0},{4,12},{12,4},{16,24},{24,16},{20,28},{28,20},{1,9},{9... | collective-permute-start | bytes 1572872 | tf_op jit(solution)/shard_map/ppermute | solution.py:1533
  614.2 18.9 %collective-permute-start.102 = (f32[2,1024]{1,0:T(2,128)S(1)}, f32[2,1024]{1,0:T(2,128)S(1)}, u32[]{:S(2)}, u32[]{:S(2)}) collective-permute-start(f32[2,1024]{1,0:T(2,128)S(1)} %fusion.66), channel_id=1, source_target_pairs={{0,4},{4,0},{8,12},{12,8},{16,20},{20,16},{24,28},{28,24},{1,5},{5... | collective-permute-start | bytes 24584 | tf_op jit(solution)/shard_map/ppermute | solution.py:1514
  628.6 26.0 %collective-permute-start.109 = (bf16[128,1024]{1,0:T(8,128)(2,1)S(1)}, bf16[128,1024]{1,0:T(8,128)(2,1)S(1)}, u32[]{:S(2)}, u32[]{:S(2)}) collective-permute-start(bf16[128,1024]{1,0:T(8,128)(2,1)S(1)} %dynamic-slice_bitcast_fusion.4), channel_id=1, source_target_pairs={{0,16},{16,0},{4,20},{20,4},{8,24},{24,8},{12,28},{28,12},{1,17},{... | collective-permute-start | bytes 786440 | tf_op jit(solution)/shard_map/ppermute | solution.py:1533
  631.6 22.9 %collective-permute-start.107 = (bf16[128,1024]{1,0:T(8,128)(2,1)S(1)}, bf16[128,1024]{1,0:T(8,128)(2,1)S(1)}, u32[]{:S(2)}, u32[]{:S(2)}) collective-permute-start(bf16[128,1024]{1,0:T(8,128)(2,1)S(1)} %dynamic-slice_bitcast_fusion.5), channel_id=1, source_target_pairs={{0,16},{16,0},{4,20},{20,4},{8,24},{24,8},{12,28},{28,12},{1,17},{... | collective-permute-start | bytes 786440 | tf_op jit(solution)/shard_map/ppermute | solution.py:1533
  (162 other events, 1421.5 us)
Sparse Core Ops, SparseCore 0:
  300.6 89.5 reduce-scatter.3
  394.2 87.9 reduce-scatter.5
  485.8 135.0 reduce-scatter.7

commit v4 on v3

--- a/solution.py
+++ b/solution.py
@@ -936,7 +936,7 @@
 def attend_backward_call(qkv, live_column, grad_mixed, log_total):
     length = qkv.shape[0]
     heads = qkv.shape[1] // (3 * HEAD_DIM)
-    block = length // 2
+    block = length
 
     def whole(kind):
         return pl.BlockSpec((length, HEAD_DIM), lambda h, b: (0, head_column(h, kind)))
@@ -955,7 +955,7 @@
         out_specs=pl.BlockSpec(qkv.shape, lambda h, b: (0, 0)),
         out_shape=jax.ShapeDtypeStruct(qkv.shape, BF16),
         scratch_shapes=[pltpu.VMEM((length, HEAD_DIM), F32), pltpu.VMEM((length, HEAD_DIM), F32)],
-        compiler_params=pltpu.CompilerParams(vmem_limit_bytes=40 << 20),
+        compiler_params=pltpu.CompilerParams(vmem_limit_bytes=44 << 20),
         cost_estimate=cost(10 * heads * length * length * HEAD_DIM, 8 * qkv.size),
         name="attend_backward",
     )(live_column, qkv, qkv, qkv, grad_mixed, log_total)
@@ -1531,7 +1531,7 @@
         keep = lax.dynamic_index_in_dim(parts, at, axis, keepdims=False)
         send = lax.dynamic_index_in_dim(parts, 1 - at, axis, keepdims=False)
         arrived = lax.ppermute(send, "dp", pairs)
-        earlier = yield arrived
+        earlier = yield grad
         total = keep.astype(F32) + after(arrived, *earlier).astype(F32)
         grad = total.astype(BF16)
     yield total
@@ -1778,25 +1778,25 @@
     next(gain_run)
     gain_run.send(())
     gain_run.send(())
-    all_run.send((input_grad,))
-    grad_head = after(grad_head, input_grad).astype(F32)
-    grad_second_both = after(grad_second_both, input_grad).astype(F32)
-    arrived = run_out.send((input_grad,))
-    gains = all_run.send((arrived,))
-    loss = gains[3, 0] / gains[3, 1]
-    depth_grad = lax.dynamic_slice_in_dim(gains[4:], own * width, width, 1)
-    arrived = run_in.send((arrived,))
-    gain_run.send((arrived,))
-    middle = after(middle, arrived).astype(F32)
+    out_one = run_out.send((input_grad,))
+    all_run.send((out_one,))
+    grad_head = after(grad_head, out_one).astype(F32)
+    grad_second_both = after(grad_second_both, out_one).astype(F32)
+    out_two = run_out.send((out_one,))
+    in_one = run_in.send((out_two,))
+    gain_run.send((in_one,))
+    middle = after(middle, in_one).astype(F32)
     attend_grads, mixer_sum = middle[:, : 8 * width], middle[:, 8 * width :]
     crossed = cross(sides(attend_grads[:, 3 * width : 6 * width], attend_grads[:, 7 * width :]).astype(BF16))
     own_part = sides(attend_grads[:, : 3 * width], attend_grads[:, 6 * width : 7 * width])
-    run_out.send((arrived,))
-    arrived = run_in.send((own_part,))
-    attend_grads = own_part + after(crossed, arrived).astype(F32)
-    gain_run.send((arrived,))
-    grad_first_out = run_out.send(())
-    grad_first_in = run_in.send(())
+    in_two = run_in.send((own_part,))
+    gain_run.send((in_two,))
+    attend_grads = own_part + after(crossed, in_two).astype(F32)
+    gains = all_run.send((attend_grads,))
+    loss = gains[3, 0] / gains[3, 1]
+    depth_grad = lax.dynamic_slice_in_dim(gains[4:], own * width, width, 1)
+    grad_first_out = run_out.send((attend_grads,))
+    grad_first_in = run_in.send((grad_first_out,))
     first_gain_grad = gain_run.send((grad_first_in,))
     grad_second_out, grad_second_in = jnp.split(grad_second_both, 2, axis=1)
     grad_query, grad_key, grad_value, grad_out = jnp.split(attend_grads, 4, axis=1)

time: 691 us -> 677 us (0.980)
  waiting for transfers between devices: 251 us -> 243 us
    ppermute x10, waiting for transfers between devices: 20.8 us -> 4.46 us  [sum_steps(): arrived = lax.ppermute(values, axis, pairs)]
    unnamed x154 -> x150, local copies, waits for them, and re-layouts: 18.8 us -> 17.1 us
  transfers between devices with their start and end apart: 114 -> 114, of which waited for: 67 -> 68; matrix products, arithmetic and copies ran while one was open for 7% -> 8% of each run, Pallas kernels for 29% -> 29%
where the time goes in v4:
time: 677 us; the launch traced here: 667 us
  waiting for transfers between devices  243 us (36%)
  Pallas kernels  239 us (35%)
  starting transfers between devices  94.8 us (14%)
  local copies, waits for them, and re-layouts  33.7 us (5%)
  other arithmetic  24.1 us (4%)
  between operations  18.1 us (3%)
  matrix products  13.5 us (2%)
    ppermute x31, waiting for transfers between devices, cross(): return lax.ppermute(values, 'mp', CHIP_PAIRS)  131 us
    pallas_call x12, Pallas kernels, pieces_call(): pl.pallas_call(kernel, grid=(steps,), in_specs=in_specs, out_specs=[place...  67.4 us
    ppermute x6, waiting for transfers between devices, reduce_by_steps(): arrived = lax.ppermute(send, 'dp', pairs)  67.3 us
    ppermute x31, starting transfers between devices, cross(): return lax.ppermute(values, 'mp', CHIP_PAIRS)  46.6 us
    pallas_call x6, Pallas kernels, rows_call(): pl.pallas_call(kernel, grid_spec=pltpu.PrefetchScalarGridSpec(num_scalar_...  32.1 us
    pallas_call x3, Pallas kernels, weights_call(): pl.pallas_call(lambda *refs: kernel(number, *refs[:2 * number], refs[-1])...  30.8 us
    ppermute x54, waiting for transfers between devices, swap(): return lax.ppermute(values, 'mp', CORE_PAIRS)  23.3 us
    pallas_call x5, Pallas kernels, norm_backward(): pl.pallas_call(kernel, grid=(rows // block,), in_specs=[row, one] + part_...  21.6 us
  transfers between devices with their start and end apart: 114, of which 68 were waited for; matrix products, arithmetic and copies ran while one was open for 8% of the time, Pallas kernels for 29%

profile of v4, /device:TPU:0, one launch (start us, length us, event | category | flops | bytes accessed | tf_op | source)
XLA Modules:
  0.0 666.9 jit_solution(3472309510817474635)
XLA Ops:
  17.7 7.7 %branch_forward.6 = (bf16[2048,1024]{1,0:T(8,128)(2,1)}, bf16[2048,1024]{1,0:T(8,128)(2,1)}, bf16[2048,1024]{1,0:T(8,128)(2,1)}, bf16[512,1024]{1,0:T(8,128)(2,1)S(1)}, bf16[512,1024]{1,0:T(8,128)(2,1)S(1)}) custom-call(bf16[512,1024]{1,0:T(8,128)(2,1)S(1)} %norm_forward.5.refs_0_, bf16[512,1024]{1,0:T(8,128)(2,1)} %collective-permute-done.refs_1_, ...), custom_call_target="tpu_custom_call" | custom-call | flops 4294967 | bytes 4194 | tf_op jit(solution)/shard_map/branch_forward/pallas_call | solution.py:754
  63.3 8.1 %collective-permute-done.12.refs_2_ = bf16[256,1024]{1,0:T(8,128)(2,1)S(1)} collective-permute-done((bf16[256,1024]{1,0:T(8,128)(2,1)S(1)}, bf16[256,1024]{1,0:T(8,128)(2,1)S(1)}, u32[]{:S(2)}, u32[]{:S(2)}) %collective-permute-start.12) | collective-permute-done | bytes 524320 | tf_op jit(solution)/shard_map/ppermute | solution.py:516
  73.2 11.2 %collective-permute-done.19.refs_3_ = bf16[256,1024]{1,0:T(8,128)(2,1)S(1)} collective-permute-done((bf16[256,1024]{1,0:T(8,128)(2,1)S(1)}, bf16[256,1024]{1,0:T(8,128)(2,1)S(1)}, u32[]{:S(2)}, u32[]{:S(2)}) %collective-permute-start.19) | collective-permute-done | bytes 524320 | tf_op jit(solution)/shard_map/ppermute | solution.py:516
  102.5 6.7 %qkv.1 = (bf16[1024,1536]{1,0:T(8,128)(2,1)S(1)}, bf16[1024,1024]{1,0:T(8,128)(2,1)}) custom-call(s32[2]{0:T(128)S(1)} %pad_add_fusion.1.scalar_ref, bf16[512,1024]{1,0:T(8,128)(2,1)S(1)} %get-tuple-element.207.refs_0_, bf16[512,1024]{1,0:T(8,128)(2,1)S(1)} %collective-permute-done.20.refs_1_, bf16[1024,256]{1,0:T(8,128)(2,1)} %refs_1_.3, ...), custom_call_target="tpu_custom_call" | custom-call | flops 3221225472 | bytes 3145728 | tf_op jit(solution)/shard_map/qkv/pallas_call | solution.py:1032
  113.7 8.6 %attend_forward.1 = (bf16[1024,512]{1,0:T(8,128)(2,1)S(1)}, f32[4,1,1024]{2,1,0:T(1,128)S(1)}) custom-call(f32[1024,1]{1,0:T(8,128)S(1)} %fusion.11.live_ref, bf16[1024,1536]{1,0:T(8,128)(2,1)S(1)} %get-tuple-element.210.query_ref.keys_ref.values_ref, bf16[1024,1536]{1,0:T(8,128)(2,1)S(1)} %get-tuple-element.210.query_ref.keys_ref.values_ref, ...), custom_call_target="tpu_custom_call" | custom-call | flops 2147483648 | bytes 12582912 | tf_op jit(solution)/shard_map/attend_forward/pallas_call | solution.py:875
  136.8 7.9 %mixer_front.1 = (bf16[1024,1024]{1,0:T(8,128)(2,1)}, f32[1024,512]{1,0:T(8,128)}, f32[1024,512]{1,0:T(8,128)}, f32[1024,512]{1,0:T(8,128)S(1)}, f32[3,512]{1,0:T(4,128)S(1)}) custom-call(s32[2]{0:T(128)S(1)} %pad_add_fusion.2.scalar_ref, bf16[512,1024]{1,0:T(8,128)(2,1)S(1)} %get-tuple-element.216.own_ref, ...), custom_call_target="tpu_custom_call" | custom-call | flops 2147483648 | bytes 2097152 | tf_op jit(solution)/shard_map/mixer_front/pallas_call | solution.py:1175
  174.0 6.5 branch_forward.9
  192.6 7.7 %collective-permute-done.42.refs_0_ = bf16[256,1024]{1,0:T(8,128)(2,1)S(1)} collective-permute-done((bf16[256,1024]{1,0:T(8,128)(2,1)S(1)}, bf16[256,1024]{1,0:T(8,128)(2,1)S(1)}, u32[]{:S(2)}, u32[]{:S(2)}) %collective-permute-start.42) | collective-permute-done | bytes 524320 | tf_op jit(solution)/shard_map/ppermute | solution.py:516
  217.3 11.8 %collective-permute-done.47.refs_3_ = bf16[256,1024]{1,0:T(8,128)(2,1)S(1)} collective-permute-done((bf16[256,1024]{1,0:T(8,128)(2,1)S(1)}, bf16[256,1024]{1,0:T(8,128)(2,1)S(1)}, u32[]{:S(2)}, u32[]{:S(2)}) %collective-permute-start.47) | collective-permute-done | bytes 524320 | tf_op jit(solution)/shard_map/ppermute | solution.py:516
  240.0 7.9 %collective-permute-done.49.first_ref.refs_0_ = bf16[256,1024]{1,0:T(8,128)(2,1)S(1)} collective-permute-done((bf16[256,1024]{1,0:T(8,128)(2,1)S(1)}, bf16[256,1024]{1,0:T(8,128)(2,1)S(1)}, u32[]{:S(2)}, u32[]{:S(2)}) %collective-permute-start.49) | collective-permute-done | bytes 524320 | tf_op jit(solution)/shard_map/ppermute | solution.py:516
  277.7 12.1 %collective-permute-done.55 = bf16[256,1024]{1,0:T(8,128)(2,1)S(1)} collective-permute-done((bf16[256,1024]{1,0:T(8,128)(2,1)S(1)}, bf16[256,1024]{1,0:T(8,128)(2,1)S(1)}, u32[]{:S(2)}, u32[]{:S(2)}) %collective-permute-start.55) | collective-permute-done | bytes 524320 | tf_op jit(solution)/shard_map/ppermute | solution.py:516
  303.2 8.6 %branch_backward.6 = (bf16[2048,1024]{1,0:T(8,128)(2,1)}, bf16[2048,1024]{1,0:T(8,128)(2,1)}, bf16[512,1024]{1,0:T(8,128)(2,1)S(1)}, bf16[512,1024]{1,0:T(8,128)(2,1)}) custom-call(bf16[512,1024]{1,0:T(8,128)(2,1)S(1)} %get-tuple-element.251.refs_0_, bf16[512,1024]{1,0:T(8,128)(2,1)S(1)} %collective-permute-done.56.refs_1_, ...), custom_call_target="tpu_custom_call" | custom-call | flops 4294967 | bytes 4194 | tf_op jit(solution)/shard_map/branch_backward/pallas_call | solution.py:754
  323.1 6.5 collective-permute-done.64.refs_0_
  347.4 15.4 %second_weights.1 = bf16[1024,2048]{1,0:T(8,128)(2,1)} custom-call(bf16[2048,1024]{1,0:T(8,128)(2,1)} %get-tuple-element.271.refs_0_, bf16[2048,1024]{1,0:T(8,128)(2,1)} %get-tuple-element.272.refs_1_, bf16[2048,1024]{1,0:T(8,128)(2,1)} %get-tuple-element.273.refs_2_, bf16[2048,1024]{1,0:T(8,128)(2,1)} %get-tuple-element.274.refs_3_), custom_call_target="tpu_custom_call" | custom-call | flops 8589934592 | bytes 4194304 | tf_op jit(solution)/shard_map/second_weights/pallas_call | solution.py:1471
  392.7 12.1 %mixer_back.1 = (bf16[1024,1024]{1,0:T(8,128)(2,1)S(1)}, f32[5,512]{1,0:T(8,128)S(1)}, bf16[512,1024]{1,0:T(8,128)(2,1)S(1)}, bf16[512,1024]{1,0:T(8,128)(2,1)}) custom-call(s32[2]{0:T(128)S(1)} %pad_add_fusion.2.scalar_ref, f32[1024,512]{1,0:T(8,128)} %copy-done.13, f32[1024,512]{1,0:T(8,128)} %copy-done.12, f32[1024,512]{1,0:T(8,128)} %get-tuple-element.279.value_in, ...), custom_call_target="tpu_custom_call" | custom-call | flops 2147483648 | bytes 2097152 | tf_op jit(solution)/shard_map/mixer_back/pallas_call | solution.py:1245
  416.9 7.1 %mixer_weights.1 = bf16[1024,1536]{1,0:T(8,128)(2,1)} custom-call(bf16[1024,1024]{1,0:T(8,128)(2,1)} %get-tuple-element.294.refs_0_, bf16[1024,1024]{1,0:T(8,128)(2,1)S(1)} %copy-done.32, bf16[1024,1024]{1,0:T(8,128)(2,1)} %get-tuple-element.296.refs_2_, bf16[1024,512]{1,0:T(8,128)(2,1)} %get-tuple-element.297.refs_3_), custom_call_target="tpu_custom_call" | custom-call | flops 3221225472 | bytes 3145728 | tf_op jit(solution)/shard_map/mixer_weights/pallas_call | solution.py:1471
  434.3 15.4 %attend_backward.1.refs_0_.refs_1_ = bf16[1024,1536]{1,0:T(8,128)(2,1)S(1)} custom-call(f32[1024,1]{1,0:T(8,128)S(1)} %copy-done.15, bf16[1024,1536]{1,0:T(8,128)(2,1)S(1)} %copy-done.9, bf16[1024,1536]{1,0:T(8,128)(2,1)S(1)} %copy-done.9, bf16[1024,1536]{1,0:T(8,128)(2,1)S(1)} %copy-done.9, bf16[1024,512]{1,0:T(8,128)(2,1)S(1)} %get-tuple-element.298.grad_ref, ...), custom_call_target="tpu_custom_call" | custom-call | flops 5368709120 | bytes 12582912 | tf_op jit(solution)/shard_map/attend_backward/pallas_call | solution.py:944
  452.6 7.1 %qkv_back.1 = (bf16[512,1024]{1,0:T(8,128)(2,1)S(1)}, bf16[512,1024]{1,0:T(8,128)(2,1)S(1)}) custom-call(s32[2]{0:T(128)S(1)} %pad_add_fusion.1.scalar_ref, bf16[1024,1536]{1,0:T(8,128)(2,1)S(1)} %attend_backward.1.refs_0_.refs_1_, bf16[1024,256]{1,0:T(8,128)(2,1)} %refs_1_.3, bf16[1024,256]{1,0:T(8,128)(2,1)} %refs_2_.19, bf16[1024,256]{1,0:T(8,128)(2,1)} %refs_3_.24, ...), custom_call_target="tpu_custom_call" | custom-call | flops 3221225472 | bytes 3145728 | tf_op jit(solution)/shard_map/qkv_back/pallas_call | solution.py:1032
  466.7 8.3 %attend_weights.1 = bf16[1024,2048]{1,0:T(8,128)(2,1)} custom-call(bf16[1024,1024]{1,0:T(8,128)(2,1)} %get-tuple-element.309.refs_0_, bf16[1024,1536]{1,0:T(8,128)(2,1)S(1)} %attend_backward.1.refs_0_.refs_1_, bf16[1024,1024]{1,0:T(8,128)(2,1)} %get-tuple-element.311.refs_2_, bf16[1024,512]{1,0:T(8,128)(2,1)} %copy-done.33), custom_call_target="tpu_custom_call" | custom-call | flops 4294967296 | bytes 4194304 | tf_op jit(solution)/shard_map/attend_weights/pallas_call | solution.py:1471
  484.6 8.0 %branch_backward.9 = (bf16[2048,1024]{1,0:T(8,128)(2,1)}, bf16[2048,1024]{1,0:T(8,128)(2,1)}, bf16[512,1024]{1,0:T(8,128)(2,1)S(1)}, bf16[512,1024]{1,0:T(8,128)(2,1)S(1)}) custom-call(bf16[512,1024]{1,0:T(8,128)(2,1)S(1)} %get-tuple-element.305.refs_0_, bf16[512,1024]{1,0:T(8,128)(2,1)S(1)} %collective-permute-done.84.refs_1_, ...), custom_call_target="tpu_custom_call" | custom-call | flops 4294967 | bytes 4194 | tf_op jit(solution)/shard_map/branch_backward/pallas_call | solution.py:754
  527.1 8.3 %convolution_convert_fusion.1 = bf16[1024,1024]{1,0:T(8,128)(2,1)S(1)} fusion(bf16[2048,1024]{1,0:T(8,128)(2,1)} %get-tuple-element.325, bf16[2048,1024]{1,0:T(8,128)(2,1)} %get-tuple-element.326), kind=kOutput, calls=%fused_computation.7 | convolution fusion | flops 4296015872 | bytes 10485760 | tf_op jit(solution)/shard_map/dot_general | solution.py:66
  548.3 28.1 %collective-permute-done.95 = bf16[4,128,1024]{2,1,0:T(8,128)(2,1)S(1)} collective-permute-done((bf16[4,128,1024]{2,1,0:T(8,128)(2,1)S(1)}, bf16[4,128,1024]{2,1,0:T(8,128)(2,1)S(1)}, u32[]{:S(2)}, u32[]{:S(2)}) %collective-permute-start.95) | collective-permute-done | bytes 1048608 | tf_op jit(solution)/shard_map/ppermute | solution.py:1533
  583.2 17.2 %collective-permute-done.101 = bf16[2,128,1024]{2,1,0:T(8,128)(2,1)S(1)} collective-permute-done((bf16[2,128,1024]{2,1,0:T(8,128)(2,1)S(1)}, bf16[2,128,1024]{2,1,0:T(8,128)(2,1)S(1)}, u32[]{:S(2)}, u32[]{:S(2)}) %collective-permute-start.101) | collective-permute-done | bytes 524320 | tf_op jit(solution)/shard_map/ppermute | solution.py:1533
  615.7 17.2 %collective-permute-done.103 = bf16[2,128,1024]{2,1,0:T(8,128)(2,1)S(1)} collective-permute-done((bf16[2,128,1024]{2,1,0:T(8,128)(2,1)S(1)}, bf16[2,128,1024]{2,1,0:T(8,128)(2,1)S(1)}, u32[]{:S(2)}, u32[]{:S(2)}) %collective-permute-start.103) | collective-permute-done | bytes 524320 | tf_op jit(solution)/shard_map/ppermute | solution.py:1533
  (528 shorter events, 393.3 us)
Async XLA Ops:
  7.2 385.4 %reduce-scatter.4.cloned.1.call-start = ((), (), s32[]{:S(2)}) async-start(), calls=%async_computation.3 | async-start | bytes 4718592 | tf_op jit(solution)/shard_map/reduce_scatter | solution.py:1503
  32.5 20.4 %collective-permute-start.1 = (bf16[256,768]{1,0:T(8,128)(2,1)S(1)}, bf16[256,768]{1,0:T(8,128)(2,1)}, u32[]{:S(2)}, u32[]{:S(2)}) collective-permute-start(bf16[256,768]{1,0:T(8,128)(2,1)S(1)} %fusion.15), channel_id=1, source_target_pairs={{0,2},{2,0},{1,3},{3,1},{4,6},{6,4},{5,7},{7,5},{8,10},{10,8},{9,1... | collective-permute-start | bytes 1179656 | tf_op jit(solution)/shard_map/ppermute | solution.py:516
  48.9 24.3 %collective-permute-start.6 = (bf16[512,1024]{1,0:T(8,128)(2,1)S(1)}, bf16[512,1024]{1,0:T(8,128)(2,1)S(1)}, u32[]{:S(2)}, u32[]{:S(2)}) collective-permute-start(bf16[512,1024]{1,0:T(8,128)(2,1)S(1)} %copy-done.35), channel_id=1, source_target_pairs={{0,1},{1,0},{2,3},{3,2},{4,5},{5,4},{6,7},{7,6},{8,9},{9,8},{10,11... | collective-permute-start | bytes 3145736 | tf_op jit(solution)/shard_map/ppermute | solution.py:512
  89.5 24.2 %collective-permute-start.24 = (bf16[1024,256]{1,0:T(8,128)(2,1)S(1)}, bf16[1024,256]{1,0:T(8,128)(2,1)S(1)}, u32[]{:S(2)}, u32[]{:S(2)}) collective-permute-start(bf16[1024,256]{1,0:T(8,128)(2,1)S(1)} %copy-done.49), channel_id=1, source_target_pairs={{0,2},{2,0},{1,3},{3,1},{4,6},{6,4},{5,7},{7,5},{8,10},{10,8},{9,1... | collective-permute-start | bytes 1572872 | tf_op jit(solution)/shard_map/ppermute | solution.py:516
  96.7 27.9 %collective-permute-start.25 = (bf16[1024,256]{1,0:T(8,128)(2,1)S(1)}, bf16[1024,256]{1,0:T(8,128)(2,1)S(1)}, u32[]{:S(2)}, u32[]{:S(2)}) collective-permute-start(bf16[1024,256]{1,0:T(8,128)(2,1)S(1)} %copy-done.50), channel_id=1, source_target_pairs={{0,2},{2,0},{1,3},{3,1},{4,6},{6,4},{5,7},{7,5},{8,10},{10,8},{9,1... | collective-permute-start | bytes 1572872 | tf_op jit(solution)/shard_map/ppermute | solution.py:516
  200.9 16.3 %collective-permute-start.35 = (bf16[512,1024]{1,0:T(8,128)(2,1)S(1)}, bf16[512,1024]{1,0:T(8,128)(2,1)S(1)}, u32[]{:S(2)}, u32[]{:S(2)}) collective-permute-start(bf16[512,1024]{1,0:T(8,128)(2,1)S(1)} %get-tuple-element.225), channel_id=1, source_target_pairs={{0,1},{1,0},{2,3},{3,2},{4,5},{5,4},{6,7},{7,6},{8,9},{9,8},{10,11... | collective-permute-start | bytes 3145736 | tf_op jit(solution)/shard_map/ppermute | solution.py:512
  300.5 181.4 %reduce-scatter.6.cloned.1.call-start = ((), (), s32[]{:S(2)}) async-start(), calls=%async_computation.4 | async-start | bytes 4718592 | tf_op jit(solution)/shard_map/reduce_scatter | solution.py:1503
  339.0 23.8 %collective-permute-start.57 = (bf16[512,1024]{1,0:T(8,128)(2,1)}, bf16[512,1024]{1,0:T(8,128)(2,1)S(1)}, u32[]{:S(2)}, u32[]{:S(2)}) collective-permute-start(bf16[512,1024]{1,0:T(8,128)(2,1)} %get-tuple-element.254), channel_id=1, source_target_pairs={{0,1},{1,0},{2,3},{3,2},{4,5},{5,4},{6,7},{7,6},{8,9},{9,8},{10,11... | collective-permute-start | bytes 3145736 | tf_op jit(solution)/shard_map/ppermute | solution.py:512
  345.7 17.1 %collective-permute-start.69 = (bf16[256,1024]{1,0:T(8,128)(2,1)}, bf16[256,1024]{1,0:T(8,128)(2,1)S(1)}, u32[]{:S(2)}, u32[]{:S(2)}) collective-permute-start(bf16[256,1024]{1,0:T(8,128)(2,1)} %add_convert_fusion.3), channel_id=1, source_target_pairs={{0,2},{2,0},{1,3},{3,1},{4,6},{6,4},{5,7},{7,5},{8,10},{10,8},{9,1... | collective-permute-start | bytes 1572872 | tf_op jit(solution)/shard_map/ppermute | solution.py:516
  392.6 245.6 %reduce-scatter.8.cloned.1.call-start = ((), (), s32[]{:S(2)}) async-start(), calls=%async_computation.5 | async-start | bytes 6488064 | tf_op jit(solution)/shard_map/reduce_scatter | solution.py:1503
  428.4 24.3 %collective-permute-start.80 = (bf16[1024,512]{1,0:T(8,128)(2,1)S(1)}, bf16[1024,512]{1,0:T(8,128)(2,1)S(1)}, u32[]{:S(2)}, u32[]{:S(2)}) collective-permute-start(bf16[1024,512]{1,0:T(8,128)(2,1)S(1)} %get-tuple-element.300), channel_id=1, source_target_pairs={{0,2},{2,0},{1,3},{3,1},{4,6},{6,4},{5,7},{7,5},{8,10},{10,8},{9,1... | collective-permute-start | bytes 3145736 | tf_op jit(solution)/shard_map/ppermute | solution.py:516
  483.6 24.1 %collective-permute-start.82 = (bf16[256,1024]{1,0:T(8,128)(2,1)S(1)}, bf16[256,1024]{1,0:T(8,128)(2,1)S(1)}, u32[]{:S(2)}, u32[]{:S(2)}) collective-permute-start(bf16[256,1024]{1,0:T(8,128)(2,1)S(1)} %get-tuple-element.433), channel_id=1, source_target_pairs={{0,2},{2,0},{1,3},{3,1},{4,6},{6,4},{5,7},{7,5},{8,10},{10,8},{9,1... | collective-permute-start | bytes 1572872 | tf_op jit(solution)/shard_map/ppermute | solution.py:516
  518.7 24.8 %collective-permute-start.96 = (bf16[512,1024]{1,0:T(8,128)(2,1)}, bf16[512,1024]{1,0:T(8,128)(2,1)S(1)}, u32[]{:S(2)}, u32[]{:S(2)}) collective-permute-start(bf16[512,1024]{1,0:T(8,128)(2,1)} %copy-done.36), channel_id=1, source_target_pairs={{0,1},{1,0},{2,3},{3,2},{4,5},{5,4},{6,7},{7,6},{8,9},{9,8},{10,11... | collective-permute-start | bytes 3145736 | tf_op jit(solution)/shard_map/ppermute | solution.py:512
  525.6 17.9 %collective-permute-start.97 = (bf16[256,1024]{1,0:T(8,128)(2,1)S(1)}, bf16[256,1024]{1,0:T(8,128)(2,1)S(1)}, u32[]{:S(2)}, u32[]{:S(2)}) collective-permute-start(bf16[256,1024]{1,0:T(8,128)(2,1)S(1)} %add_convert_fusion.2), channel_id=1, source_target_pairs={{0,2},{2,0},{1,3},{3,1},{4,6},{6,4},{5,7},{7,5},{8,10},{10,8},{9,1... | collective-permute-start | bytes 1572872 | tf_op jit(solution)/shard_map/ppermute | solution.py:516
  535.5 40.9 %collective-permute-start.95 = (bf16[4,128,1024]{2,1,0:T(8,128)(2,1)S(1)}, bf16[4,128,1024]{2,1,0:T(8,128)(2,1)S(1)}, u32[]{:S(2)}, u32[]{:S(2)}) collective-permute-start(bf16[4,128,1024]{2,1,0:T(8,128)(2,1)S(1)} %dynamic-slice_bitcast_fusion.1), channel_id=1, source_target_pairs={{0,4},{4,0},{8,12},{12,8},{16,20},{20,16},{24,28},{28,24},{1,5},{5... | collective-permute-start | bytes 3145736 | tf_op jit(solution)/shard_map/ppermute | solution.py:1533
  543.0 62.5 %collective-permute-start.100 = (bf16[4,128,1024]{2,1,0:T(8,128)(2,1)}, bf16[4,128,1024]{2,1,0:T(8,128)(2,1)}, u32[]{:S(2)}, u32[]{:S(2)}) collective-permute-start(bf16[4,128,1024]{2,1,0:T(8,128)(2,1)} %dynamic-slice_bitcast_fusion), channel_id=1, source_target_pairs={{0,4},{4,0},{8,12},{12,8},{16,20},{20,16},{24,28},{28,24},{1,5},{5... | collective-permute-start | bytes 3145736 | tf_op jit(solution)/shard_map/ppermute | solution.py:1533
  576.8 23.6 %collective-permute-start.101 = (bf16[2,128,1024]{2,1,0:T(8,128)(2,1)S(1)}, bf16[2,128,1024]{2,1,0:T(8,128)(2,1)S(1)}, u32[]{:S(2)}, u32[]{:S(2)}) collective-permute-start(bf16[2,128,1024]{2,1,0:T(8,128)(2,1)S(1)} %dynamic-slice_bitcast_fusion.3), channel_id=1, source_target_pairs={{0,8},{8,0},{4,12},{12,4},{16,24},{24,16},{20,28},{28,20},{1,9},{9... | collective-permute-start | bytes 1572872 | tf_op jit(solution)/shard_map/ppermute | solution.py:1533
  580.8 30.2 %collective-permute-start.94 = (f32[9,1024]{1,0:T(8,128)S(1)}, f32[9,1024]{1,0:T(8,128)S(1)}, u32[]{:S(2)}, u32[]{:S(2)}) collective-permute-start(f32[9,1024]{1,0:T(8,128)S(1)} %add.295), channel_id=1, source_target_pairs={{0,8},{8,0},{4,12},{12,4},{16,24},{24,16},{20,28},{28,20},{1,9},{9... | collective-permute-start | bytes 110600 | tf_op jit(solution)/shard_map/ppermute | solution.py:1514
  607.5 25.5 %collective-permute-start.103 = (bf16[2,128,1024]{2,1,0:T(8,128)(2,1)S(1)}, bf16[2,128,1024]{2,1,0:T(8,128)(2,1)S(1)}, u32[]{:S(2)}, u32[]{:S(2)}) collective-permute-start(bf16[2,128,1024]{2,1,0:T(8,128)(2,1)S(1)} %dynamic-slice_bitcast_fusion.2), channel_id=1, source_target_pairs={{0,8},{8,0},{4,12},{12,4},{16,24},{24,16},{20,28},{28,20},{1,9},{9... | collective-permute-start | bytes 1572872 | tf_op jit(solution)/shard_map/ppermute | solution.py:1533
  610.9 38.7 %collective-permute-start.98 = (f32[9,1024]{1,0:T(8,128)S(1)}, f32[9,1024]{1,0:T(8,128)S(1)}, u32[]{:S(2)}, u32[]{:S(2)}) collective-permute-start(f32[9,1024]{1,0:T(8,128)S(1)} %add.300), channel_id=1, source_target_pairs={{0,16},{16,0},{4,20},{20,4},{8,24},{24,8},{12,28},{28,12},{1,17},{... | collective-permute-start | bytes 110600 | tf_op jit(solution)/shard_map/ppermute | solution.py:1514
  613.5 19.6 %collective-permute-start.107 = (f32[2,1024]{1,0:T(2,128)S(1)}, f32[2,1024]{1,0:T(2,128)S(1)}, u32[]{:S(2)}, u32[]{:S(2)}) collective-permute-start(f32[2,1024]{1,0:T(2,128)S(1)} %add.312), channel_id=1, source_target_pairs={{0,8},{8,0},{4,12},{12,4},{16,24},{24,16},{20,28},{28,20},{1,9},{9... | collective-permute-start | bytes 24584 | tf_op jit(solution)/shard_map/ppermute | solution.py:1514
  615.0 35.8 %collective-permute-start.110 = (bf16[128,1024]{1,0:T(8,128)(2,1)S(1)}, bf16[128,1024]{1,0:T(8,128)(2,1)}, u32[]{:S(2)}, u32[]{:S(2)}) collective-permute-start(bf16[128,1024]{1,0:T(8,128)(2,1)S(1)} %dynamic-slice_bitcast_fusion.4), channel_id=1, source_target_pairs={{0,16},{16,0},{4,20},{20,4},{8,24},{24,8},{12,28},{28,12},{1,17},{... | collective-permute-start | bytes 786440 | tf_op jit(solution)/shard_map/ppermute | solution.py:1533
  633.2 21.2 %collective-permute-start.108 = (f32[2,1024]{1,0:T(2,128)S(1)}, f32[2,1024]{1,0:T(2,128)}, u32[]{:S(2)}, u32[]{:S(2)}) collective-permute-start(f32[2,1024]{1,0:T(2,128)S(1)} %add.313), channel_id=1, source_target_pairs={{0,16},{16,0},{4,20},{20,4},{8,24},{24,8},{12,28},{28,12},{1,17},{... | collective-permute-start | bytes 24584 | tf_op jit(solution)/shard_map/ppermute | solution.py:1514
  633.7 18.2 %collective-permute-start.109 = (bf16[128,1024]{1,0:T(8,128)(2,1)S(1)}, bf16[128,1024]{1,0:T(8,128)(2,1)}, u32[]{:S(2)}, u32[]{:S(2)}) collective-permute-start(bf16[128,1024]{1,0:T(8,128)(2,1)S(1)} %dynamic-slice_bitcast_fusion.5), channel_id=1, source_target_pairs={{0,16},{16,0},{4,20},{20,4},{8,24},{24,8},{12,28},{28,12},{1,17},{... | collective-permute-start | bytes 786440 | tf_op jit(solution)/shard_map/ppermute | solution.py:1533
  (160 other events, 1394.8 us)
Sparse Core Ops, SparseCore 0:
  300.6 89.3 reduce-scatter.3
  394.0 87.7 reduce-scatter.5
  485.5 139.7 reduce-scatter.7
